TPU v7x, 128 devices: a whole 4x4x4 slice. The times are simulated.
128 devices in a mesh: dp: 16 (over x, y_hi, core), ctx: 4 (over z), tensor: 2 (over y_lo).
Axes of the slice: x: 4, y: 4 (y_hi: 2, y_lo: 2; y = y_hi * 2 + y_lo), z: 4, core: 2. Of those that a mesh axis runs over, the one named last changes fastest.
Arguments:
- tokens: bfloat16 [2, 8192, 1088], P(None, ('dp', 'ctx', 'tensor')), may hold values from -6 to 6
- qkv_weight: bfloat16 [2, 1088, 3264], P(None, 'dp'), may hold values from -0.1875 to 0.1875
- out_weight: bfloat16 [2, 1088, 1088], P(None, 'dp'), may hold values from -1.5 to 1.5
- up_weight: bfloat16 [2, 1088, 4352], P(None, 'dp', 'tensor'), may hold values from -0.1875 to 0.1875
- down_weight: bfloat16 [2, 1088, 4352], P(None, 'dp', 'tensor'), may hold values from -0.09375 to 0.09375
- vectors: bfloat16 [2, 12, 1088], P(None, None, 'dp'), as said below
- segments: int32 [2, 8192], P(None, ('dp', 'ctx', 'tensor')), may hold values from 0 to 2, as said below
- cotangent: float32 [2, 8192, 1088], P(None, ('dp', 'ctx', 'tensor')), may hold values from -6 to 6
Outputs:
- out: float32 [2, 8192, 1088], P(None, ('dp', 'ctx', 'tensor'))
- grad_tokens: float32 [2, 8192, 1088], P(None, ('dp', 'ctx', 'tensor'))
- grad_qkv: float32 [2, 1088, 3264], P(None, 'dp')
- grad_out: float32 [2, 1088, 1088], P(None, 'dp')
- grad_up: float32 [2, 1088, 4352], P(None, 'dp', 'tensor')
- grad_down: float32 [2, 1088, 4352], P(None, 'dp', 'tensor')
- grad_vectors: float32 [2, 12, 1088], P(None, None, 'dp')
Inputs may be any that keep to these rules, and one draw needn't show every extreme that they name: `segments`: each sequence of 512 rows holds three documents numbered 0, 1, 2 in order of position. `vectors`: rows 0 and 5 of each layer lie between 0.5 and 1.5.
All inputs are finite; a program needn't handle non-finite values.
Results may differ from a plain program's by a relative error of at most 0.019.
Values may be sent and summed in bfloat16 or wider, within the bound.
A program may use at most 256 MiB of HBM per device.

v0:
```python
from functools import reduce
import math

import jax
import jax.numpy as jnp
from jax import lax
from jax.sharding import PartitionSpec as P

HEADS = 17
FF = 4352


EPSILON = 1e-05
MASKED = -1e30


def layer_norm(inputs, gain_row, shift_row):
    row_mean = jnp.mean(inputs, -1, keepdims=True)
    centred = inputs - row_mean
    spread = jnp.mean(centred * centred, -1, keepdims=True)
    return centred * lax.rsqrt(spread + EPSILON) * gain_row + shift_row


def gelu_exact(inputs):
    return jax.nn.gelu(inputs, approximate=False)


def contract_rows(factor_one, factor_two):
    return lax.dot_general(
        factor_one, factor_two, (((0,), (0,)), ((), ())), preferred_element_type=jnp.float32
    )


def contract_cols(factor_one, factor_two):
    return lax.dot_general(
        factor_one, factor_two, (((1,), (1,)), ((), ())), preferred_element_type=jnp.float32
    )


def fetch_layer(qkv_weight, out_weight, up_weight, down_weight, vectors, layer_id):
    return (
        lax.all_gather(qkv_weight[layer_id], "dp", axis=0, tiled=True),
        lax.all_gather(out_weight[layer_id], "dp", axis=0, tiled=True),
        lax.all_gather(up_weight[layer_id], "dp", axis=0, tiled=True),
        lax.all_gather(down_weight[layer_id], "dp", axis=0, tiled=True),
        lax.all_gather(vectors[layer_id], "dp", axis=1, tiled=True),
    )


def fetch_again(qkv_weight, out_weight, up_weight, down_weight, vectors, layer_id):
    return (
        lax.all_gather(qkv_weight[layer_id], "dp", axis=0, tiled=True),
        lax.all_gather(out_weight[layer_id], "dp", axis=0, tiled=True),
        lax.all_gather(up_weight[layer_id], "dp", axis=0, tiled=True),
        lax.all_gather(down_weight[layer_id], "dp", axis=0, tiled=True),
        lax.all_gather(vectors[layer_id], "dp", axis=1, tiled=True),
    )


def split_vectors(vector_low, tensor_index, hidden_half):
    vector_rows = vector_low.astype(jnp.float32)
    bias_up = lax.dynamic_slice_in_dim(
        vector_rows[8:].reshape(-1), tensor_index * hidden_half, hidden_half
    )
    return (vector_rows, bias_up)


def make_allowed(doc_own, doc_all, positions):
    key_positions = jnp.arange(doc_all.shape[0], dtype=jnp.int32)
    return (doc_own[:, None] == doc_all[None, :]) & (key_positions[None, :] <= positions[:, None])


def head_scores(queries, keys_all, allowed):
    row_count, model_width = queries.shape
    head_size = model_width // HEADS
    query_heads = queries.reshape(row_count, HEADS, head_size)
    key_heads = keys_all.reshape(keys_all.shape[0], HEADS, head_size)
    scores = jnp.einsum(
        "qhd,khd->hqk", query_heads, key_heads, preferred_element_type=jnp.float32
    ) * (1.0 / math.sqrt(head_size))
    return jnp.where(allowed[None], scores, MASKED)


def weight_terms(operand_list):

    def joined(slot_id):
        return jnp.concatenate([element[slot_id] for element in operand_list], 0)

    attn_in_back = contract_rows(joined(0), joined(1))
    attn_out_back = contract_rows(joined(2), joined(3))
    up_back = contract_rows(joined(4), joined(5))
    down_back = contract_rows(joined(6), joined(7))
    vector_back = reduce(jnp.add, [element[8] for element in operand_list])
    return (attn_in_back, attn_out_back, up_back, down_back, vector_back)


def reduce_layer(terms):
    attn_in_back, attn_out_back, up_back, down_back, vector_back = (
        lax.psum_scatter(
            terms[0].astype(jnp.bfloat16), "dp", scatter_dimension=0, tiled=True
        ).astype(jnp.float32),
        lax.psum_scatter(
            terms[1].astype(jnp.bfloat16), "dp", scatter_dimension=0, tiled=True
        ).astype(jnp.float32),
        lax.psum_scatter(
            terms[2].astype(jnp.bfloat16), "dp", scatter_dimension=0, tiled=True
        ).astype(jnp.float32),
        lax.psum_scatter(
            terms[3].astype(jnp.bfloat16), "dp", scatter_dimension=0, tiled=True
        ).astype(jnp.float32),
        lax.psum_scatter(
            terms[4].astype(jnp.bfloat16), "dp", scatter_dimension=1, tiled=True
        ).astype(jnp.float32),
    )
    attn_in_back, attn_out_back, vector_back = (
        lax.psum(attn_in_back.astype(jnp.bfloat16), ("ctx", "tensor")).astype(jnp.float32),
        lax.psum(attn_out_back.astype(jnp.bfloat16), ("ctx", "tensor")).astype(jnp.float32),
        lax.psum(vector_back.astype(jnp.bfloat16), ("ctx", "tensor")).astype(jnp.float32),
    )
    up_back, down_back = (
        lax.psum(up_back.astype(jnp.bfloat16), "ctx").astype(jnp.float32),
        lax.psum(down_back.astype(jnp.bfloat16), "ctx").astype(jnp.float32),
    )
    return (attn_in_back, attn_out_back, up_back, down_back, vector_back)


def body(tokens, qkv_weight, out_weight, up_weight, down_weight, vectors, segments, cotangent):
    micro_count, row_count, model_width = tokens.shape
    layers = qkv_weight.shape[0]
    hidden_half = up_weight.shape[2]
    head_size = model_width // HEADS
    score_scale = 1.0 / math.sqrt(head_size)
    tensor_index = lax.axis_index("tensor")
    positions = lax.axis_index(("ctx", "tensor")) * row_count + jnp.arange(
        row_count, dtype=jnp.int32
    )
    results = []
    input_grads = []
    operand_sets = []
    totals = [None] * layers
    for micro_index in range(micro_count):
        doc_own = segments[micro_index].astype(jnp.bfloat16)
        residual = tokens[micro_index].astype(jnp.float32)
        memory = []
        for layer_id in range(layers):
            weights = fetch_layer(qkv_weight, out_weight, up_weight, down_weight, vectors, layer_id)
            w_attn_in, w_attn_out, w_up, w_down, vector_low = weights
            vector_rows, bias_up = split_vectors(vector_low, tensor_index, hidden_half)
            normed_low = layer_norm(residual, vector_rows[0], vector_rows[1]).astype(jnp.bfloat16)
            projected = jnp.dot(normed_low, w_attn_in, preferred_element_type=jnp.float32)
            queries = (projected[:, :model_width] + vector_rows[2]).astype(jnp.bfloat16)
            keys_own = projected[:, model_width : 2 * model_width].astype(jnp.bfloat16)
            values_own = (projected[:, 2 * model_width :] + vector_rows[3]).astype(jnp.bfloat16)
            gathered = (
                lax.all_gather(keys_own, ("ctx", "tensor"), axis=0, tiled=True),
                lax.all_gather(values_own, ("ctx", "tensor"), axis=0, tiled=True),
                lax.all_gather(doc_own, ("ctx", "tensor"), axis=0, tiled=True),
            )
            keys_all, values_all, doc_all = gathered
            allowed = make_allowed(doc_own, doc_all, positions)
            scores = head_scores(queries, keys_all, allowed)
            row_max = jnp.max(scores, -1, keepdims=True)
            exponent = jnp.exp(scores - row_max)
            row_total = jnp.sum(exponent, -1, keepdims=True)
            probs_low = (exponent / row_total).astype(jnp.bfloat16)
            log_total = row_max + jnp.log(row_total)
            value_heads = values_all.reshape(values_all.shape[0], HEADS, head_size)
            attended = jnp.einsum(
                "hqk,khd->qhd", probs_low, value_heads, preferred_element_type=jnp.float32
            ).reshape(row_count, model_width)
            attended_low = attended.astype(jnp.bfloat16)
            midway = (
                residual
                + jnp.dot(attended_low, w_attn_out, preferred_element_type=jnp.float32)
                + vector_rows[4]
            )
            mlp_input = lax.all_gather(
                layer_norm(midway, vector_rows[5], vector_rows[6]).astype(jnp.bfloat16),
                "tensor",
                axis=0,
                tiled=True,
            )
            hidden_pre = jnp.dot(mlp_input, w_up, preferred_element_type=jnp.float32) + bias_up
            hidden = gelu_exact(hidden_pre).astype(jnp.bfloat16)

            def down_terms(offset, amount, hidden=hidden, w_down=w_down):
                return contract_cols(hidden, w_down)

            branch = lax.psum_scatter(
                down_terms(jnp.int32(0), lax.axis_size("tensor") * row_count).astype(jnp.bfloat16),
                "tensor",
                scatter_dimension=0,
                tiled=True,
            ).astype(jnp.float32)
            memory.append(
                (
                    weights,
                    gathered,
                    residual,
                    normed_low,
                    queries,
                    keys_own,
                    values_own,
                    log_total,
                    attended,
                    attended_low,
                    midway,
                    mlp_input,
                    hidden_pre,
                    hidden,
                )
            )
            residual = midway + branch + vector_rows[7]
        results.append(residual)
        gradient = cotangent[micro_index]
        operands_here = [None] * layers
        for layer_id in reversed(range(layers)):
            (
                weights,
                gathered,
                layer_input,
                normed_low,
                queries,
                keys_own,
                values_own,
                log_total,
                attended,
                attended_low,
                midway,
                mlp_input,
                hidden_pre,
                hidden,
            ) = memory[layer_id]
            weights = fetch_again(qkv_weight, out_weight, up_weight, down_weight, vectors, layer_id)
            gathered = (
                lax.all_gather(keys_own, ("ctx", "tensor"), axis=0, tiled=True),
                lax.all_gather(values_own, ("ctx", "tensor"), axis=0, tiled=True),
                lax.all_gather(doc_own, ("ctx", "tensor"), axis=0, tiled=True),
            )
            w_attn_in, w_attn_out, w_up, w_down, vector_low = weights
            vector_rows, bias_up = split_vectors(vector_low, tensor_index, hidden_half)
            keys_all, values_all, doc_all = gathered
            branch_back = gradient.astype(jnp.bfloat16)
            rows_back = lax.all_gather(branch_back, "tensor", axis=0, tiled=True)
            hidden_back = jnp.dot(rows_back, w_down, preferred_element_type=jnp.float32)
            preact_back = jax.vjp(gelu_exact, hidden_pre)[1](hidden_back)[0].astype(jnp.bfloat16)

            def up_terms(offset, amount, preact_back=preact_back, w_up=w_up):
                return contract_cols(preact_back, w_up)

            normed_two_back = lax.psum_scatter(
                up_terms(jnp.int32(0), lax.axis_size("tensor") * row_count).astype(jnp.bfloat16),
                "tensor",
                scatter_dimension=0,
                tiled=True,
            ).astype(jnp.float32)
            midway_back, gain_two_back, shift_two_back = jax.vjp(
                layer_norm, midway, vector_rows[5], vector_rows[6]
            )[1](normed_two_back)
            midway_back = midway_back + gradient
            attn_back = midway_back.astype(jnp.bfloat16)
            attended_back = contract_cols(attn_back, w_attn_out).astype(jnp.bfloat16)
            allowed = make_allowed(doc_own, doc_all, positions)
            scores = head_scores(queries, keys_all, allowed)
            probs = jnp.exp(scores - log_total)
            probs_low = probs.astype(jnp.bfloat16)
            query_heads = queries.reshape(row_count, HEADS, head_size)
            key_heads = keys_all.reshape(keys_all.shape[0], HEADS, head_size)
            value_heads = values_all.reshape(values_all.shape[0], HEADS, head_size)
            output_heads = attended_back.reshape(row_count, HEADS, head_size)
            probs_back = jnp.einsum(
                "qhd,khd->hqk", output_heads, value_heads, preferred_element_type=jnp.float32
            )
            row_dot = jnp.einsum(
                "qhd,qhd->hq",
                output_heads.astype(jnp.float32),
                attended.reshape(row_count, HEADS, head_size),
            )[:, :, None]
            scores_back = (probs * (probs_back - row_dot)).astype(jnp.bfloat16)
            queries_back = (
                (
                    jnp.einsum(
                        "hqk,khd->qhd", scores_back, key_heads, preferred_element_type=jnp.float32
                    )
                    * score_scale
                )
                .reshape(row_count, model_width)
                .astype(jnp.bfloat16)
            )

            def key_terms(
                offset,
                amount,
                scores_back=scores_back,
                probs_low=probs_low,
                query_heads=query_heads,
                output_heads=output_heads,
            ):
                keys_term = (
                    jnp.einsum(
                        "hqk,qhd->khd", scores_back, query_heads, preferred_element_type=jnp.float32
                    )
                    * score_scale
                )
                values_term = jnp.einsum(
                    "hqk,qhd->khd", probs_low, output_heads, preferred_element_type=jnp.float32
                )
                return jnp.concatenate(
                    [keys_term.reshape(amount, -1), values_term.reshape(amount, -1)], 1
                )

            key_value_back = lax.psum_scatter(
                key_terms(jnp.int32(0), lax.axis_size(("ctx", "tensor")) * row_count).astype(
                    jnp.bfloat16
                ),
                ("ctx", "tensor"),
                scatter_dimension=0,
                tiled=True,
            ).astype(jnp.float32)
            keys_back = key_value_back[:, :model_width].astype(jnp.bfloat16)
            values_back = key_value_back[:, model_width:].astype(jnp.bfloat16)
            projected_back = jnp.concatenate([queries_back, keys_back, values_back], 1)
            normed_back = contract_cols(projected_back, w_attn_in)
            input_back, gain_one_back, shift_one_back = jax.vjp(
                layer_norm, layer_input, vector_rows[0], vector_rows[1]
            )[1](normed_back)
            gradient = midway_back + input_back
            bias_up_full = lax.dynamic_update_slice_in_dim(
                jnp.zeros((FF,), jnp.float32),
                jnp.sum(preact_back.astype(jnp.float32), 0),
                tensor_index * hidden_half,
                0,
            )
            small_rows = jnp.stack(
                [
                    gain_one_back,
                    shift_one_back,
                    jnp.sum(queries_back.astype(jnp.float32), 0),
                    jnp.sum(values_back.astype(jnp.float32), 0),
                    jnp.sum(attn_back.astype(jnp.float32), 0),
                    gain_two_back,
                    shift_two_back,
                    jnp.sum(branch_back.astype(jnp.float32), 0),
                ]
            )
            vector_part = jnp.concatenate([small_rows, bias_up_full.reshape(-1, model_width)], 0)
            operands = (
                normed_low,
                projected_back,
                attended_low,
                attn_back,
                mlp_input,
                preact_back,
                rows_back,
                hidden,
                vector_part,
            )
            operands_here[layer_id] = operands
        operand_sets.append(operands_here)
        input_grads.append(gradient)
    for layer_id in range(layers):
        totals[layer_id] = reduce_layer(
            weight_terms([operands_here[layer_id] for operands_here in operand_sets])
        )
    stacked = [
        jnp.stack([totals[layer_id][slot_id] for layer_id in range(layers)]) for slot_id in range(5)
    ]
    return (
        jnp.stack(results),
        jnp.stack(input_grads),
        stacked[0],
        stacked[1],
        stacked[2],
        stacked[3],
        stacked[4],
    )


def solution(mesh):
    return jax.shard_map(
        body,
        mesh=mesh,
        in_specs=(
            P(None, ("dp", "ctx", "tensor"), None),
            P(None, "dp", None),
            P(None, "dp", None),
            P(None, "dp", "tensor"),
            P(None, "dp", "tensor"),
            P(None, None, "dp"),
            P(None, ("dp", "ctx", "tensor")),
            P(None, ("dp", "ctx", "tensor"), None),
        ),
        out_specs=(
            P(None, ("dp", "ctx", "tensor"), None),
            P(None, ("dp", "ctx", "tensor"), None),
            P(None, "dp", None),
            P(None, "dp", None),
            P(None, "dp", "tensor"),
            P(None, "dp", "tensor"),
            P(None, None, "dp"),
        ),
        check_vma=False,
    )
```

profile of v0, /device:TPU:0, one launch (start us, length us, event | category | flops | bytes accessed | tf_op | source)
XLA Modules:
  0.0 2259.3 jit_solution(7374891333641478565)
XLA Ops:
  18.4 27.5 %all-gather = bf16[1,12,1088]{1,0,2:T(2,128)(2,1)S(1)} all-gather(bf16[1,12,68]{1,0,2:T(2,128)(2,1)S(1)} %copy.230), channel_id=2, replica_groups=mesh['dp'=16,'ctx'=4,'tensor'=2] {'dp'}, dimensions={2}, use_global_device_ids=true | all-gather | bytes 27744 | tf_op jit(solution)/shard_map/all_gather | solution.py:46
  47.5 28.0 %slice_reduce_fusion.8 = (f32[1088]{0:T(1024)}, f32[1088]{0:T(1024)}, f32[1088]{0:T(1024)S(1)}, f32[1088]{0:T(1024)S(1)}, f32[1088]{0:T(1024)S(1)}, /*index=5*/f...) fusion(f32[1,12,1088]{1,0,2:T(1,128)S(1)} %convert_element_type.574), kind=kLoop, calls=%fused_computation.287 | loop fusion | bytes 69632 | tf_op jit(solution)/shard_map/slice | solution.py:213
  75.9 42.2 %all-gather.45.cloned.1.call-done = bf16[1,1088,3264]{2,0,1:T(2,128)(2,1)} async-done(((bf16[1,68,3264]{2,0,1:T(2,128)(2,1)}), bf16[1,1088,3264]{2,0,1:T(2,128)(2,1)}) %all-gather.45.cloned.1.call-update) | async-done | bytes 7102480 | tf_op jit(solution)/shard_map/all_gather | solution.py:42
  118.1 9.2 copy.222
  144.7 19.0 all-reduce.22
  164.5 13.8 all-gather.47.cloned.1.call-done
  181.1 76.3 %all-gather.49.cloned.1.call-done = bf16[1,1088,2176]{2,0,1:T(2,128)(2,1)} async-done(((bf16[1,68,2176]{2,0,1:T(2,128)(2,1)}), bf16[1,1088,2176]{2,0,1:T(2,128)(2,1)}) %all-gather.49.cloned.1.call-update) | async-done | bytes 4734992 | tf_op jit(solution)/shard_map/all_gather | solution.py:44
  257.3 6.6 copy.224
  263.9 71.5 %all-gather.51.cloned.1.call-done = bf16[1,1088,2176]{2,0,1:T(2,128)(2,1)} async-done(((bf16[1,68,2176]{2,0,1:T(2,128)(2,1)}), bf16[1,1088,2176]{2,0,1:T(2,128)(2,1)}) %all-gather.51.cloned.1.call-update) | async-done | bytes 4734992 | tf_op jit(solution)/shard_map/all_gather | solution.py:45
  335.4 6.6 copy.225
  342.4 33.2 %all-gather.39.cloned.1.call-done = bf16[512,1088]{1,0:T(8,128)(2,1)} async-done(((bf16[64,1088]{1,0:T(8,128)(2,1)}), bf16[512,1088]{1,0:T(8,128)(2,1)}) %all-gather.39.cloned.1.call-update) | async-done | bytes 1114128 | tf_op jit(solution)/shard_map/all_gather | solution.py:155
  378.0 40.0 %all-gather.37.cloned.1.call-done = bf16[512,1088]{1,0:T(8,128)(2,1)} async-done(((bf16[64,1088]{1,0:T(8,128)(2,1)}), bf16[512,1088]{1,0:T(8,128)(2,1)}) %all-gather.37.cloned.1.call-update) | async-done | bytes 1114128 | tf_op jit(solution)/shard_map/all_gather | solution.py:156
  420.4 40.2 %all-gather.29.cloned.1.call-done = bf16[512,1088]{1,0:T(8,128)(2,1)} async-done(((bf16[64,1088]{1,0:T(8,128)(2,1)}), bf16[512,1088]{1,0:T(8,128)(2,1)}) %all-gather.29.cloned.1.call-update) | async-done | bytes 1114128 | tf_op jit(solution)/shard_map/all_gather | solution.py:156
  462.9 39.6 %all-gather.31.cloned.1.call-done = bf16[512,1088]{1,0:T(8,128)(2,1)} async-done(((bf16[64,1088]{1,0:T(8,128)(2,1)}), bf16[512,1088]{1,0:T(8,128)(2,1)}) %all-gather.31.cloned.1.call-update) | async-done | bytes 1114128 | tf_op jit(solution)/shard_map/all_gather | solution.py:155
  517.2 10.2 all_gather.62
  527.4 5.8 all_gather.148
  541.0 6.1 multiply_convert_fusion.11
  548.0 5.7 fusion.90
  555.8 26.5 %all-gather.6 = bf16[1,12,1088]{1,0,2:T(2,128)(2,1)S(1)} all-gather(bf16[1,12,68]{1,0,2:T(2,128)(2,1)S(1)} %copy.231), channel_id=8, replica_groups=mesh['dp'=16,'ctx'=4,'tensor'=2] {'dp'}, dimensions={2}, use_global_device_ids=true | all-gather | bytes 27744 | tf_op jit(solution)/shard_map/all_gather | solution.py:46
  582.9 27.9 %slice_reduce_fusion = (f32[1088]{0:T(1024)}, f32[1088]{0:T(1024)}, f32[1088]{0:T(1024)S(1)}, f32[1088]{0:T(1024)}, f32[1088]{0:T(1024)S(1)}, /*index=5*/f32[1088]{0:T(1024)S(1)}, f32[1088]{0:T(1024)S(1)}, f32[1088]{0:T(1024)S(1)}) fusion(f32[1,12,1088]{1,0,2:T(1,128)S(1)} %convert_element_type.575), kind=kLoop, calls=%fused_computation.279 | loop fusion | bytes 69632 | tf_op jit(solution)/shard_map/slice | solution.py:213
  612.9 9.2 copy.226
  627.5 17.9 reduce-scatter.39.cloned.1.call-done
  663.5 6.4 all_gather.152
  669.9 5.9 all_gather.154
  675.8 32.0 %all-gather.55.cloned.1.call-done = bf16[1,1088,1088]{2,0,1:T(2,128)(2,1)} async-done(((bf16[1,68,1088]{2,0,1:T(2,128)(2,1)}), bf16[1,1088,1088]{2,0,1:T(2,128)(2,1)}) %all-gather.55.cloned.1.call-update) | async-done | bytes 2367504 | tf_op jit(solution)/shard_map/all_gather | solution.py:43
  710.6 76.4 %all-gather.57.cloned.1.call-done = bf16[1,1088,2176]{2,0,1:T(2,128)(2,1)} async-done(((bf16[1,68,2176]{2,0,1:T(2,128)(2,1)}), bf16[1,1088,2176]{2,0,1:T(2,128)(2,1)}) %all-gather.57.cloned.1.call-update) | async-done | bytes 4734992 | tf_op jit(solution)/shard_map/all_gather | solution.py:44
  787.0 6.6 copy.228
  793.6 70.9 %all-gather.59.cloned.1.call-done = bf16[1,1088,2176]{2,0,1:T(2,128)(2,1)} async-done(((bf16[1,68,2176]{2,0,1:T(2,128)(2,1)}), bf16[1,1088,2176]{2,0,1:T(2,128)(2,1)}) %all-gather.59.cloned.1.call-update) | async-done | bytes 4734992 | tf_op jit(solution)/shard_map/all_gather | solution.py:45
  864.5 6.6 copy.229
  874.7 30.0 %all-gather.35.cloned.1.call-done = bf16[512,1088]{1,0:T(8,128)(2,1)} async-done(((bf16[64,1088]{1,0:T(8,128)(2,1)}), bf16[512,1088]{1,0:T(8,128)(2,1)}) %all-gather.35.cloned.1.call-update) | async-done | bytes 1114128 | tf_op jit(solution)/shard_map/all_gather | solution.py:155
  911.9 34.7 %all-gather.33.cloned.1.call-done = bf16[512,1088]{1,0:T(8,128)(2,1)} async-done(((bf16[64,1088]{1,0:T(8,128)(2,1)}), bf16[512,1088]{1,0:T(8,128)(2,1)}) %all-gather.33.cloned.1.call-update) | async-done | bytes 1114128 | tf_op jit(solution)/shard_map/all_gather | solution.py:156
  949.0 39.4 %all-gather.43.cloned.1.call-done = bf16[512,1088]{1,0:T(8,128)(2,1)} async-done(((bf16[64,1088]{1,0:T(8,128)(2,1)}), bf16[512,1088]{1,0:T(8,128)(2,1)}) %all-gather.43.cloned.1.call-update) | async-done | bytes 1114128 | tf_op jit(solution)/shard_map/all_gather | solution.py:155
  998.2 31.9 %all-gather.41.cloned.1.call-done = bf16[512,1088]{1,0:T(8,128)(2,1)} async-done(((bf16[64,1088]{1,0:T(8,128)(2,1)}), bf16[512,1088]{1,0:T(8,128)(2,1)}) %all-gather.41.cloned.1.call-update) | async-done | bytes 1114128 | tf_op jit(solution)/shard_map/all_gather | solution.py:156
  1037.5 6.5 all_gather.70
  1044.0 5.8 all_gather.151
  1061.8 6.2 multiply_convert_fusion.10
  1068.0 6.2 convert_reduce_fusion.1
  1099.6 11.7 reduce-scatter.45.cloned.1.call-done
  1111.3 17.9 reduce-scatter.41.cloned.1.call-done
  1170.0 34.3 %reduce-scatter.59.cloned.1.call-done = bf16[64,2176]{1,0:T(8,128)(2,1)} async-done(((bf16[512,2176]{1,0:T(8,128)(2,1)}), bf16[64,2176]{1,0:T(8,128)(2,1)}) %reduce-scatter.59.cloned.1.call-update) | async-done | bytes 278544
  1205.6 5.6 fusion.8
  1211.2 49.8 %reduce-scatter.55.cloned.1.call-done = bf16[64,2176]{1,0:T(8,128)(2,1)} async-done(((bf16[512,2176]{1,0:T(8,128)(2,1)}), bf16[64,2176]{1,0:T(8,128)(2,1)}) %reduce-scatter.55.cloned.1.call-update) | async-done | bytes 278544
  1262.4 6.1 multiply_reduce_fusion.1
  1270.2 6.3 all_gather.153
  1277.3 5.8 all_gather.155
  1290.1 6.5 convert_reduce_fusion.2
  1304.2 17.8 reduce-scatter.53.cloned.1.call-done
  1415.6 39.5 %reduce-scatter.61.cloned.1.call-done = bf16[64,2176]{1,0:T(8,128)(2,1)} async-done(((bf16[512,2176]{1,0:T(8,128)(2,1)}), bf16[64,2176]{1,0:T(8,128)(2,1)}) %reduce-scatter.61.cloned.1.call-update) | async-done | bytes 278544
  1458.3 6.4 fusion.16
  1469.8 425.5 %fusion.350 = (bf16[72,3264]{1,0:T(8,128)(2,1)}, bf16[72,3264]{1,0:T(8,128)(2,1)}, bf16[80,1088]{1,0:T(8,128)(2,1)}, bf16[80,1088]{1,0:T(8,128)(2,1)}, bf16[80,2...) fusion(bf16[1088,3264]{1,0:T(8,128)(2,1)} %convolution_convert_fusion, ...), kind=kCustom, calls=%all-reduce-scatter.8 | all-reduce-scatter fusion | flops 21446656 | bytes 40561152
  1896.1 36.7 %collective-permute-start.6 = (bf16[80,1088]{1,0:T(8,128)(2,1)}, bf16[80,1088]{1,0:T(8,128)(2,1)}, u32[]{:S(2)}, u32[]{:S(2)}) collective-permute-start(bf16[80,1088]{1,0:T(8,128)(2,1)} %get-tuple-element.111), channel_id=1, source_target_pairs={{0,16},{8,24},{16,32},{24,40},{32,48},{40,56},{48,64},{56,72},{64,... | collective-permute-start | bytes 522248
  1936.2 6.6 collective-permute-start.11
  1943.6 5.6 fusion.287
  1958.1 67.7 %all-reduce.20 = (bf16[12,1088]{1,0:T(8,128)(2,1)S(1)}, bf16[12,1088]{1,0:T(8,128)(2,1)}) all-reduce(bf16[12,1088]{1,0:T(8,128)(2,1)S(1)} %add_convert_fusion.10, bf16[12,1088]{1,0:T(8,128)(2,1)S(1)} %add_convert_fusion.11), channel_id=35, replica_groups=mesh['dp'=16,'ctx'=4,'tensor'=2] {'dp'}, use_global_device_ids=true, to_apply=%region_106.107.clone | all-reduce | flops 26112 | bytes 104448
  2033.7 6.5 concatenate.123
  2048.3 7.6 concatenate.125
  2056.7 8.7 collective-permute-start.15
  2071.1 7.6 concatenate.124
  2083.6 6.5 collective-permute-start.16
  2090.1 7.6 concatenate.127
  2108.0 7.6 concatenate.126
  2130.0 16.9 all-reduce.21
  2148.4 11.7 all-reduce.31.cloned.1.call-done
  2164.6 83.0 %all-reduce.29.cloned.1.call-done = (bf16[1,68,3264]{2,1,0:T(8,128)(2,1)}, bf16[1,68,3264]{2,1,0:T(8,128)(2,1)}, bf16[1,68,1088]{2,1,0:T(8,128)(2,1)}, bf16[1,68,1088]{2,1,0:T(8,128)(2,1)}) async-done(((bf16[1,68,3264]{2,1,0:T(8,128)(2,1)}, bf16[1,68,3264]{2,1,0:T(8,128)(2,1)}, bf16[1,68,1088]{2,1,0:T(8,128)(2,1)}, bf16[1,68,1088]{2,1,0:T(8,128)(2,1)}), (bf16[1,68,3264]{2,1,0:T(8,128)(2,1)}, ...) | async-done | bytes 1183760 | tf_op jit(solution)/shard_map/psum | solution.py:116
  (927 shorter events, 397.0 us)
Async XLA Ops:
  7.2 110.9 %all-gather.45.cloned.1.call-start = ((), (), s32[]{:S(2)}) async-start(), calls=%async_computation.28 | async-start | bytes 15388672 | tf_op jit(solution)/shard_map/all_gather | solution.py:42
  11.5 166.8 %all-gather.47.cloned.1.call-start = ((), (), s32[]{:S(2)}) async-start(), calls=%async_computation.29 | async-start | bytes 5326848 | tf_op jit(solution)/shard_map/all_gather | solution.py:43
  13.7 243.6 %all-gather.49.cloned.1.call-start = ((), (), s32[]{:S(2)}) async-start(), calls=%async_computation.30 | async-start | bytes 10061824 | tf_op jit(solution)/shard_map/all_gather | solution.py:44
  15.7 319.7 %all-gather.51.cloned.1.call-start = ((), (), s32[]{:S(2)}) async-start(), calls=%async_computation.31 | async-start | bytes 10061824 | tf_op jit(solution)/shard_map/all_gather | solution.py:45
  17.6 358.0 %all-gather.39.cloned.1.call-start = ((), (), s32[]{:S(2)}) async-start(), calls=%async_computation.19 | async-start | bytes 1327104 | tf_op jit(solution)/shard_map/all_gather | solution.py:155
  75.5 441.4 %copy-start.137 = (f32[1088]{0:T(1024)}, f32[1088]{0:T(1024)S(1)}, u32[]{:S(2)}) copy-start(f32[1088]{0:T(1024)S(1)} %get-tuple-element.53) | copy-start | bytes 13060
  75.8 56.8 %copy-start.80 = (bf16[64,1088]{1,0:T(8,128)(2,1)}, bf16[64,1088]{1,0:T(8,128)(2,1)S(1)}, u32[]{:S(2)}) copy-start(bf16[64,1088]{1,0:T(8,128)(2,1)S(1)} %get-tuple-element.166) | copy-start | bytes 417796
  132.6 285.5 %all-gather.37.cloned.1.call-start = ((), (), s32[]{:S(2)}) async-start(), calls=%async_computation.18 | async-start | bytes 1327104 | tf_op jit(solution)/shard_map/all_gather | solution.py:156
  137.7 322.9 %all-gather.29.cloned.1.call-start = ((), (), s32[]{:S(2)}) async-start(), calls=%async_computation.12 | async-start | bytes 1327104 | tf_op jit(solution)/shard_map/all_gather | solution.py:156
  138.5 364.0 %all-gather.31.cloned.1.call-start = ((), (), s32[]{:S(2)}) async-start(), calls=%async_computation.13 | async-start | bytes 1327104 | tf_op jit(solution)/shard_map/all_gather | solution.py:155
  139.3 473.6 %all-gather.53.cloned.1.call-start = ((), (), s32[]{:S(2)}) async-start(), calls=%async_computation.32 | async-start | bytes 15388672 | tf_op jit(solution)/shard_map/all_gather | solution.py:42
  140.0 487.4 %reduce-scatter.43.cloned.1.call-start = ((), (), s32[]{:S(2)}) async-start(), calls=%async_computation.20 | async-start | bytes 442368 | tf_op jit(solution)/shard_map/reduce_scatter | solution.py:189
  181.1 334.9 %copy-start = (bf16[1,1088,1088]{2,1,0:T(8,128)(2,1)}, bf16[1,1088,1088]{2,1,0:T(8,128)(2,1)S(1)}, u32[]{:S(2)}) copy-start(bf16[1,1088,1088]{2,1,0:T(8,128)(2,1)S(1)} %copy.223) | copy-start | bytes 7102468
  342.2 169.0 %copy-start.57 = (bf16[64,1088]{0,1:T(8,128)(2,1)}, bf16[64,1088]{0,1:T(8,128)(2,1)S(1)}, u32[]{:S(2)}) copy-start(bf16[64,1088]{0,1:T(8,128)(2,1)S(1)} %copy.142) | copy-start | bytes 417796
  342.4 162.4 %copy-start.59 = (bf16[64,1088]{0,1:T(8,128)(2,1)}, bf16[64,1088]{0,1:T(8,128)(2,1)S(1)}, u32[]{:S(2)}) copy-start(bf16[64,1088]{0,1:T(8,128)(2,1)S(1)} %copy.131) | copy-start | bytes 417796
  540.9 104.4 %reduce-scatter.39.cloned.1.call-start = ((), (), s32[]{:S(2)}) async-start(), calls=%async_computation.14 | async-start | bytes 442368 | tf_op jit(solution)/shard_map/reduce_scatter | solution.py:189
  553.7 154.1 %all-gather.55.cloned.1.call-start = ((), (), s32[]{:S(2)}) async-start(), calls=%async_computation.33 | async-start | bytes 5326848 | tf_op jit(solution)/shard_map/all_gather | solution.py:43
  554.3 232.7 %all-gather.57.cloned.1.call-start = ((), (), s32[]{:S(2)}) async-start(), calls=%async_computation.34 | async-start | bytes 10061824 | tf_op jit(solution)/shard_map/all_gather | solution.py:44
  555.0 309.4 %all-gather.59.cloned.1.call-start = ((), (), s32[]{:S(2)}) async-start(), calls=%async_computation.35 | async-start | bytes 10061824 | tf_op jit(solution)/shard_map/all_gather | solution.py:45
  555.6 349.1 %all-gather.35.cloned.1.call-start = ((), (), s32[]{:S(2)}) async-start(), calls=%async_computation.16 | async-start | bytes 1327104 | tf_op jit(solution)/shard_map/all_gather | solution.py:155
  652.7 293.8 %all-gather.33.cloned.1.call-start = ((), (), s32[]{:S(2)}) async-start(), calls=%async_computation.15 | async-start | bytes 1327104 | tf_op jit(solution)/shard_map/all_gather | solution.py:156
  657.9 330.4 %all-gather.43.cloned.1.call-start = ((), (), s32[]{:S(2)}) async-start(), calls=%async_computation.22 | async-start | bytes 1327104 | tf_op jit(solution)/shard_map/all_gather | solution.py:155
  658.7 371.4 %all-gather.41.cloned.1.call-start = ((), (), s32[]{:S(2)}) async-start(), calls=%async_computation.21 | async-start | bytes 1327104 | tf_op jit(solution)/shard_map/all_gather | solution.py:156
  874.6 214.1 %reduce-scatter.51.cloned.1.call-start = ((), (), s32[]{:S(2)}) async-start(), calls=%async_computation.26 | async-start | bytes 442368 | tf_op jit(solution)/shard_map/reduce_scatter | solution.py:251
  1061.3 32.1 %reduce-scatter.47.cloned.1.call-start = ((), (), s32[]{:S(2)}) async-start(), calls=%async_computation.24 | async-start | bytes 442368 | tf_op jit(solution)/shard_map/reduce_scatter | solution.py:251
  1077.3 34.0 %reduce-scatter.45.cloned.1.call-start = ((), (), s32[]{:S(2)}) async-start(), calls=%async_computation.23 | async-start | bytes 442368 | tf_op jit(solution)/shard_map/reduce_scatter | solution.py:189
  1082.2 47.0 %reduce-scatter.41.cloned.1.call-start = ((), (), s32[]{:S(2)}) async-start(), calls=%async_computation.17 | async-start | bytes 442368 | tf_op jit(solution)/shard_map/reduce_scatter | solution.py:189
  1088.5 115.8 %reduce-scatter.59.cloned.1.call-start = ((), (), s32[]{:S(2)}) async-start(), calls=%async_computation.38 | async-start | bytes 2506752
  1148.1 112.9 %reduce-scatter.55.cloned.1.call-start = ((), (), s32[]{:S(2)}) async-start(), calls=%async_computation.36 | async-start | bytes 2506752
  1162.1 142.1 %reduce-scatter.49.cloned.1.call-start = ((), (), s32[]{:S(2)}) async-start(), calls=%async_computation.25 | async-start | bytes 442368 | tf_op jit(solution)/shard_map/reduce_scatter | solution.py:251
  1170.0 92.3 %copy-start.53 = (bf16[64,17,64]{0,2,1:T(8,128)(2,1)}, bf16[64,17,64]{0,2,1:T(8,128)(2,1)S(1)}, u32[]{:S(2)}) copy-start(bf16[64,17,64]{0,2,1:T(8,128)(2,1)S(1)} %copy.151) | copy-start | bytes 417796
  1205.6 77.5 %slice-start.8 = ((s8[4734976]{0:T(1024)(128)(4,1)}), s8[540672]{0:T(1024)(128)(4,1)S(1)}, s32[]{:S(2)}) async-start(s8[4734976]{0:T(1024)(128)(4,1)} %bitcast.465), calls=%async_computation.50 | async-start | bytes 1081344
  1290.1 31.9 %reduce-scatter.53.cloned.1.call-start = ((), (), s32[]{:S(2)}) async-start(), calls=%async_computation.27 | async-start | bytes 442368 | tf_op jit(solution)/shard_map/reduce_scatter | solution.py:251
  1299.1 115.0 %reduce-scatter.57.cloned.1.call-start = ((), (), s32[]{:S(2)}) async-start(), calls=%async_computation.37 | async-start | bytes 2506752
  1342.0 113.1 %reduce-scatter.61.cloned.1.call-start = ((), (), s32[]{:S(2)}) async-start(), calls=%async_computation.39 | async-start | bytes 2506752
  1352.8 807.3 %all-reduce.31.cloned.1.call-start = ((), (), s32[]{:S(2)}) async-start(), calls=%async_computation.41 | async-start | bytes 2506752 | tf_op jit(solution)/shard_map/psum | solution.py:121
  1469.8 473.7 %copy-start.11 = (bf16[2,64,1088]{2,1,0:T(8,128)(2,1)S(1)}, bf16[2,64,1088]{2,1,0:T(8,128)(2,1)}, u32[]{:S(2)}) copy-start(bf16[2,64,1088]{2,1,0:T(8,128)(2,1)} %param.8) | copy-start | bytes 835588
  1469.8 473.7 %copy-start.140 = (f32[1088]{0:T(1024)S(1)}, f32[1088]{0:T(1024)}, u32[]{:S(2)}) copy-start(f32[1088]{0:T(1024)} %copy-done.139) | copy-start | bytes 13060
  1469.8 473.7 %copy-start.194 = (f32[64]{0:T(128)S(1)}, f32[64]{0:T(128)}, u32[]{:S(2)}) copy-start(f32[64]{0:T(128)} %copy-done.193) | copy-start | bytes 772
  1469.8 473.7 %copy-start.197 = (f32[64]{0:T(128)S(1)}, f32[64]{0:T(128)}, u32[]{:S(2)}) copy-start(f32[64]{0:T(128)} %copy-done.196) | copy-start | bytes 772
  1896.1 131.2 %collective-permute-start.6 = (bf16[80,1088]{1,0:T(8,128)(2,1)}, bf16[80,1088]{1,0:T(8,128)(2,1)}, u32[]{:S(2)}, u32[]{:S(2)}) collective-permute-start(bf16[80,1088]{1,0:T(8,128)(2,1)} %get-tuple-element.111), channel_id=1, source_target_pairs={{0,16},{8,24},{16,32},{24,40},{32,48},{40,56},{48,64},{56,72},{64,... | collective-permute-start | bytes 522248
  1932.7 96.5 %collective-permute-start.5 = (bf16[80,1088]{1,0:T(8,128)(2,1)}, bf16[80,1088]{1,0:T(8,128)(2,1)}, u32[]{:S(2)}, u32[]{:S(2)}) collective-permute-start(bf16[80,1088]{1,0:T(8,128)(2,1)} %get-tuple-element.111), channel_id=1, source_target_pairs={{0,8},{8,16},{16,24},{24,32},{32,40},{40,48},{48,56},{56,64},{64,7... | collective-permute-start | bytes 522248
  1934.7 107.5 %collective-permute-start.12 = (bf16[80,2176]{1,0:T(8,128)(2,1)}, bf16[80,2176]{1,0:T(8,128)(2,1)S(1)}, u32[]{:S(2)}, u32[]{:S(2)}) collective-permute-start(bf16[80,2176]{1,0:T(8,128)(2,1)} %get-tuple-element.113), channel_id=1, source_target_pairs={{0,16},{8,24},{16,32},{24,40},{32,48},{40,56},{48,64},{56,72},{64,... | collective-permute-start | bytes 1044488
  1936.2 108.0 %collective-permute-start.11 = (bf16[80,2176]{1,0:T(8,128)(2,1)}, bf16[80,2176]{1,0:T(8,128)(2,1)}, u32[]{:S(2)}, u32[]{:S(2)}) collective-permute-start(bf16[80,2176]{1,0:T(8,128)(2,1)} %get-tuple-element.113), channel_id=1, source_target_pairs={{0,8},{8,16},{16,24},{24,32},{32,40},{40,48},{48,56},{56,64},{64,7... | collective-permute-start | bytes 1044488
  1950.9 74.9 %collective-permute-start.7 = (bf16[20,1088]{1,0:T(8,128)(2,1)S(1)}, bf16[20,1088]{1,0:T(8,128)(2,1)}, u32[]{:S(2)}, u32[]{:S(2)}) collective-permute-start(bf16[20,1088]{1,0:T(8,128)(2,1)S(1)} %slice.333), channel_id=1, source_target_pairs={{0,24},{8,32},{16,40},{24,48},{32,56},{40,64},{48,72},{56,80},{64,... | collective-permute-start | bytes 130568
  1954.2 77.1 %copy-start.84 = (bf16[80,2176]{1,0:T(8,128)(2,1)S(1)}, bf16[80,2176]{1,0:T(8,128)(2,1)}, u32[]{:S(2)}) copy-start(bf16[80,2176]{1,0:T(8,128)(2,1)} %get-tuple-element.116) | copy-start | bytes 1044484
  1954.2 77.7 %copy-start.44 = (bf16[72,3264]{1,0:T(8,128)(2,1)S(1)}, bf16[72,3264]{1,0:T(8,128)(2,1)}, u32[]{:S(2)}) copy-start(bf16[72,3264]{1,0:T(8,128)(2,1)} %get-tuple-element.109) | copy-start | bytes 1410052
  1954.4 78.5 %copy-start.45 = (bf16[72,3264]{1,0:T(8,128)(2,1)S(1)}, bf16[72,3264]{1,0:T(8,128)(2,1)}, u32[]{:S(2)}) copy-start(bf16[72,3264]{1,0:T(8,128)(2,1)} %get-tuple-element.110) | copy-start | bytes 1410052
  2025.8 14.3 collective-permute-start.13
  2027.2 38.2 %collective-permute-start.9 = (bf16[80,2176]{1,0:T(8,128)(2,1)S(1)}, bf16[80,2176]{1,0:T(8,128)(2,1)}, u32[]{:S(2)}, u32[]{:S(2)}) collective-permute-start(bf16[80,2176]{1,0:T(8,128)(2,1)S(1)} %copy-done.86), channel_id=1, source_target_pairs={{0,16},{8,24},{16,32},{24,40},{32,48},{40,56},{48,64},{56,72},{64,... | collective-permute-start | bytes 1044488
  2029.2 38.6 %collective-permute-start.8 = (bf16[80,2176]{1,0:T(8,128)(2,1)S(1)}, bf16[80,2176]{1,0:T(8,128)(2,1)}, u32[]{:S(2)}, u32[]{:S(2)}) collective-permute-start(bf16[80,2176]{1,0:T(8,128)(2,1)S(1)} %copy-done.86), channel_id=1, source_target_pairs={{0,8},{8,16},{16,24},{24,32},{32,40},{40,48},{48,56},{56,64},{64,7... | collective-permute-start | bytes 1044488
  2040.1 41.7 %collective-permute-start.18 = (bf16[80,2176]{1,0:T(8,128)(2,1)S(1)}, bf16[80,2176]{1,0:T(8,128)(2,1)}, u32[]{:S(2)}, u32[]{:S(2)}) collective-permute-start(bf16[80,2176]{1,0:T(8,128)(2,1)S(1)} %copy-done.85), channel_id=1, source_target_pairs={{0,16},{8,24},{16,32},{24,40},{32,48},{40,56},{48,64},{56,72},{64,... | collective-permute-start | bytes 1044488
  2042.2 41.4 %collective-permute-start.17 = (bf16[80,2176]{1,0:T(8,128)(2,1)S(1)}, bf16[80,2176]{1,0:T(8,128)(2,1)}, u32[]{:S(2)}, u32[]{:S(2)}) collective-permute-start(bf16[80,2176]{1,0:T(8,128)(2,1)S(1)} %copy-done.85), channel_id=1, source_target_pairs={{0,8},{8,16},{16,24},{24,32},{32,40},{40,48},{48,56},{56,64},{64,7... | collective-permute-start | bytes 1044488
  2044.2 12.5 collective-permute-start.10
  2056.7 43.7 %collective-permute-start.15 = (bf16[80,2176]{1,0:T(8,128)(2,1)S(1)}, bf16[80,2176]{1,0:T(8,128)(2,1)}, u32[]{:S(2)}, u32[]{:S(2)}) collective-permute-start(bf16[80,2176]{1,0:T(8,128)(2,1)S(1)} %copy-done.84), channel_id=1, source_target_pairs={{0,16},{8,24},{16,32},{24,40},{32,48},{40,56},{48,64},{56,72},{64,... | collective-permute-start | bytes 1044488
  2065.4 37.3 %collective-permute-start.14 = (bf16[80,2176]{1,0:T(8,128)(2,1)S(1)}, bf16[80,2176]{1,0:T(8,128)(2,1)}, u32[]{:S(2)}, u32[]{:S(2)}) collective-permute-start(bf16[80,2176]{1,0:T(8,128)(2,1)S(1)} %copy-done.84), channel_id=1, source_target_pairs={{0,8},{8,16},{16,24},{24,32},{32,40},{40,48},{48,56},{56,64},{64,7... | collective-permute-start | bytes 1044488
  2067.8 11.8 collective-permute-start.19
  2079.6 38.6 %collective-permute-start.3 = (bf16[80,1088]{1,0:T(8,128)(2,1)S(1)}, bf16[80,1088]{1,0:T(8,128)(2,1)S(1)}, u32[]{:S(2)}, u32[]{:S(2)}) collective-permute-start(bf16[80,1088]{1,0:T(8,128)(2,1)S(1)} %copy-done.125), channel_id=1, source_target_pairs={{0,16},{8,24},{16,32},{24,40},{32,48},{40,56},{48,64},{56,72},{64,... | collective-permute-start | bytes 522248
  2081.8 36.3 %collective-permute-start.2 = (bf16[80,1088]{1,0:T(8,128)(2,1)S(1)}, bf16[80,1088]{1,0:T(8,128)(2,1)S(1)}, u32[]{:S(2)}, u32[]{:S(2)}) collective-permute-start(bf16[80,1088]{1,0:T(8,128)(2,1)S(1)} %copy-done.125), channel_id=1, source_target_pairs={{0,8},{8,16},{16,24},{24,32},{32,40},{40,48},{48,56},{56,64},{64,7... | collective-permute-start | bytes 522248
  2083.6 15.0 collective-permute-start.16
  2098.5 19.6 collective-permute-start.4
  2100.4 20.6 collective-permute-start
  2102.7 20.7 collective-permute-start.1
  2116.4 131.2 %all-reduce.29.cloned.1.call-start = ((), (), s32[]{:S(2)}) async-start(), calls=%async_computation.40 | async-start | bytes 2580480 | tf_op jit(solution)/shard_map/psum | solution.py:116
  (256 other events, 2142.7 us)
Sparse Core Ops, SparseCore 0:
  11.6 106.3 all-gather.44
  121.2 57.0 all-gather.46
  181.4 75.9 all-gather.48
  260.3 75.0 all-gather.50
  336.9 38.7 all-gather.38
  377.7 40.2 all-gather.36
  420.2 40.2 all-gather.28
  462.2 40.2 all-gather.30
  504.8 107.9 all-gather.52
  615.1 12.3 reduce-scatter.42
  629.8 15.5 reduce-scatter.38
  647.7 60.0 all-gather.54
  710.9 76.0 all-gather.56
  789.4 75.0 all-gather.58
  865.9 38.7 all-gather.34
  906.2 40.2 all-gather.32
  948.0 40.2 all-gather.42
  989.8 40.2 all-gather.40
  1061.4 14.1 reduce-scatter.50
  1077.8 15.5 reduce-scatter.46
  1095.7 15.5 reduce-scatter.44
  1113.6 15.5 reduce-scatter.40
  1148.2 56.0 reduce-scatter.58
  1206.7 54.2 reduce-scatter.54
  1290.2 13.9 reduce-scatter.48
  1306.4 15.5 reduce-scatter.52
  1342.1 56.0 reduce-scatter.56
  1400.8 54.2 reduce-scatter.60
  2116.5 43.4 all-reduce.30
  2163.5 84.0 all-reduce.28
where the time goes:
time: 2270 us; the launch traced here: 2260 us
  waiting for transfers between devices  975 us (43%)
  blocking collectives  636 us (28%)
  local copies, waits for them, and re-layouts  293 us (13%)
  matrix products  186 us (8%)
  starting transfers between devices  99.5 us (4%)
  other arithmetic  49.6 us (2%)
    unnamed x3, blocking collectives  512 us
    all_gather x2, waiting for transfers between devices, fetch_layer(): lax.all_gather(up_weight[layer_id], 'dp', axis=0, tiled=True)  153 us
    unnamed x585, local copies, waits for them, and re-layouts  152 us
    all_gather x4, waiting for transfers between devices, body(): lax.all_gather(values_own, ('ctx', 'tensor'), axis=0, tiled=True)  147 us
    all_gather x2, waiting for transfers between devices, fetch_layer(): lax.all_gather(down_weight[layer_id], 'dp', axis=0, tiled=True)  142 us
    all_gather x4, waiting for transfers between devices, body(): lax.all_gather(keys_own, ('ctx', 'tensor'), axis=0, tiled=True)  142 us
    unnamed x54, waiting for transfers between devices  127 us
    unnamed x24, starting transfers between devices  97.4 us
  transfers between devices with their start and end apart: 50, of which 28 were waited for; matrix products, arithmetic and copies ran while one was open for 18% of the time, Pallas kernels for 0%

commit v1 on v0

v1 whole, which is shorter than its diff:
```python
import functools

import jax
import jax.numpy as jnp
from jax import lax
from jax.experimental import pallas as pl
from jax.experimental.pallas import tpu as pltpu
from jax.sharding import PartitionSpec as P

EPSILON = 1e-05
MASKED = -1e30
MESH = pl.DeviceIdType.MESH
F32 = jnp.float32
BF16 = jnp.bfloat16
GROUP = 8
SLOTS = 5
HEAD = 64
WINDOW = 384
STRIDE = 256
PADDED = 1152
CHUNK = 128


def places():
    dp = lax.axis_index("dp")
    return {
        "x": dp // 4,
        "y": (dp // 2) % 2,
        "c": dp % 2,
        "z": lax.axis_index("ctx"),
        "t": lax.axis_index("tensor"),
    }


def shifted(value, x=0, y=0, c=0, z=0, t=0):
    pairs = []
    for i in range(128):
        ix, iy, ic, iz, it = i // 32, (i // 16) % 2, (i // 8) % 2, (i // 2) % 4, i % 2
        ix, iy, ic, iz, it = (ix + x) % 4, (iy + y) % 2, (ic + c) % 2, (iz + z) % 4, (it + t) % 2
        pairs.append((i, (((ix * 2 + iy) * 2 + ic) * 4 + iz) * 2 + it))
    return lax.ppermute(value, ("dp", "ctx", "tensor"), pairs)


def pair_up(first, mine, other):
    return jnp.where(first, jnp.concatenate([mine, other], 0), jnp.concatenate([other, mine], 0))


def ring_gather(axis, piece):
    half = piece.shape[0] // 2
    below = shifted(piece, **{axis: 1})
    above = shifted(piece, **{axis: -1})
    far_a = shifted(below[:half], **{axis: 1})
    far_b = shifted(above[half:], **{axis: -1})
    return {0: piece, -1: below, 1: above, 2: jnp.concatenate([far_a, far_b], 0)}


def ring_sum(axis, me, piece_of):
    far = piece_of((me + 2) % 4)
    half = far.shape[0] // 2
    via_up = shifted(far[:half], **{axis: 1})
    via_down = shifted(far[half:], **{axis: -1})
    up = piece_of((me + 1) % 4).astype(F32)
    down = piece_of((me + 3) % 4).astype(F32)
    up = jnp.concatenate([up[:half] + via_up.astype(F32), up[half:]], 0).astype(BF16)
    down = jnp.concatenate([down[:half], down[half:] + via_down.astype(F32)], 0).astype(BF16)
    from_below = shifted(up, **{axis: 1})
    from_above = shifted(down, **{axis: -1})
    total = piece_of(me).astype(F32) + from_below.astype(F32) + from_above.astype(F32)
    return total.astype(BF16)


def attn_start(z):
    return (z * 13) // 3 * 128


def mlp_start(z):
    return z * 512


QUARTER = 640


def columns(array, start):
    return lax.dynamic_slice_in_dim(array, pl.multiple_of(start, 128), QUARTER, 1)


def rows_of(array, start, count):
    return lax.dynamic_slice_in_dim(array, start, count, 0)


def padded(matrix, extra=None):
    rows, width = matrix.shape
    parts = [matrix]
    if extra is not None:
        parts.append(extra)
        width += extra.shape[1]
    parts.append(jnp.zeros((rows, PADDED - width), matrix.dtype))
    return jnp.concatenate(parts, 1)


def gather_layer(at, qkv, out, up, down, vec):
    width = out.shape[1]
    rows = out.shape[0]
    c0, y0 = at["c"] == 0, at["y"] == 0
    role0 = jnp.concatenate([padded(qkv[:, :width], vec.T), padded(qkv[:, width : 2 * width])], 1)
    role1 = jnp.concatenate([padded(qkv[:, 2 * width :]), padded(out)], 1)
    start = attn_start(at["z"])
    role0, role1 = columns(role0, start), columns(role1, start)

    def two_level(a, b):
        mine, give = jnp.where(c0, a, b), jnp.where(c0, b, a)
        pair = pair_up(c0, mine, shifted(give, c=1))
        return pair_up(y0, pair, shifted(pair, y=1))

    own = two_level(role0, role1)
    quarter = jnp.zeros((width, QUARTER), BF16)
    for distance, piece in ring_gather("x", own).items():
        quarter = lax.dynamic_update_slice(
            quarter, piece, ((at["x"] + distance) % 4 * (4 * rows), 0)
        )
    attn = jnp.zeros((2, width, 2 * PADDED), BF16)
    for distance, piece in ring_gather("z", quarter).items():
        place = attn_start((at["z"] + distance) % 4)
        attn = lax.dynamic_update_slice(attn, piece[None], (at["c"], 0, place))
        attn = lax.dynamic_update_slice(attn, shifted(piece, c=1)[None], (1 - at["c"], 0, place))
    own = two_level(up, down)
    mlp = jnp.zeros((2, width, up.shape[1]), BF16)
    for distance, piece in ring_gather("x", own).items():
        place = (at["x"] + distance) % 4 * (4 * rows)
        mlp = lax.dynamic_update_slice(mlp, piece[None], (at["c"], place, 0))
        mlp = lax.dynamic_update_slice(mlp, shifted(piece, c=1)[None], (1 - at["c"], place, 0))
    return attn, mlp


def contract_rows(a, b):
    return lax.dot_general(a, b, (((0,), (0,)), ((), ())), preferred_element_type=F32)


def contract_cols(a, b):
    return lax.dot_general(a, b, (((1,), (1,)), ((), ())), preferred_element_type=F32)


def block_diagonal(a, b):
    zero = jnp.zeros_like(a)
    return jnp.concatenate(
        [jnp.concatenate([a, zero], 1), jnp.concatenate([zero, b], 1)], 0
    )


def finish(at, piece, start_of, width):
    whole = jnp.zeros((piece.shape[0], width), BF16)
    for distance, block in ring_gather("z", piece).items():
        whole = lax.dynamic_update_slice(whole, block, (0, start_of((at["z"] + distance) % 4)))
    rows = piece.shape[0] // 2
    mine = rows_of(whole, at["c"] * rows, rows)
    got = shifted(rows_of(whole, (1 - at["c"]) * rows, rows), c=1)
    c0 = at["c"] == 0
    return jnp.where(c0, mine, got), jnp.where(c0, got, mine)


def reduce_layer(at, operands):
    a, dq, dk, dv, o, dz, m, du, dy, g, vec = operands
    c0 = at["c"] == 0
    width = a.shape[1]
    pick = lambda p, q: jnp.where(c0, p, q)
    vec_cols = jnp.pad(vec.T, ((0, 0), (width, 2 * PADDED - width - vec.shape[0])))
    dz = jnp.pad(dz, ((0, 0), (0, PADDED - width)))
    give = contract_rows(
        jnp.concatenate([a, pick(o, a)], 0), block_diagonal(pick(dv, dq), pick(dz, dk))
    ) + pick(0.0, 1.0) * vec_cols
    got = shifted(give.astype(BF16), c=1)
    keep = contract_rows(
        jnp.concatenate([a, pick(a, o)], 0), block_diagonal(pick(dq, dv), pick(dk, dz))
    ) + pick(1.0, 0.0) * vec_cols
    attn = (keep + got.astype(F32)).astype(BF16)
    give = contract_rows(pick(dy, m), pick(g, du)).astype(BF16)
    got = shifted(give, c=1)
    mlp = (contract_rows(pick(m, dy), pick(du, g)) + got.astype(F32)).astype(BF16)

    rows = width // 4
    attn = ring_sum("z", at["z"], lambda i: columns(attn, attn_start(i)))
    mlp = ring_sum("x", at["x"], lambda i: rows_of(mlp, i * rows, rows))
    attn = ring_sum("x", at["x"], lambda i: rows_of(attn, i * rows, rows))
    mlp = ring_sum("z", at["z"], lambda i: columns(mlp, mlp_start(i)))
    half = rows // 2
    mine = rows_of(attn, at["y"] * half, half).astype(F32)
    got = shifted(rows_of(attn, (1 - at["y"]) * half, half), y=1, t=1).astype(F32)
    attn = (mine + got).astype(BF16)
    attn = (attn.astype(F32) + shifted(attn, t=1).astype(F32)).astype(BF16)
    mine = rows_of(mlp, at["y"] * half, half).astype(F32)
    got = shifted(rows_of(mlp, (1 - at["y"]) * half, half), y=1).astype(F32)
    mlp = (mine + got).astype(BF16)
    qk, vo = finish(at, attn, attn_start, 2 * PADDED)
    up, down = finish(at, mlp, mlp_start, du.shape[1])
    in_back = jnp.concatenate(
        [qk[:, :width], qk[:, PADDED : PADDED + width], vo[:, :width]], 1
    ).astype(F32)
    out_back = vo[:, PADDED : PADDED + width].astype(F32)
    vec_back = qk[:, width : width + 12].T.astype(F32)
    return in_back, out_back, up.astype(F32), down.astype(F32), vec_back


def group_place():
    return lax.axis_index("ctx") * 2 + lax.axis_index("tensor")


def member(index):
    return (lax.axis_index("dp"), index // 2, lax.rem(index, 2))


def meet(me):
    barrier = pltpu.get_barrier_semaphore()
    for k in range(1, GROUP):
        pl.semaphore_signal(
            barrier, inc=1, device_id=member(lax.rem(me + k, GROUP)), device_id_type=MESH
        )
    pl.semaphore_wait(barrier, GROUP - 1)


def to_heads(me, sources, landed, local_sem, send_sem, recv_sem):
    copies = []
    for k in range(1, GROUP):
        peer = lax.rem(me + k, GROUP)
        rows = pl.ds(pl.multiple_of(peer // 4 * 64, 64), 64)
        lanes = pl.ds(pl.multiple_of(lax.rem(peer, 4) * STRIDE, 128), WINDOW)
        for n, (src, dst) in enumerate(zip(sources, landed)):
            copy = pltpu.make_async_remote_copy(
                src_ref=src.at[rows, lanes],
                dst_ref=dst.at[pl.ds(pl.multiple_of(me * 64, 64), 64)],
                send_sem=send_sem.at[n, k],
                recv_sem=recv_sem.at[n, k],
                device_id=member(peer),
                device_id_type=MESH,
            )
            copy.start()
            copies.append(copy)
    rows = pl.ds(pl.multiple_of(me // 4 * 64, 64), 64)
    lanes = pl.ds(pl.multiple_of(lax.rem(me, 4) * STRIDE, 128), WINDOW)
    for n, (src, dst) in enumerate(zip(sources, landed)):
        copy = pltpu.make_async_copy(
            src.at[rows, lanes], dst.at[pl.ds(pl.multiple_of(me * 64, 64), 64)], local_sem.at[n]
        )
        copy.start()
        copies.append(copy)
    return copies


def to_rows(me, sources, landed, local_sem, send_sem, recv_sem):
    copies = []
    for k in range(1, GROUP):
        peer = lax.rem(me + k, GROUP)
        for n, (src, dst) in enumerate(zip(sources, landed)):
            copy = pltpu.make_async_remote_copy(
                src_ref=src.at[pl.ds(pl.multiple_of(peer * 64, 64), 64)],
                dst_ref=dst.at[me],
                send_sem=send_sem.at[n, k],
                recv_sem=recv_sem.at[n, k],
                device_id=member(peer),
                device_id_type=MESH,
            )
            copy.start()
            copies.append(copy)
    for n, (src, dst) in enumerate(zip(sources, landed)):
        copy = pltpu.make_async_copy(
            src.at[pl.ds(pl.multiple_of(me * 64, 64), 64)], dst.at[me], local_sem.at[n]
        )
        copy.start()
        copies.append(copy)
    return copies


def side_by_side(landed, out):
    for micro in range(2):
        rows = slice(micro * 64, micro * 64 + 64)
        for group in range(4):
            width = WINDOW if group == 3 else STRIDE
            out[rows, group * STRIDE : group * STRIDE + width] = landed[micro * 4 + group, :, :width]


def matmul(a, b, dims):
    return lax.dot_general(a, b, ((dims[:1], dims[1:]), ((), ())), preferred_element_type=F32)


def attend_kernel(
    q, k, v, bias, out, q_all, k_all, v_all, o_all, log_total,
    o_low, o_landed, local_sem, send_sem, recv_sem,
):
    me = group_place()
    meet(me)
    copies = to_heads(
        me, (q, k, v), (q_all, k_all, v_all), local_sem, send_sem, recv_sem
    )
    o_low[...] = jnp.zeros_like(o_low)
    o_all[...] = jnp.zeros_like(o_all)
    log_total[...] = jnp.zeros_like(log_total)
    for copy in copies:
        copy.wait()
    for head in range(SLOTS):
        lanes = slice(head * HEAD, head * HEAD + HEAD)
        keys, values = k_all[:, lanes], v_all[:, lanes]
        for start in range(0, 512, CHUNK):
            rows, reach = slice(start, start + CHUNK), start + CHUNK
            queries = q_all[rows, lanes] * 0.125
            scores = matmul(queries, keys[:reach], (1, 1)) + bias[rows, :reach]
            top = jnp.max(scores, 1, keepdims=True)
            weights = jnp.exp(scores - top)
            total = jnp.sum(weights, 1, keepdims=True)
            result = matmul(weights.astype(BF16), values[:reach], (1, 0)) / total
            o_all[rows, lanes] = result
            o_low[rows, lanes] = result.astype(BF16)
            log_total[rows, head : head + 1] = top + jnp.log(total)
    copies = to_rows(
        me, (o_low,), (o_landed,), local_sem.at[3:4], send_sem.at[3:4], recv_sem.at[3:4]
    )
    for copy in copies:
        copy.wait()
    side_by_side(o_landed, out)


def attend(q, k, v, bias, collective):
    shape = jax.ShapeDtypeStruct
    vmem = pl.BlockSpec(memory_space=pltpu.VMEM)
    return pl.pallas_call(
        attend_kernel,
        out_shape=(
            shape((128, PADDED), BF16),
            shape((512, WINDOW), BF16),
            shape((512, WINDOW), BF16),
            shape((512, WINDOW), BF16),
            shape((512, WINDOW), F32),
            shape((512, 128), F32),
        ),
        in_specs=[vmem] * 4,
        out_specs=[vmem] * 6,
        scratch_shapes=[
            pltpu.VMEM((512, WINDOW), BF16),
            pltpu.VMEM((GROUP, 64, WINDOW), BF16),
            pltpu.SemaphoreType.DMA((4,)),
            pltpu.SemaphoreType.DMA((4, GROUP)),
            pltpu.SemaphoreType.DMA((4, GROUP)),
        ],
        compiler_params=pltpu.CompilerParams(
            collective_id=collective, has_side_effects=True, vmem_limit_bytes=32 * 2**20
        ),
    )(q, k, v, bias)


def attend_back_kernel(
    do, q_all, k_all, v_all, o_all, log_total, bias, dq, dk, dv,
    do_all, dq_low, dk_low, dv_low, dq_landed, dk_landed, dv_landed, dk_sum, dv_sum,
    local_sem, send_sem, recv_sem,
):
    me = group_place()
    meet(me)
    copies = to_heads(
        me, (do,), (do_all,), local_sem.at[3:4], send_sem.at[3:4], recv_sem.at[3:4]
    )
    dq_low[...] = jnp.zeros_like(dq_low)
    dk_low[...] = jnp.zeros_like(dk_low)
    dv_low[...] = jnp.zeros_like(dv_low)
    for copy in copies:
        copy.wait()
    for head in range(SLOTS):
        lanes = slice(head * HEAD, head * HEAD + HEAD)
        keys, values = k_all[:, lanes], v_all[:, lanes]
        dk_sum[...] = jnp.zeros_like(dk_sum)
        dv_sum[...] = jnp.zeros_like(dv_sum)
        for start in range(0, 512, CHUNK):
            rows, reach = slice(start, start + CHUNK), start + CHUNK
            queries = q_all[rows, lanes] * 0.125
            grads = do_all[rows, lanes]
            scores = matmul(queries, keys[:reach], (1, 1)) + bias[rows, :reach]
            probs = jnp.exp(scores - log_total[rows, head : head + 1])
            probs_back = matmul(grads, values[:reach], (1, 1))
            delta = jnp.sum(grads.astype(F32) * o_all[rows, lanes], 1, keepdims=True)
            scores_back = (probs * (probs_back - delta)).astype(BF16)
            dq_low[rows, lanes] = (matmul(scores_back, keys[:reach], (1, 0)) * 0.125).astype(BF16)
            dk_sum[:reach] += matmul(scores_back, queries, (0, 0))
            dv_sum[:reach] += matmul(probs.astype(BF16), grads, (0, 0))
        dk_low[:, lanes] = dk_sum[...].astype(BF16)
        dv_low[:, lanes] = dv_sum[...].astype(BF16)
    copies = to_rows(
        me,
        (dq_low, dk_low, dv_low),
        (dq_landed, dk_landed, dv_landed),
        local_sem,
        send_sem,
        recv_sem,
    )
    for copy in copies:
        copy.wait()
    side_by_side(dq_landed, dq)
    side_by_side(dk_landed, dk)
    side_by_side(dv_landed, dv)


def attend_back(do, saved, bias, collective):
    shape = jax.ShapeDtypeStruct
    vmem = pl.BlockSpec(memory_space=pltpu.VMEM)
    return pl.pallas_call(
        attend_back_kernel,
        out_shape=(shape((128, PADDED), BF16),) * 3,
        in_specs=[vmem] * 7,
        out_specs=[vmem] * 3,
        scratch_shapes=[pltpu.VMEM((512, WINDOW), BF16)] * 4
        + [pltpu.VMEM((GROUP, 64, WINDOW), BF16)] * 3
        + [pltpu.VMEM((512, HEAD), F32)] * 2
        + [
            pltpu.SemaphoreType.DMA((4,)),
            pltpu.SemaphoreType.DMA((4, GROUP)),
            pltpu.SemaphoreType.DMA((4, GROUP)),
        ],
        compiler_params=pltpu.CompilerParams(
            collective_id=collective, has_side_effects=True, vmem_limit_bytes=32 * 2**20
        ),
    )(do, *saved, bias)


def score_bias(segments):
    docs = lax.all_gather(segments.astype(BF16), ("ctx", "tensor"), axis=1, tiled=True)
    docs = lax.dynamic_index_in_dim(docs, lax.axis_index("ctx") // 2, 0, keepdims=False)
    place = jnp.arange(docs.shape[0], dtype=jnp.int32)
    allowed = (docs[:, None] == docs[None, :]) & (place[None, :] <= place[:, None])
    return jnp.where(allowed, 0.0, MASKED).astype(F32)


def layer_norm(inputs, gain_row, shift_row):
    row_mean = jnp.mean(inputs, -1, keepdims=True)
    centred = inputs - row_mean
    spread = jnp.mean(centred * centred, -1, keepdims=True)
    return centred * lax.rsqrt(spread + EPSILON) * gain_row + shift_row


def gelu_exact(inputs):
    return jax.nn.gelu(inputs, approximate=False)


def dot(a, b):
    return jnp.dot(a, b, preferred_element_type=F32)


def body(tokens, qkv_weight, out_weight, up_weight, down_weight, vectors, segments, cotangent):
    micro_count, row_count, width = tokens.shape
    layers = qkv_weight.shape[0]
    hidden_half = up_weight.shape[2]
    total_rows = micro_count * row_count
    at = places()
    bias = score_bias(segments)
    weights = [
        gather_layer(at, qkv_weight[l], out_weight[l], up_weight[l], down_weight[l], vectors[l])
        for l in range(layers)
    ]
    wide = lambda row: jnp.pad(row, (0, PADDED - width))
    residual = tokens.reshape(total_rows, width).astype(F32)
    memory = []
    for l in range(layers):
        attn_w, mlp_w = weights[l]
        vec = attn_w[0, :, width : width + 12].T.astype(F32)
        bias_up = lax.dynamic_slice_in_dim(vec[8:].reshape(-1), at["t"] * hidden_half, hidden_half)
        normed = layer_norm(residual, vec[0], vec[1]).astype(BF16)
        both = dot(normed, attn_w[0])
        q = (both[:, :PADDED] + wide(vec[2])).astype(BF16)
        k = both[:, PADDED:].astype(BF16)
        v = (dot(normed, attn_w[1, :, :PADDED]) + wide(vec[3])).astype(BF16)
        o, *saved = attend(q, k, v, bias, 1)
        o = o[:, :width]
        midway = residual + dot(o, attn_w[1, :, PADDED : PADDED + width]) + vec[4]
        m_own = layer_norm(midway, vec[5], vec[6]).astype(BF16)
        m_peer = shifted(m_own, t=1)
        u_own = dot(m_own, mlp_w[0]) + bias_up
        u_peer = dot(m_peer, mlp_w[0]) + bias_up
        g_peer = gelu_exact(u_peer).astype(BF16)
        got = shifted(contract_cols(g_peer, mlp_w[1]).astype(BF16), t=1)
        g_own = gelu_exact(u_own).astype(BF16)
        branch = contract_cols(g_own, mlp_w[1]) + got.astype(F32)
        memory.append(
            (vec, bias_up, normed, saved, o, residual, midway, m_own, m_peer, u_own, u_peer, g_own, g_peer)
        )
        residual = midway + branch + vec[7]
    result = residual
    gradient = cotangent.reshape(total_rows, width)
    totals = [None] * layers
    for l in reversed(range(layers)):
        attn_w, mlp_w = weights[l]
        vec, bias_up, normed, saved, o, layer_in, midway, m_own, m_peer, u_own, u_peer, g_own, g_peer = memory[l]
        dy_own = gradient.astype(BF16)
        dy_peer = shifted(dy_own, t=1)
        back = lambda u, dy: jax.vjp(gelu_exact, u)[1](dot(dy, mlp_w[1]))[0].astype(BF16)
        du_own = back(u_own, dy_own)
        du_peer = back(u_peer, dy_peer)
        got = shifted(contract_cols(du_peer, mlp_w[0]).astype(BF16), t=1)
        dm = contract_cols(du_own, mlp_w[0]) + got.astype(F32)
        midway_back, gain_two, shift_two = jax.vjp(layer_norm, midway, vec[5], vec[6])[1](dm)
        midway_back = midway_back + gradient
        dz = midway_back.astype(BF16)
        do = contract_cols(dz, attn_w[1, :, PADDED : PADDED + width]).astype(BF16)
        do = jnp.pad(do, ((0, 0), (0, PADDED - width)))
        dq, dk, dv = attend_back(do, saved, bias, 2)
        da = contract_cols(jnp.concatenate([dq, dk], 1), attn_w[0]) + contract_cols(
            dv, attn_w[1, :, :PADDED]
        )
        input_back, gain_one, shift_one = jax.vjp(layer_norm, layer_in, vec[0], vec[1])[1](da)
        gradient = midway_back + input_back
        m = jnp.concatenate([m_own, m_peer], 0)
        du = jnp.concatenate([du_own, du_peer], 0)
        dy = jnp.concatenate([dy_own, dy_peer], 0)
        g = jnp.concatenate([g_own, g_peer], 0)
        bias_back = lax.dynamic_update_slice_in_dim(
            jnp.zeros((2 * hidden_half,), F32), jnp.sum(du.astype(F32), 0), at["t"] * hidden_half, 0
        )
        down_rows = lambda v: jnp.sum(v.astype(F32), 0)[:width]
        small = jnp.stack(
            [gain_one, shift_one, down_rows(dq), down_rows(dv), down_rows(dz), gain_two, shift_two, down_rows(dy_own)]
        )
        vec_back = jnp.concatenate([small, bias_back.reshape(-1, width)], 0)
        totals[l] = reduce_layer(
            at, (normed, dq, dk, dv, o, dz, m, du, dy, g, vec_back)
        )
    stacked = [jnp.stack([totals[l][n] for l in range(layers)]) for n in range(5)]
    shape = (micro_count, row_count, width)
    return (result.reshape(shape), gradient.reshape(shape), *stacked)


def solution(mesh):
    return jax.shard_map(
        body,
        mesh=mesh,
        in_specs=(
            P(None, ("dp", "ctx", "tensor"), None),
            P(None, "dp", None),
            P(None, "dp", None),
            P(None, "dp", "tensor"),
            P(None, "dp", "tensor"),
            P(None, None, "dp"),
            P(None, ("dp", "ctx", "tensor")),
            P(None, ("dp", "ctx", "tensor"), None),
        ),
        out_specs=(
            P(None, ("dp", "ctx", "tensor"), None),
            P(None, ("dp", "ctx", "tensor"), None),
            P(None, "dp", None),
            P(None, "dp", None),
            P(None, "dp", "tensor"),
            P(None, "dp", "tensor"),
            P(None, None, "dp"),
        ),
        check_vma=False,
    )
```

time: 2270 us -> 918 us (0.40)
  waiting for transfers between devices: 975 us -> 210 us
  blocking collectives: 636 us -> 20.1 us
  Pallas kernels: 0 us -> 116 us
  local copies, waits for them, and re-layouts: 293 us -> 214 us
  starting transfers between devices: 99.5 us -> 126 us
  matrix products: 186 us -> 163 us
    all_gather x16 -> x0, waiting for transfers between devices: 674 us -> none  [the longest x2 153 us: fetch_layer(): lax.all_gather(up_weight[layer_id], 'dp', axis=0, tiled=True)]
    unnamed x3 -> x0, blocking collectives: 512 us -> none
    ppermute x0 -> x118, waiting for transfers between devices: none -> 210 us  [shifted(): return lax.ppermute(value, ('dp', 'ctx', 'tensor'), pairs)]
    unnamed x54 -> x0, waiting for transfers between devices: 127 us -> none
    ppermute x0 -> x118, starting transfers between devices: none -> 126 us  [shifted(): return lax.ppermute(value, ('dp', 'ctx', 'tensor'), pairs)]
    unnamed x585 -> x268, local copies, waits for them, and re-layouts: 152 us -> 34.6 us
    pallas_call x0 -> x4, Pallas kernels: none -> 116 us  [the longest x2 59.5 us: attend_back(): pl.pallas_call(attend_back_kernel, out_shape=(shape((128, PADDED), BF16),...]
    unnamed x24 -> x0, starting transfers between devices: 97.4 us -> none
  transfers between devices with their start and end apart: 50 -> 118, of which waited for: 28 -> 41; matrix products, arithmetic and copies ran while one was open for 18% -> 44% of each run, Pallas kernels for 0% -> 13%
where the time goes in v1:
time: 918 us; the launch traced here: 904 us
  local copies, waits for them, and re-layouts  214 us (23%)
  waiting for transfers between devices  210 us (23%)
  matrix products  163 us (18%)
  starting transfers between devices  126 us (14%)
  Pallas kernels  116 us (13%)
  other arithmetic  51.9 us (6%)
  blocking collectives  20.1 us (2%)
    ppermute x118, waiting for transfers between devices, shifted(): return lax.ppermute(value, ('dp', 'ctx', 'tensor'), pairs)  210 us
    ppermute x118, starting transfers between devices, shifted(): return lax.ppermute(value, ('dp', 'ctx', 'tensor'), pairs)  126 us
    dot_general x14, matrix products, dot(): return jnp.dot(a, b, preferred_element_type=F32)  68.7 us
    pallas_call x2, Pallas kernels, attend_back(): pl.pallas_call(attend_back_kernel, out_shape=(shape((128, PADDED), BF16),...  59.5 us
    pallas_call x2, Pallas kernels, attend(): pl.pallas_call(attend_kernel, out_shape=(shape((128, PADDED), BF16), shap...  56.3 us
    dot_general x14, matrix products, contract_cols(): lax.dot_general(a, b, (((1,), (1,)), ((), ())), preferred_element_type=F32)  54.2 us
    dot_general x8, matrix products, contract_rows(): lax.dot_general(a, b, (((0,), (0,)), ((), ())), preferred_element_type=F32)  39.8 us
    unnamed x268, local copies, waits for them, and re-layouts  34.6 us
  transfers between devices with their start and end apart: 118, of which 41 were waited for; matrix products, arithmetic and copies ran while one was open for 44% of the time, Pallas kernels for 13%

profile of v1, /device:TPU:0, one launch (start us, length us, event | category | flops | bytes accessed | tf_op | source)
XLA Modules:
  0.0 904.4 jit_solution(3499935162095400404)
XLA Ops:
  11.1 20.1 %all-gather = bf16[8,64,2]{1,2,0:T(2,128)(2,1)S(1)} all-gather(bf16[1,64,2]{1,2,0:T(2,128)(2,1)S(1)} %convert_bitcast_fusion.2), channel_id=1, replica_groups=mesh['dp'=16,'ctx'=4,'tensor'=2] {'ctx','tensor'}, dimensions={0}, use_global_device_ids=true | all-gather | bytes 2304 | tf_op jit(solution)/shard_map/all_gather | solution.py:420
  60.1 3.8 collective-permute-start.5
  77.8 4.7 broadcast.389.clone
  86.5 4.7 broadcast.389.clone.1
  97.7 4.2 broadcast.395.clone
  105.0 4.2 broadcast.395.clone.1
  112.2 4.0 collective-permute-done.17
  125.4 16.4 %collective-permute-done.43 = bf16[272,2176]{1,0:T(8,128)(2,1)S(1)} collective-permute-done((bf16[272,2176]{1,0:T(8,128)(2,1)S(1)}, bf16[272,2176]{1,0:T(8,128)(2,1)S(1)}, u32[]{:S(2)}, u32[]{:S(2)}) %collective-permute-start.43) | collective-permute-done | bytes 1183776 | tf_op jit(solution)/shard_map/ppermute | solution.py:41
  141.8 4.8 collective-permute-done.45
  179.5 4.7 collective-permute-done.7
  184.2 3.8 collective-permute-start.48
  216.5 7.0 collective-permute-done.37
  229.4 8.6 collective-permute-done.11
  269.1 3.6 copy.216
  308.5 4.1 fusion.5
  315.4 29.8 %shard_map.135 = (bf16[128,1152]{1,0:T(8,128)(2,1)S(1)}, bf16[512,384]{1,0:T(8,128)(2,1)S(1)}, bf16[512,384]{1,0:T(8,128)(2,1)S(1)}, bf16[512,384]{1,0:T(8,128)(...) custom-call(bf16[128,1152]{1,0:T(8,128)(2,1)S(1)} %fusion.111.q, bf16[128,1152]{1,0:T(8,128)(2,1)S(1)} %slice.853.k, ...), custom_call_target="tpu_custom_call" | custom-call | tf_op jit(solution)/shard_map/pallas_call | solution.py:323
  350.9 6.4 multiply_convert_fusion.3
  358.6 6.2 multiply_convert_fusion.2
  365.7 3.7 fusion.32
  372.0 5.4 collective-permute-done.25
  377.4 4.3 fusion.170
  382.2 4.2 fusion.7
  389.1 26.5 %shard_map.136 = (bf16[128,1152]{1,0:T(8,128)(2,1)S(1)}, bf16[512,384]{1,0:T(8,128)(2,1)S(1)}, bf16[512,384]{1,0:T(8,128)(2,1)S(1)}, bf16[512,384]{1,0:T(8,128)(...) custom-call(bf16[128,1152]{1,0:T(8,128)(2,1)S(1)} %fusion.110.q, bf16[128,1152]{1,0:T(8,128)(2,1)S(1)} %slice.852.k, ...), custom_call_target="tpu_custom_call" | custom-call | tf_op jit(solution)/shard_map/pallas_call | solution.py:323
  422.4 6.0 multiply_convert_fusion.1
  428.4 6.2 add_convert_fusion.17
  435.7 6.3 multiply_convert_fusion
  442.8 4.5 fusion.30
  449.4 5.8 add_convert_fusion.16
  456.0 4.5 fusion.31
  467.8 5.6 convolution_convert_fusion
  473.7 4.8 multiply_reduce_fusion
  480.5 3.6 convolution_convert_fusion.3
  489.3 30.5 %shard_map.137 = (bf16[128,1152]{1,0:T(8,128)(2,1)S(1)}, bf16[128,1152]{1,0:T(8,128)(2,1)S(1)}, bf16[128,1152]{1,0:T(8,128)(2,1)S(1)}) custom-call(bf16[128,1152]{1,0:T(8,128)(2,1)S(1)} %pad.45.do, bf16[512,384]{1,0:T(8,128)(2,1)S(1)} %copy-done.7, bf16[512,384]{1,0:T(8,128)(2,1)S(1)} %copy-done.9, bf16[512,384]{1,0:T(8,128)(2,1)S(1)} %copy-done.11, ...), custom_call_target="tpu_custom_call" | custom-call | tf_op jit(solution)/shard_map/pallas_call | solution.py:400
  524.0 3.6 multiply_reduce_fusion.1
  531.4 6.3 add_convert_fusion.15
  538.9 5.2 fusion.1
  544.8 4.9 fusion.29
  549.7 5.5 add_convert_fusion.14
  556.0 4.5 fusion.33
  565.1 5.7 convolution_convert_fusion.1
  572.2 4.8 multiply_reduce_fusion.2
  584.9 29.1 %shard_map.138 = (bf16[128,1152]{1,0:T(8,128)(2,1)S(1)}, bf16[128,1152]{1,0:T(8,128)(2,1)S(1)}, bf16[128,1152]{1,0:T(8,128)(2,1)S(1)}) custom-call(bf16[128,1152]{1,0:T(8,128)(2,1)S(1)} %pad.46.do, bf16[512,384]{1,0:T(8,128)(2,1)S(1)} %copy-done.1, bf16[512,384]{1,0:T(8,128)(2,1)S(1)} %copy-done.3, bf16[512,384]{1,0:T(8,128)(2,1)S(1)} %copy-done.5, ...), custom_call_target="tpu_custom_call" | custom-call | tf_op jit(solution)/shard_map/pallas_call | solution.py:400
  623.5 5.2 fusion
  630.4 4.1 fusion.3
  638.2 4.1 fusion.2
  645.9 5.4 add_convert_fusion
  657.7 4.4 add_convert_fusion.1
  665.2 6.8 collective-permute-done.73
  673.0 16.9 %collective-permute-done.107 = bf16[272,2176]{1,0:T(8,128)(2,1)S(1)} collective-permute-done((bf16[272,2176]{1,0:T(8,128)(2,1)S(1)}, bf16[272,2176]{1,0:T(8,128)(2,1)S(1)}, u32[]{:S(2)}, u32[]{:S(2)}) %collective-permute-start.107) | collective-permute-done | bytes 1183776 | tf_op jit(solution)/shard_map/ppermute | solution.py:41
  689.9 3.7 collective-permute-done.105
  702.5 25.9 %collective-permute-done.110 = bf16[136,640]{1,0:T(8,128)(2,1)S(1)} collective-permute-done((bf16[136,640]{1,0:T(8,128)(2,1)S(1)}, bf16[136,640]{1,0:T(8,128)(2,1)S(1)}, u32[]{:S(2)}, u32[]{:S(2)}) %collective-permute-start.110) | collective-permute-done | bytes 174112 | tf_op jit(solution)/shard_map/ppermute | solution.py:41
  731.7 4.8 collective-permute-done.111
  736.6 5.7 collective-permute-done.109
  749.6 24.1 %collective-permute-done.93 = bf16[136,640]{1,0:T(8,128)(2,1)S(1)} collective-permute-done((bf16[136,640]{1,0:T(8,128)(2,1)S(1)}, bf16[136,640]{1,0:T(8,128)(2,1)S(1)}, u32[]{:S(2)}, u32[]{:S(2)}) %collective-permute-start.93) | collective-permute-done | bytes 174112 | tf_op jit(solution)/shard_map/ppermute | solution.py:41
  779.8 3.7 collective-permute-start.96
  789.6 3.8 collective-permute-done.115
  801.7 6.1 collective-permute-done.97
  812.4 6.4 collective-permute-done.78
  820.2 6.7 collective-permute-done.58
  835.7 3.7 collective-permute-done.100
  866.7 4.3 collective-permute-done.65
  872.8 3.7 collective-permute-done.66
  883.6 3.6 collective-permute-start.70
  889.4 3.7 collective-permute-done.69
  (795 shorter events, 411.5 us)
Async XLA Ops:
  5.8 26.9 %collective-permute-start.26 = (bf16[68,640]{1,0:T(8,128)(2,1)S(1)}, bf16[68,640]{1,0:T(8,128)(2,1)S(1)}, u32[]{:S(2)}, u32[]{:S(2)}) collective-permute-start(bf16[68,640]{1,0:T(8,128)(2,1)S(1)} %get-tuple-element.189), channel_id=1, source_target_pairs={{0,8},{1,9},{2,10},{3,11},{4,12},{5,13},{6,14},{7,15},{8,0},{9,1},... | collective-permute-start | bytes 261128 | tf_op jit(solution)/shard_map/ppermute | solution.py:41
  6.5 29.2 %collective-permute-start = (bf16[68,640]{1,0:T(8,128)(2,1)S(1)}, bf16[68,640]{1,0:T(8,128)(2,1)S(1)}, u32[]{:S(2)}, u32[]{:S(2)}) collective-permute-start(bf16[68,640]{1,0:T(8,128)(2,1)S(1)} %get-tuple-element.191), channel_id=1, source_target_pairs={{0,8},{1,9},{2,10},{3,11},{4,12},{5,13},{6,14},{7,15},{8,0},{9,1},... | collective-permute-start | bytes 261128 | tf_op jit(solution)/shard_map/ppermute | solution.py:41
  9.6 38.1 %collective-permute-start.14 = (bf16[68,2176]{1,0:T(8,128)(2,1)}, bf16[68,2176]{1,0:T(8,128)(2,1)}, u32[]{:S(2)}, u32[]{:S(2)}) collective-permute-start(bf16[68,2176]{1,0:T(8,128)(2,1)} %get-tuple-element.181), channel_id=1, source_target_pairs={{0,8},{1,9},{2,10},{3,11},{4,12},{5,13},{6,14},{7,15},{8,0},{9,1},... | collective-permute-start | bytes 887816 | tf_op jit(solution)/shard_map/ppermute | solution.py:41
  11.0 41.9 %collective-permute-start.40 = (bf16[68,2176]{1,0:T(8,128)(2,1)}, bf16[68,2176]{1,0:T(8,128)(2,1)}, u32[]{:S(2)}, u32[]{:S(2)}) collective-permute-start(bf16[68,2176]{1,0:T(8,128)(2,1)} %get-tuple-element.179), channel_id=1, source_target_pairs={{0,8},{1,9},{2,10},{3,11},{4,12},{5,13},{6,14},{7,15},{8,0},{9,1},... | collective-permute-start | bytes 887816 | tf_op jit(solution)/shard_map/ppermute | solution.py:41
  52.8 31.0 %collective-permute-start.15 = (bf16[136,2176]{1,0:T(8,128)(2,1)}, bf16[136,2176]{1,0:T(8,128)(2,1)}, u32[]{:S(2)}, u32[]{:S(2)}) collective-permute-start(bf16[136,2176]{1,0:T(8,128)(2,1)} %maximum_select_fusion.4), channel_id=1, source_target_pairs={{0,16},{1,17},{2,18},{3,19},{4,20},{5,21},{6,22},{7,23},{8,24},{9,... | collective-permute-start | bytes 1775624 | tf_op jit(solution)/shard_map/ppermute | solution.py:41
  67.3 28.5 %collective-permute-start.41 = (bf16[136,2176]{1,0:T(8,128)(2,1)}, bf16[136,2176]{1,0:T(8,128)(2,1)}, u32[]{:S(2)}, u32[]{:S(2)}) collective-permute-start(bf16[136,2176]{1,0:T(8,128)(2,1)} %maximum_select_fusion.5), channel_id=1, source_target_pairs={{0,16},{1,17},{2,18},{3,19},{4,20},{5,21},{6,22},{7,23},{8,24},{9,... | collective-permute-start | bytes 1775624 | tf_op jit(solution)/shard_map/ppermute | solution.py:41
  71.0 75.7 %collective-permute-start.32 = (bf16[1088,640]{1,0:T(8,128)(2,1)}, bf16[1088,640]{1,0:T(8,128)(2,1)}, u32[]{:S(2)}, u32[]{:S(2)}) collective-permute-start(bf16[1088,640]{1,0:T(8,128)(2,1)} %maximum_dynamic-update-slice_fusion.1), channel_id=1, source_target_pairs={{0,8},{1,9},{2,10},{3,11},{4,12},{5,13},{6,14},{7,15},{8,0},{9,1},... | collective-permute-start | bytes 4177928 | tf_op jit(solution)/shard_map/ppermute | solution.py:41
  85.9 26.3 %collective-permute-start.16 = (bf16[272,2176]{1,0:T(8,128)(2,1)S(1)}, bf16[272,2176]{1,0:T(8,128)(2,1)S(1)}, u32[]{:S(2)}, u32[]{:S(2)}) collective-permute-start(bf16[272,2176]{1,0:T(8,128)(2,1)S(1)} %maximum_select_fusion.1), channel_id=1, source_target_pairs={{0,8},{1,9},{2,10},{3,11},{4,12},{5,13},{6,14},{7,15},{8,0},{9,1},... | collective-permute-start | bytes 3551240 | tf_op jit(solution)/shard_map/ppermute | solution.py:41
  86.5 29.6 %collective-permute-start.17 = (bf16[272,2176]{1,0:T(8,128)(2,1)S(1)}, bf16[272,2176]{1,0:T(8,128)(2,1)}, u32[]{:S(2)}, u32[]{:S(2)}) collective-permute-start(bf16[272,2176]{1,0:T(8,128)(2,1)S(1)} %maximum_select_fusion.1), channel_id=1, source_target_pairs={{0,32},{1,33},{2,34},{3,35},{4,36},{5,37},{6,38},{7,39},{8,40},{9,... | collective-permute-start | bytes 3551240 | tf_op jit(solution)/shard_map/ppermute | solution.py:41
  92.5 29.7 %collective-permute-start.19 = (bf16[272,2176]{1,0:T(8,128)(2,1)S(1)}, bf16[272,2176]{1,0:T(8,128)(2,1)}, u32[]{:S(2)}, u32[]{:S(2)}) collective-permute-start(bf16[272,2176]{1,0:T(8,128)(2,1)S(1)} %maximum_select_fusion.1), channel_id=1, source_target_pairs={{0,96},{1,97},{2,98},{3,99},{4,100},{5,101},{6,102},{7,103},{8,104... | collective-permute-start | bytes 3551240 | tf_op jit(solution)/shard_map/ppermute | solution.py:41
  97.7 24.5 %collective-permute-start.42 = (bf16[272,2176]{1,0:T(8,128)(2,1)S(1)}, bf16[272,2176]{1,0:T(8,128)(2,1)S(1)}, u32[]{:S(2)}, u32[]{:S(2)}) collective-permute-start(bf16[272,2176]{1,0:T(8,128)(2,1)S(1)} %maximum_select_fusion.3), channel_id=1, source_target_pairs={{0,8},{1,9},{2,10},{3,11},{4,12},{5,13},{6,14},{7,15},{8,0},{9,1},... | collective-permute-start | bytes 3551240 | tf_op jit(solution)/shard_map/ppermute | solution.py:41
  112.1 29.7 %collective-permute-start.43 = (bf16[272,2176]{1,0:T(8,128)(2,1)S(1)}, bf16[272,2176]{1,0:T(8,128)(2,1)S(1)}, u32[]{:S(2)}, u32[]{:S(2)}) collective-permute-start(bf16[272,2176]{1,0:T(8,128)(2,1)S(1)} %maximum_select_fusion.3), channel_id=1, source_target_pairs={{0,32},{1,33},{2,34},{3,35},{4,36},{5,37},{6,38},{7,39},{8,40},{9,... | collective-permute-start | bytes 3551240 | tf_op jit(solution)/shard_map/ppermute | solution.py:41
  116.1 30.5 %collective-permute-start.45 = (bf16[272,2176]{1,0:T(8,128)(2,1)S(1)}, bf16[272,2176]{1,0:T(8,128)(2,1)}, u32[]{:S(2)}, u32[]{:S(2)}) collective-permute-start(bf16[272,2176]{1,0:T(8,128)(2,1)S(1)} %maximum_select_fusion.3), channel_id=1, source_target_pairs={{0,96},{1,97},{2,98},{3,99},{4,100},{5,101},{6,102},{7,103},{8,104... | collective-permute-start | bytes 3551240 | tf_op jit(solution)/shard_map/ppermute | solution.py:41
  122.2 47.8 %collective-permute-start.33 = (bf16[1088,640]{1,0:T(8,128)(2,1)}, bf16[1088,640]{1,0:T(8,128)(2,1)}, u32[]{:S(2)}, u32[]{:S(2)}) collective-permute-start(bf16[1088,640]{1,0:T(8,128)(2,1)} %maximum_dynamic-update-slice_fusion.1), channel_id=1, source_target_pairs={{0,2},{1,3},{2,4},{3,5},{4,6},{5,7},{6,0},{7,1},{8,10},{9,11},{10,... | collective-permute-start | bytes 4177928 | tf_op jit(solution)/shard_map/ppermute | solution.py:41
  122.2 53.6 %collective-permute-start.35 = (bf16[1088,640]{1,0:T(8,128)(2,1)}, bf16[1088,640]{1,0:T(8,128)(2,1)}, u32[]{:S(2)}, u32[]{:S(2)}) collective-permute-start(bf16[1088,640]{1,0:T(8,128)(2,1)} %maximum_dynamic-update-slice_fusion.1), channel_id=1, source_target_pairs={{0,6},{1,7},{2,0},{3,1},{4,2},{5,3},{6,4},{7,5},{8,14},{9,15},{10,... | collective-permute-start | bytes 4177928 | tf_op jit(solution)/shard_map/ppermute | solution.py:41
  141.8 19.5 %collective-permute-start.6 = (bf16[1088,640]{1,0:T(8,128)(2,1)}, bf16[1088,640]{1,0:T(8,128)(2,1)}, u32[]{:S(2)}, u32[]{:S(2)}) collective-permute-start(bf16[1088,640]{1,0:T(8,128)(2,1)} %maximum_dynamic-update-slice_fusion), channel_id=1, source_target_pairs={{0,8},{1,9},{2,10},{3,11},{4,12},{5,13},{6,14},{7,15},{8,0},{9,1},... | collective-permute-start | bytes 4177928 | tf_op jit(solution)/shard_map/ppermute | solution.py:41
  146.6 37.6 %collective-permute-start.7 = (bf16[1088,640]{1,0:T(8,128)(2,1)}, bf16[1088,640]{1,0:T(8,128)(2,1)}, u32[]{:S(2)}, u32[]{:S(2)}) collective-permute-start(bf16[1088,640]{1,0:T(8,128)(2,1)} %maximum_dynamic-update-slice_fusion), channel_id=1, source_target_pairs={{0,2},{1,3},{2,4},{3,5},{4,6},{5,7},{6,0},{7,1},{8,10},{9,11},{10,... | collective-permute-start | bytes 4177928 | tf_op jit(solution)/shard_map/ppermute | solution.py:41
  146.6 44.9 %collective-permute-start.9 = (bf16[1088,640]{1,0:T(8,128)(2,1)}, bf16[1088,640]{1,0:T(8,128)(2,1)}, u32[]{:S(2)}, u32[]{:S(2)}) collective-permute-start(bf16[1088,640]{1,0:T(8,128)(2,1)} %maximum_dynamic-update-slice_fusion), channel_id=1, source_target_pairs={{0,6},{1,7},{2,0},{3,1},{4,2},{5,3},{6,4},{7,5},{8,14},{9,15},{10,... | collective-permute-start | bytes 4177928 | tf_op jit(solution)/shard_map/ppermute | solution.py:41
  161.4 42.4 %collective-permute-start.21 = (bf16[136,2176]{1,0:T(8,128)(2,1)}, bf16[136,2176]{1,0:T(8,128)(2,1)}, u32[]{:S(2)}, u32[]{:S(2)}) collective-permute-start(bf16[136,2176]{1,0:T(8,128)(2,1)} %slice.660), channel_id=1, source_target_pairs={{0,32},{1,33},{2,34},{3,35},{4,36},{5,37},{6,38},{7,39},{8,40},{9,... | collective-permute-start | bytes 1775624 | tf_op jit(solution)/shard_map/ppermute | solution.py:41
  170.0 40.1 %collective-permute-start.22 = (bf16[136,2176]{1,0:T(8,128)(2,1)}, bf16[136,2176]{1,0:T(8,128)(2,1)}, u32[]{:S(2)}, u32[]{:S(2)}) collective-permute-start(bf16[136,2176]{1,0:T(8,128)(2,1)} %slice.661), channel_id=1, source_target_pairs={{0,96},{1,97},{2,98},{3,99},{4,100},{5,101},{6,102},{7,103},{8,104... | collective-permute-start | bytes 1775624 | tf_op jit(solution)/shard_map/ppermute | solution.py:41
  175.8 30.0 %collective-permute-start.47 = (bf16[136,2176]{1,0:T(8,128)(2,1)}, bf16[136,2176]{1,0:T(8,128)(2,1)}, u32[]{:S(2)}, u32[]{:S(2)}) collective-permute-start(bf16[136,2176]{1,0:T(8,128)(2,1)} %slice.686), channel_id=1, source_target_pairs={{0,32},{1,33},{2,34},{3,35},{4,36},{5,37},{6,38},{7,39},{8,40},{9,... | collective-permute-start | bytes 1775624 | tf_op jit(solution)/shard_map/ppermute | solution.py:41
  184.2 27.9 %collective-permute-start.48 = (bf16[136,2176]{1,0:T(8,128)(2,1)}, bf16[136,2176]{1,0:T(8,128)(2,1)}, u32[]{:S(2)}, u32[]{:S(2)}) collective-permute-start(bf16[136,2176]{1,0:T(8,128)(2,1)} %slice.687), channel_id=1, source_target_pairs={{0,96},{1,97},{2,98},{3,99},{4,100},{5,101},{6,102},{7,103},{8,104... | collective-permute-start | bytes 1775624 | tf_op jit(solution)/shard_map/ppermute | solution.py:41
  191.6 54.6 %collective-permute-start.18 = (bf16[272,2176]{1,0:T(8,128)(2,1)}, bf16[272,2176]{1,0:T(8,128)(2,1)}, u32[]{:S(2)}, u32[]{:S(2)}) collective-permute-start(bf16[272,2176]{1,0:T(8,128)(2,1)} %collective-permute-done.17), channel_id=1, source_target_pairs={{0,8},{1,9},{2,10},{3,11},{4,12},{5,13},{6,14},{7,15},{8,0},{9,1},... | collective-permute-start | bytes 3551240 | tf_op jit(solution)/shard_map/ppermute | solution.py:41
  203.8 19.6 %collective-permute-start.37 = (bf16[544,640]{1,0:T(8,128)(2,1)S(1)}, bf16[544,640]{1,0:T(8,128)(2,1)S(1)}, u32[]{:S(2)}, u32[]{:S(2)}) collective-permute-start(bf16[544,640]{1,0:T(8,128)(2,1)S(1)} %slice.671), channel_id=1, source_target_pairs={{0,2},{1,3},{2,4},{3,5},{4,6},{5,7},{6,0},{7,1},{8,10},{9,11},{10,... | collective-permute-start | bytes 2088968 | tf_op jit(solution)/shard_map/ppermute | solution.py:41
  205.7 19.2 %collective-permute-start.38 = (bf16[544,640]{1,0:T(8,128)(2,1)S(1)}, bf16[544,640]{1,0:T(8,128)(2,1)S(1)}, u32[]{:S(2)}, u32[]{:S(2)}) collective-permute-start(bf16[544,640]{1,0:T(8,128)(2,1)S(1)} %slice.672), channel_id=1, source_target_pairs={{0,6},{1,7},{2,0},{3,1},{4,2},{5,3},{6,4},{7,5},{8,14},{9,15},{10,... | collective-permute-start | bytes 2088968 | tf_op jit(solution)/shard_map/ppermute | solution.py:41
  210.1 28.0 %collective-permute-start.11 = (bf16[544,640]{1,0:T(8,128)(2,1)}, bf16[544,640]{1,0:T(8,128)(2,1)}, u32[]{:S(2)}, u32[]{:S(2)}) collective-permute-start(bf16[544,640]{1,0:T(8,128)(2,1)} %slice.645), channel_id=1, source_target_pairs={{0,2},{1,3},{2,4},{3,5},{4,6},{5,7},{6,0},{7,1},{8,10},{9,11},{10,... | collective-permute-start | bytes 2088968 | tf_op jit(solution)/shard_map/ppermute | solution.py:41
  212.1 28.0 %collective-permute-start.12 = (bf16[544,640]{1,0:T(8,128)(2,1)}, bf16[544,640]{1,0:T(8,128)(2,1)}, u32[]{:S(2)}, u32[]{:S(2)}) collective-permute-start(bf16[544,640]{1,0:T(8,128)(2,1)} %slice.646), channel_id=1, source_target_pairs={{0,6},{1,7},{2,0},{3,1},{4,2},{5,3},{6,4},{7,5},{8,14},{9,15},{10,... | collective-permute-start | bytes 2088968 | tf_op jit(solution)/shard_map/ppermute | solution.py:41
  223.4 226.0 %collective-permute-start.52 = (bf16[128,1088]{1,0:T(8,128)(2,1)}, bf16[128,1088]{1,0:T(8,128)(2,1)}, u32[]{:S(2)}, u32[]{:S(2)}) collective-permute-start(bf16[128,1088]{1,0:T(8,128)(2,1)} %get-tuple-element.214), channel_id=1, source_target_pairs={{0,1},{1,0},{2,3},{3,2},{4,5},{5,4},{6,7},{7,6},{8,9},{9,8},{10,11... | collective-permute-start | bytes 835592 | tf_op jit(solution)/shard_map/ppermute | solution.py:41
  224.9 26.1 %collective-permute-start.20 = (bf16[272,2176]{1,0:T(8,128)(2,1)}, bf16[272,2176]{1,0:T(8,128)(2,1)}, u32[]{:S(2)}, u32[]{:S(2)}) collective-permute-start(bf16[272,2176]{1,0:T(8,128)(2,1)} %collective-permute-done.19), channel_id=1, source_target_pairs={{0,8},{1,9},{2,10},{3,11},{4,12},{5,13},{6,14},{7,15},{8,0},{9,1},... | collective-permute-start | bytes 3551240 | tf_op jit(solution)/shard_map/ppermute | solution.py:41
  240.1 21.2 %collective-permute-start.46 = (bf16[272,2176]{1,0:T(8,128)(2,1)}, bf16[272,2176]{1,0:T(8,128)(2,1)}, u32[]{:S(2)}, u32[]{:S(2)}) collective-permute-start(bf16[272,2176]{1,0:T(8,128)(2,1)} %collective-permute-done.45), channel_id=1, source_target_pairs={{0,8},{1,9},{2,10},{3,11},{4,12},{5,13},{6,14},{7,15},{8,0},{9,1},... | collective-permute-start | bytes 3551240 | tf_op jit(solution)/shard_map/ppermute | solution.py:41
  246.2 18.9 %collective-permute-start.34 = (bf16[1088,640]{1,0:T(8,128)(2,1)}, bf16[1088,640]{1,0:T(8,128)(2,1)}, u32[]{:S(2)}, u32[]{:S(2)}) collective-permute-start(bf16[1088,640]{1,0:T(8,128)(2,1)} %collective-permute-done.33), channel_id=1, source_target_pairs={{0,8},{1,9},{2,10},{3,11},{4,12},{5,13},{6,14},{7,15},{8,0},{9,1},... | collective-permute-start | bytes 4177928 | tf_op jit(solution)/shard_map/ppermute | solution.py:41
  261.3 23.2 %collective-permute-start.10 = (bf16[1088,640]{1,0:T(8,128)(2,1)}, bf16[1088,640]{1,0:T(8,128)(2,1)}, u32[]{:S(2)}, u32[]{:S(2)}) collective-permute-start(bf16[1088,640]{1,0:T(8,128)(2,1)} %collective-permute-done.9), channel_id=1, source_target_pairs={{0,8},{1,9},{2,10},{3,11},{4,12},{5,13},{6,14},{7,15},{8,0},{9,1},... | collective-permute-start | bytes 4177928 | tf_op jit(solution)/shard_map/ppermute | solution.py:41
  265.1 30.1 %collective-permute-start.23 = (bf16[272,2176]{1,0:T(8,128)(2,1)}, bf16[272,2176]{1,0:T(8,128)(2,1)}, u32[]{:S(2)}, u32[]{:S(2)}) collective-permute-start(bf16[272,2176]{1,0:T(8,128)(2,1)} %constant_dynamic-update-slice_fusion.38), channel_id=1, source_target_pairs={{0,8},{1,9},{2,10},{3,11},{4,12},{5,13},{6,14},{7,15},{8,0},{9,1},... | collective-permute-start | bytes 3551240 | tf_op jit(solution)/shard_map/ppermute | solution.py:41
  268.9 28.7 %collective-permute-start.49 = (bf16[272,2176]{1,0:T(8,128)(2,1)}, bf16[272,2176]{1,0:T(8,128)(2,1)}, u32[]{:S(2)}, u32[]{:S(2)}) collective-permute-start(bf16[272,2176]{1,0:T(8,128)(2,1)} %copy-done.39), channel_id=1, source_target_pairs={{0,8},{1,9},{2,10},{3,11},{4,12},{5,13},{6,14},{7,15},{8,0},{9,1},... | collective-permute-start | bytes 3551240 | tf_op jit(solution)/shard_map/ppermute | solution.py:41
  272.7 31.9 %collective-permute-start.39 = (bf16[1088,640]{1,0:T(8,128)(2,1)}, bf16[1088,640]{1,0:T(8,128)(2,1)}, u32[]{:S(2)}, u32[]{:S(2)}) collective-permute-start(bf16[1088,640]{1,0:T(8,128)(2,1)} %constant_dynamic-update-slice_fusion.40), channel_id=1, source_target_pairs={{0,8},{1,9},{2,10},{3,11},{4,12},{5,13},{6,14},{7,15},{8,0},{9,1},... | collective-permute-start | bytes 4177928 | tf_op jit(solution)/shard_map/ppermute | solution.py:41
  449.2 95.6 %collective-permute-start.51 = (bf16[128,1088]{1,0:T(8,128)(2,1)}, bf16[128,1088]{1,0:T(8,128)(2,1)}, u32[]{:S(2)}, u32[]{:S(2)}) collective-permute-start(bf16[128,1088]{1,0:T(8,128)(2,1)} %copy.222), channel_id=1, source_target_pairs={{0,1},{1,0},{2,3},{3,2},{4,5},{5,4},{6,7},{7,6},{8,9},{9,8},{10,11... | collective-permute-start | bytes 835592 | tf_op jit(solution)/shard_map/ppermute | solution.py:41
  473.5 156.9 %collective-permute-start.103 = (bf16[1088,2176]{1,0:T(8,128)(2,1)}, bf16[1088,2176]{1,0:T(8,128)(2,1)}, u32[]{:S(2)}, u32[]{:S(2)}) collective-permute-start(bf16[1088,2176]{1,0:T(8,128)(2,1)} %convolution_convert_fusion), channel_id=1, source_target_pairs={{0,8},{1,9},{2,10},{3,11},{4,12},{5,13},{6,14},{7,15},{8,0},{9,1},... | collective-permute-start | bytes 14204936 | tf_op jit(solution)/shard_map/ppermute | solution.py:41
  529.6 20.2 %collective-permute-start.54 = (bf16[128,1088]{1,0:T(8,128)(2,1)}, bf16[128,1088]{1,0:T(8,128)(2,1)}, u32[]{:S(2)}, u32[]{:S(2)}) collective-permute-start(bf16[128,1088]{1,0:T(8,128)(2,1)} %get-tuple-element.107), channel_id=1, source_target_pairs={{0,1},{1,0},{2,3},{3,2},{4,5},{5,4},{6,7},{7,6},{8,9},{9,8},{10,11... | collective-permute-start | bytes 835592 | tf_op jit(solution)/shard_map/ppermute | solution.py:41
  544.2 98.5 %collective-permute-start.72 = (bf16[1088,2304]{1,0:T(8,128)(2,1)}, bf16[1088,2304]{1,0:T(8,128)(2,1)}, u32[]{:S(2)}, u32[]{:S(2)}) collective-permute-start(bf16[1088,2304]{1,0:T(8,128)(2,1)} %fusion.1), channel_id=1, source_target_pairs={{0,8},{1,9},{2,10},{3,11},{4,12},{5,13},{6,14},{7,15},{8,0},{9,1},... | collective-permute-start | bytes 15040520 | tf_op jit(solution)/shard_map/ppermute | solution.py:41
  570.8 67.4 %collective-permute-start.88 = (bf16[1088,2176]{1,0:T(8,128)(2,1)}, bf16[1088,2176]{1,0:T(8,128)(2,1)}, u32[]{:S(2)}, u32[]{:S(2)}) collective-permute-start(bf16[1088,2176]{1,0:T(8,128)(2,1)} %convolution_convert_fusion.1), channel_id=1, source_target_pairs={{0,8},{1,9},{2,10},{3,11},{4,12},{5,13},{6,14},{7,15},{8,0},{9,1},... | collective-permute-start | bytes 14204936 | tf_op jit(solution)/shard_map/ppermute | solution.py:41
  628.7 27.3 %collective-permute-start.56 = (bf16[1088,2304]{1,0:T(8,128)(2,1)}, bf16[1088,2304]{1,0:T(8,128)(2,1)}, u32[]{:S(2)}, u32[]{:S(2)}) collective-permute-start(bf16[1088,2304]{1,0:T(8,128)(2,1)} %fusion), channel_id=1, source_target_pairs={{0,8},{1,9},{2,10},{3,11},{4,12},{5,13},{6,14},{7,15},{8,0},{9,1},... | collective-permute-start | bytes 15040520 | tf_op jit(solution)/shard_map/ppermute | solution.py:41
  642.6 22.0 %collective-permute-start.89 = (bf16[136,2176]{1,0:T(8,128)(2,1)S(1)}, bf16[136,2176]{1,0:T(8,128)(2,1)S(1)}, u32[]{:S(2)}, u32[]{:S(2)}) collective-permute-start(bf16[136,2176]{1,0:T(8,128)(2,1)S(1)} %get-tuple-element.140), channel_id=1, source_target_pairs={{0,32},{1,33},{2,34},{3,35},{4,36},{5,37},{6,38},{7,39},{8,40},{9,... | collective-permute-start | bytes 1775624 | tf_op jit(solution)/shard_map/ppermute | solution.py:41
  642.7 21.9 %collective-permute-start.91 = (bf16[136,2176]{1,0:T(8,128)(2,1)S(1)}, bf16[136,2176]{1,0:T(8,128)(2,1)S(1)}, u32[]{:S(2)}, u32[]{:S(2)}) collective-permute-start(bf16[136,2176]{1,0:T(8,128)(2,1)S(1)} %get-tuple-element.142), channel_id=1, source_target_pairs={{0,96},{1,97},{2,98},{3,99},{4,100},{5,101},{6,102},{7,103},{8,104... | collective-permute-start | bytes 1775624 | tf_op jit(solution)/shard_map/ppermute | solution.py:41
  652.3 19.8 %collective-permute-start.73 = (bf16[544,640]{1,0:T(8,128)(2,1)S(1)}, bf16[544,640]{1,0:T(8,128)(2,1)S(1)}, u32[]{:S(2)}, u32[]{:S(2)}) collective-permute-start(bf16[544,640]{1,0:T(8,128)(2,1)S(1)} %get-tuple-element.134), channel_id=1, source_target_pairs={{0,2},{1,3},{2,4},{3,5},{4,6},{5,7},{6,0},{7,1},{8,10},{9,11},{10,... | collective-permute-start | bytes 2088968 | tf_op jit(solution)/shard_map/ppermute | solution.py:41
  652.3 20.1 %collective-permute-start.75 = (bf16[544,640]{1,0:T(8,128)(2,1)S(1)}, bf16[544,640]{1,0:T(8,128)(2,1)S(1)}, u32[]{:S(2)}, u32[]{:S(2)}) collective-permute-start(bf16[544,640]{1,0:T(8,128)(2,1)S(1)} %get-tuple-element.136), channel_id=1, source_target_pairs={{0,6},{1,7},{2,0},{3,1},{4,2},{5,3},{6,4},{7,5},{8,14},{9,15},{10,... | collective-permute-start | bytes 2088968 | tf_op jit(solution)/shard_map/ppermute | solution.py:41
  656.1 33.8 %collective-permute-start.107 = (bf16[272,2176]{1,0:T(8,128)(2,1)S(1)}, bf16[272,2176]{1,0:T(8,128)(2,1)S(1)}, u32[]{:S(2)}, u32[]{:S(2)}) collective-permute-start(bf16[272,2176]{1,0:T(8,128)(2,1)S(1)} %pad_maximum_fusion.7), channel_id=1, source_target_pairs={{0,96},{1,97},{2,98},{3,99},{4,100},{5,101},{6,102},{7,103},{8,104... | collective-permute-start | bytes 3551240 | tf_op jit(solution)/shard_map/ppermute | solution.py:41
  664.5 29.1 %collective-permute-start.105 = (bf16[272,2176]{1,0:T(8,128)(2,1)S(1)}, bf16[272,2176]{1,0:T(8,128)(2,1)S(1)}, u32[]{:S(2)}, u32[]{:S(2)}) collective-permute-start(bf16[272,2176]{1,0:T(8,128)(2,1)S(1)} %pad_maximum_fusion.6), channel_id=1, source_target_pairs={{0,32},{1,33},{2,34},{3,35},{4,36},{5,37},{6,38},{7,39},{8,40},{9,... | collective-permute-start | bytes 3551240 | tf_op jit(solution)/shard_map/ppermute | solution.py:41
  664.6 31.2 %collective-permute-start.57 = (bf16[544,640]{1,0:T(8,128)(2,1)S(1)}, bf16[544,640]{1,0:T(8,128)(2,1)S(1)}, u32[]{:S(2)}, u32[]{:S(2)}) collective-permute-start(bf16[544,640]{1,0:T(8,128)(2,1)S(1)} %get-tuple-element.128), channel_id=1, source_target_pairs={{0,2},{1,3},{2,4},{3,5},{4,6},{5,7},{6,0},{7,1},{8,10},{9,11},{10,... | collective-permute-start | bytes 2088968 | tf_op jit(solution)/shard_map/ppermute | solution.py:41
  672.0 24.3 %collective-permute-start.59 = (bf16[544,640]{1,0:T(8,128)(2,1)S(1)}, bf16[544,640]{1,0:T(8,128)(2,1)S(1)}, u32[]{:S(2)}, u32[]{:S(2)}) collective-permute-start(bf16[544,640]{1,0:T(8,128)(2,1)S(1)} %get-tuple-element.130), channel_id=1, source_target_pairs={{0,6},{1,7},{2,0},{3,1},{4,2},{5,3},{6,4},{7,5},{8,14},{9,15},{10,... | collective-permute-start | bytes 2088968 | tf_op jit(solution)/shard_map/ppermute | solution.py:41
  672.4 70.1 %collective-permute-start.92 = (bf16[272,2176]{1,0:T(8,128)(2,1)S(1)}, bf16[272,2176]{1,0:T(8,128)(2,1)S(1)}, u32[]{:S(2)}, u32[]{:S(2)}) collective-permute-start(bf16[272,2176]{1,0:T(8,128)(2,1)S(1)} %pad_maximum_fusion.5), channel_id=1, source_target_pairs={{0,96},{1,97},{2,98},{3,99},{4,100},{5,101},{6,102},{7,103},{8,104... | collective-permute-start | bytes 3551240 | tf_op jit(solution)/shard_map/ppermute | solution.py:41
  689.9 53.4 %collective-permute-start.90 = (bf16[272,2176]{1,0:T(8,128)(2,1)S(1)}, bf16[272,2176]{1,0:T(8,128)(2,1)S(1)}, u32[]{:S(2)}, u32[]{:S(2)}) collective-permute-start(bf16[272,2176]{1,0:T(8,128)(2,1)S(1)} %pad_maximum_fusion.4), channel_id=1, source_target_pairs={{0,32},{1,33},{2,34},{3,35},{4,36},{5,37},{6,38},{7,39},{8,40},{9,... | collective-permute-start | bytes 3551240 | tf_op jit(solution)/shard_map/ppermute | solution.py:41
  693.7 89.9 %collective-permute-start.76 = (bf16[1088,640]{1,0:T(8,128)(2,1)S(1)}, bf16[1088,640]{1,0:T(8,128)(2,1)S(1)}, u32[]{:S(2)}, u32[]{:S(2)}) collective-permute-start(bf16[1088,640]{1,0:T(8,128)(2,1)S(1)} %pad_maximum_fusion.3), channel_id=1, source_target_pairs={{0,6},{1,7},{2,0},{3,1},{4,2},{5,3},{6,4},{7,5},{8,14},{9,15},{10,... | collective-permute-start | bytes 4177928 | tf_op jit(solution)/shard_map/ppermute | solution.py:41
  696.4 32.0 %collective-permute-start.110 = (bf16[136,640]{1,0:T(8,128)(2,1)S(1)}, bf16[136,640]{1,0:T(8,128)(2,1)S(1)}, u32[]{:S(2)}, u32[]{:S(2)}) collective-permute-start(bf16[136,640]{1,0:T(8,128)(2,1)S(1)} %get-tuple-element.176), channel_id=1, source_target_pairs={{0,6},{1,7},{2,0},{3,1},{4,2},{5,3},{6,4},{7,5},{8,14},{9,15},{10,... | collective-permute-start | bytes 522248 | tf_op jit(solution)/shard_map/ppermute | solution.py:41
  736.6 47.1 %collective-permute-start.74 = (bf16[1088,640]{1,0:T(8,128)(2,1)S(1)}, bf16[1088,640]{1,0:T(8,128)(2,1)S(1)}, u32[]{:S(2)}, u32[]{:S(2)}) collective-permute-start(bf16[1088,640]{1,0:T(8,128)(2,1)S(1)} %pad_maximum_fusion.2), channel_id=1, source_target_pairs={{0,2},{1,3},{2,4},{3,5},{4,6},{5,7},{6,0},{7,1},{8,10},{9,11},{10,... | collective-permute-start | bytes 4177928 | tf_op jit(solution)/shard_map/ppermute | solution.py:41
  742.3 77.9 %collective-permute-start.60 = (bf16[1088,640]{1,0:T(8,128)(2,1)S(1)}, bf16[1088,640]{1,0:T(8,128)(2,1)S(1)}, u32[]{:S(2)}, u32[]{:S(2)}) collective-permute-start(bf16[1088,640]{1,0:T(8,128)(2,1)S(1)} %pad_maximum_fusion.1), channel_id=1, source_target_pairs={{0,6},{1,7},{2,0},{3,1},{4,2},{5,3},{6,4},{7,5},{8,14},{9,15},{10,... | collective-permute-start | bytes 4177928 | tf_op jit(solution)/shard_map/ppermute | solution.py:41
  743.8 29.8 %collective-permute-start.93 = (bf16[136,640]{1,0:T(8,128)(2,1)S(1)}, bf16[136,640]{1,0:T(8,128)(2,1)S(1)}, u32[]{:S(2)}, u32[]{:S(2)}) collective-permute-start(bf16[136,640]{1,0:T(8,128)(2,1)S(1)} %get-tuple-element.168), channel_id=1, source_target_pairs={{0,2},{1,3},{2,4},{3,5},{4,6},{5,7},{6,0},{7,1},{8,10},{9,11},{10,... | collective-permute-start | bytes 522248 | tf_op jit(solution)/shard_map/ppermute | solution.py:41
  749.5 24.2 %collective-permute-start.95 = (bf16[136,640]{1,0:T(8,128)(2,1)S(1)}, bf16[136,640]{1,0:T(8,128)(2,1)S(1)}, u32[]{:S(2)}, u32[]{:S(2)}) collective-permute-start(bf16[136,640]{1,0:T(8,128)(2,1)S(1)} %get-tuple-element.170), channel_id=1, source_target_pairs={{0,6},{1,7},{2,0},{3,1},{4,2},{5,3},{6,4},{7,5},{8,14},{9,15},{10,... | collective-permute-start | bytes 522248 | tf_op jit(solution)/shard_map/ppermute | solution.py:41
  779.8 19.3 %collective-permute-start.96 = (bf16[272,640]{1,0:T(8,128)(2,1)S(1)}, bf16[272,640]{1,0:T(8,128)(2,1)S(1)}, u32[]{:S(2)}, u32[]{:S(2)}) collective-permute-start(bf16[272,640]{1,0:T(8,128)(2,1)S(1)} %pad_maximum_fusion.41), channel_id=1, source_target_pairs={{0,6},{1,7},{2,0},{3,1},{4,2},{5,3},{6,4},{7,5},{8,14},{9,15},{10,... | collective-permute-start | bytes 1044488 | tf_op jit(solution)/shard_map/ppermute | solution.py:41
  796.2 30.7 %collective-permute-start.58 = (bf16[1088,640]{1,0:T(8,128)(2,1)S(1)}, bf16[1088,640]{1,0:T(8,128)(2,1)S(1)}, u32[]{:S(2)}, u32[]{:S(2)}) collective-permute-start(bf16[1088,640]{1,0:T(8,128)(2,1)S(1)} %pad_maximum_fusion), channel_id=1, source_target_pairs={{0,2},{1,3},{2,4},{3,5},{4,6},{5,7},{6,0},{7,1},{8,10},{9,11},{10,... | collective-permute-start | bytes 4177928 | tf_op jit(solution)/shard_map/ppermute | solution.py:41
  807.9 25.6 %collective-permute-start.98 = (bf16[136,640]{1,0:T(8,128)(2,1)S(1)}, bf16[136,640]{1,0:T(8,128)(2,1)S(1)}, u32[]{:S(2)}, u32[]{:S(2)}) collective-permute-start(bf16[136,640]{1,0:T(8,128)(2,1)S(1)} %get-tuple-element.101), channel_id=1, source_target_pairs={{0,2},{1,3},{2,4},{3,5},{4,6},{5,7},{6,0},{7,1},{8,10},{9,11},{10,... | collective-permute-start | bytes 522248 | tf_op jit(solution)/shard_map/ppermute | solution.py:41
  810.6 20.3 %collective-permute-start.99 = (bf16[136,640]{1,0:T(8,128)(2,1)S(1)}, bf16[136,640]{1,0:T(8,128)(2,1)S(1)}, u32[]{:S(2)}, u32[]{:S(2)}) collective-permute-start(bf16[136,640]{1,0:T(8,128)(2,1)S(1)} %get-tuple-element.101), channel_id=1, source_target_pairs={{0,6},{1,7},{2,0},{3,1},{4,2},{5,3},{6,4},{7,5},{8,14},{9,15},{10,... | collective-permute-start | bytes 522248 | tf_op jit(solution)/shard_map/ppermute | solution.py:41
  818.9 21.3 %collective-permute-start.81 = (bf16[136,640]{1,0:T(8,128)(2,1)S(1)}, bf16[136,640]{1,0:T(8,128)(2,1)S(1)}, u32[]{:S(2)}, u32[]{:S(2)}) collective-permute-start(bf16[136,640]{1,0:T(8,128)(2,1)S(1)} %constant_dynamic-slice_fusion.21), channel_id=1, source_target_pairs={{0,17},{1,16},{2,19},{3,18},{4,21},{5,20},{6,23},{7,22},{8,25},{9,... | collective-permute-start | bytes 522248 | tf_op jit(solution)/shard_map/ppermute | solution.py:41
  843.0 19.7 %collective-permute-start.64 = (bf16[272,640]{1,0:T(8,128)(2,1)}, bf16[272,640]{1,0:T(8,128)(2,1)}, u32[]{:S(2)}, u32[]{:S(2)}) collective-permute-start(bf16[272,640]{1,0:T(8,128)(2,1)} %pad_maximum_fusion.37), channel_id=1, source_target_pairs={{0,96},{1,97},{2,98},{3,99},{4,100},{5,101},{6,102},{7,103},{8,104... | collective-permute-start | bytes 1044488 | tf_op jit(solution)/shard_map/ppermute | solution.py:41
  843.8 18.9 %collective-permute-start.62 = (bf16[272,640]{1,0:T(8,128)(2,1)}, bf16[272,640]{1,0:T(8,128)(2,1)}, u32[]{:S(2)}, u32[]{:S(2)}) collective-permute-start(bf16[272,640]{1,0:T(8,128)(2,1)} %pad_maximum_fusion.36), channel_id=1, source_target_pairs={{0,32},{1,33},{2,34},{3,35},{4,36},{5,37},{6,38},{7,39},{8,40},{9,... | collective-permute-start | bytes 1044488 | tf_op jit(solution)/shard_map/ppermute | solution.py:41
  (182 other events, 1285.7 us)

commit v2 on v1

--- a/solution.py
+++ b/solution.py
@@ -39,10 +39,6 @@
         ix, iy, ic, iz, it = (ix + x) % 4, (iy + y) % 2, (ic + c) % 2, (iz + z) % 4, (it + t) % 2
         pairs.append((i, (((ix * 2 + iy) * 2 + ic) * 4 + iz) * 2 + it))
     return lax.ppermute(value, ("dp", "ctx", "tensor"), pairs)
-
-
-def pair_up(first, mine, other):
-    return jnp.where(first, jnp.concatenate([mine, other], 0), jnp.concatenate([other, mine], 0))
 
 
 def ring_gather(axis, piece):
@@ -88,6 +84,261 @@
     return lax.dynamic_slice_in_dim(array, start, count, 0)
 
 
+ROWS = 68
+TALL = 80
+BLOCK = 272
+NEAR = 144
+Q_COLS = 512
+T_START = 2048
+T_COLS = 256
+M_COLS = 2176
+
+
+def peer_at(x=0, y=0, c=0, z=0, t=0):
+    at = places()
+    dp = (lax.rem(at["x"] + x + 4, 4) * 2 + lax.rem(at["y"] + y, 2)) * 2 + lax.rem(at["c"] + c, 2)
+    return (dp, lax.rem(at["z"] + z + 4, 4), lax.rem(at["t"] + t, 2))
+
+
+class Copies:
+    def __init__(self, send_sem, recv_sem):
+        self.send_sem, self.recv_sem = send_sem, recv_sem
+        self.count = 0
+        self.open = []
+
+    def to(self, peer, src, dst):
+        n = self.count
+        self.count += 1
+        copy = pltpu.make_async_remote_copy(
+            src_ref=src,
+            dst_ref=dst,
+            send_sem=self.send_sem.at[n],
+            recv_sem=self.recv_sem.at[n],
+            device_id=peer,
+            device_id_type=MESH,
+        )
+        copy.start()
+        self.open.append(copy.wait_send)
+        return copy.wait_recv
+
+    def here(self, src, dst):
+        n = self.count
+        self.count += 1
+        copy = pltpu.make_async_copy(src, dst, self.send_sem.at[n])
+        copy.start()
+        return copy.wait
+
+    def close(self):
+        for wait in self.open:
+            wait()
+        self.open = []
+
+
+def rows_at(block, count=BLOCK, skip=0):
+    return pl.ds(pl.multiple_of(block * BLOCK + skip, 16), count)
+
+
+class RingX:
+    def __init__(self, copies, own, buf, lanes, share):
+        self.copies, self.own, self.buf, self.lanes, self.share = copies, own, buf, lanes, share
+        at = places()
+        self.c, self.x = at["c"], at["x"]
+        self.last = []
+
+    def view(self, distance, count=BLOCK, skip=0):
+        block = lax.rem(self.x + distance + 4, 4)
+        return self.buf.at[self.c, rows_at(block, count, skip), self.lanes]
+
+    def sibling(self, src, dst):
+        if self.share:
+            self.last.append(self.copies.to(peer_at(c=1), src, dst))
+
+    def start(self):
+        self.from_below = self.copies.to(peer_at(x=1), self.own, self.view(0))
+        self.from_above = self.copies.to(peer_at(x=-1), self.own, self.view(0))
+        self.last.append(self.copies.here(self.own, self.view(0)))
+        self.sibling(self.own, self.view(0))
+
+    def forward(self):
+        self.from_below()
+        part = self.view(-1, NEAR)
+        far_a = self.copies.to(peer_at(x=1), part, part)
+        self.from_above()
+        part = self.view(1, BLOCK - NEAR, NEAR)
+        far_b = self.copies.to(peer_at(x=-1), part, part)
+        self.far = (far_a, far_b)
+        self.sibling(self.view(-1), self.view(-1))
+        self.sibling(self.view(1), self.view(1))
+
+    def finish(self):
+        for wait in self.far:
+            wait()
+        self.sibling(self.view(2), self.view(2))
+
+    def close(self):
+        for wait in self.last:
+            wait()
+
+
+class RingZ:
+    def __init__(self, copies, buf):
+        self.copies, self.buf = copies, buf
+        at = places()
+        self.c, self.z = at["c"], at["z"]
+        self.last = []
+
+    def view(self, distance, rows=slice(None)):
+        block = lax.rem(self.z + distance + 4, 4)
+        return self.buf.at[self.c, rows, pl.ds(pl.multiple_of(block * Q_COLS, 128), Q_COLS)]
+
+    def sibling(self, src):
+        self.last.append(self.copies.to(peer_at(c=1), src, src))
+
+    def start(self):
+        own = self.view(0)
+        self.from_below = self.copies.to(peer_at(z=1), own, own)
+        self.from_above = self.copies.to(peer_at(z=-1), own, own)
+        self.sibling(own)
+
+    def forward(self):
+        self.from_below()
+        part = self.view(-1, pl.ds(0, 544))
+        far_a = self.copies.to(peer_at(z=1), part, part)
+        self.from_above()
+        part = self.view(1, pl.ds(544, 544))
+        far_b = self.copies.to(peer_at(z=-1), part, part)
+        self.far = (far_a, far_b)
+        self.sibling(self.view(-1))
+        self.sibling(self.view(1))
+
+    def finish(self):
+        for wait in self.far:
+            wait()
+        self.sibling(self.view(2))
+
+    def close(self):
+        for wait in self.last:
+            wait()
+
+
+def exchange_shards(copies, mine, landed):
+    c = places()["c"]
+    waits = [
+        copies.to(peer_at(c=1), mine.at[1 - c], landed.at[1]),
+        copies.to(peer_at(y=1), mine.at[c], landed.at[2]),
+        copies.to(peer_at(y=1, c=1), mine.at[1 - c], landed.at[3]),
+    ]
+    waits.append(copies.here(mine.at[c], landed.at[0]))
+    return waits
+
+
+def assemble(landed, own):
+    at = places()
+    width = own.shape[1]
+    for start in range(0, width, 256):
+        lanes = slice(start, min(start + 256, width))
+        parts = []
+        for j in range(4):
+            slot = lax.rem(j // 2 + at["y"], 2) * 2 + lax.rem(j % 2 + at["c"], 2)
+            parts.append(landed[slot, :, lanes].astype(F32)[:ROWS])
+        own[:, lanes] = jnp.concatenate(parts, 0).astype(BF16)
+
+
+def gather_barrier():
+    barrier = pltpu.get_barrier_semaphore()
+    peers = [dict(c=1), dict(y=1), dict(y=1, c=1), dict(x=1), dict(x=-1), dict(z=1), dict(z=-1)]
+    for peer in peers:
+        pl.semaphore_signal(barrier, inc=1, device_id=peer_at(**peer), device_id_type=MESH)
+    pl.semaphore_wait(barrier, len(peers))
+
+
+def gather_kernel(*refs, layers):
+    q_in, mt_in = refs[:layers], refs[layers : 2 * layers]
+    attn, mlp = refs[2 * layers : 3 * layers], refs[3 * layers : 4 * layers]
+    q_land, mt_land, q_own, mt_own, send_sem, recv_sem = refs[4 * layers :]
+    gather_barrier()
+    copies = Copies(send_sem, recv_sem)
+    z = places()["z"]
+    quarter = pl.ds(pl.multiple_of(z * Q_COLS, 128), Q_COLS)
+    arrivals = []
+    for l in range(layers):
+        first = exchange_shards(copies, q_in[l], q_land.at[l])
+        arrivals.append((first, exchange_shards(copies, mt_in[l], mt_land.at[l])))
+    rings = []
+    for l in range(layers):
+        q = RingX(copies, q_own.at[l], attn[l], quarter, False)
+        m = RingX(copies, mt_own.at[l, :, pl.ds(0, M_COLS)], mlp[l], slice(None), True)
+        t = RingX(copies, mt_own.at[l, :, pl.ds(M_COLS, T_COLS)], attn[l], pl.ds(T_START, T_COLS), True)
+        rings.append((q, m, t, RingZ(copies, attn[l])))
+
+    def begin(l):
+        q, m, t, _ = rings[l]
+        for wait in arrivals[l][0]:
+            wait()
+        assemble(q_land.at[l], q_own.at[l])
+        q.start()
+        for wait in arrivals[l][1]:
+            wait()
+        assemble(mt_land.at[l], mt_own.at[l])
+        m.start()
+        t.start()
+
+    begin(0)
+    for l in range(layers):
+        q, m, t, along_z = rings[l]
+        q.forward()
+        q.finish()
+        q.close()
+        along_z.start()
+        m.forward()
+        t.forward()
+        if l + 1 < layers:
+            begin(l + 1)
+        along_z.forward()
+        m.finish()
+        t.finish()
+        along_z.finish()
+    for group in rings:
+        for ring in group[1:]:
+            ring.close()
+    copies.close()
+
+
+def shard_rows(qkv, out, up, down, vec, z):
+    width = out.shape[1]
+    role0 = jnp.concatenate([padded(qkv[:, :width], vec.T), padded(qkv[:, width : 2 * width])], 1)
+    role1 = jnp.concatenate([padded(qkv[:, 2 * width :]), padded(out)], 1)
+    attn = jnp.pad(jnp.stack([role0, role1]), ((0, 0), (0, TALL - ROWS), (0, 0)))
+    mlp = jnp.pad(jnp.stack([up, down]), ((0, 0), (0, TALL - ROWS), (0, 0)))
+    quarter = lax.dynamic_slice_in_dim(attn, z * Q_COLS, Q_COLS, 2)
+    return quarter, jnp.concatenate([mlp, attn[:, :, T_START:]], 2)
+
+
+def gather_layers(shards, collective):
+    layers = len(shards)
+    hbm = pl.BlockSpec(memory_space=pl.ANY)
+    shape = jax.ShapeDtypeStruct
+    results = pl.pallas_call(
+        functools.partial(gather_kernel, layers=layers),
+        out_shape=[shape((2, 4 * BLOCK, 2 * PADDED), BF16)] * layers
+        + [shape((2, 4 * BLOCK, M_COLS), BF16)] * layers,
+        in_specs=[hbm] * (2 * layers),
+        out_specs=[hbm] * (2 * layers),
+        scratch_shapes=[
+            pltpu.VMEM((layers, 4, TALL, Q_COLS), BF16),
+            pltpu.VMEM((layers, 4, TALL, M_COLS + T_COLS), BF16),
+            pltpu.VMEM((layers, BLOCK, Q_COLS), BF16),
+            pltpu.VMEM((layers, BLOCK, M_COLS + T_COLS), BF16),
+            pltpu.SemaphoreType.DMA((48 * layers,)),
+            pltpu.SemaphoreType.DMA((48 * layers,)),
+        ],
+        compiler_params=pltpu.CompilerParams(
+            collective_id=collective, has_side_effects=True, vmem_limit_bytes=32 * 2**20
+        ),
+    )(*[q for q, _ in shards], *[mt for _, mt in shards])
+    return list(zip(results[:layers], results[layers:]))
+
+
 def padded(matrix, extra=None):
     rows, width = matrix.shape
     parts = [matrix]
@@ -96,40 +347,6 @@
         width += extra.shape[1]
     parts.append(jnp.zeros((rows, PADDED - width), matrix.dtype))
     return jnp.concatenate(parts, 1)
-
-
-def gather_layer(at, qkv, out, up, down, vec):
-    width = out.shape[1]
-    rows = out.shape[0]
-    c0, y0 = at["c"] == 0, at["y"] == 0
-    role0 = jnp.concatenate([padded(qkv[:, :width], vec.T), padded(qkv[:, width : 2 * width])], 1)
-    role1 = jnp.concatenate([padded(qkv[:, 2 * width :]), padded(out)], 1)
-    start = attn_start(at["z"])
-    role0, role1 = columns(role0, start), columns(role1, start)
-
-    def two_level(a, b):
-        mine, give = jnp.where(c0, a, b), jnp.where(c0, b, a)
-        pair = pair_up(c0, mine, shifted(give, c=1))
-        return pair_up(y0, pair, shifted(pair, y=1))
-
-    own = two_level(role0, role1)
-    quarter = jnp.zeros((width, QUARTER), BF16)
-    for distance, piece in ring_gather("x", own).items():
-        quarter = lax.dynamic_update_slice(
-            quarter, piece, ((at["x"] + distance) % 4 * (4 * rows), 0)
-        )
-    attn = jnp.zeros((2, width, 2 * PADDED), BF16)
-    for distance, piece in ring_gather("z", quarter).items():
-        place = attn_start((at["z"] + distance) % 4)
-        attn = lax.dynamic_update_slice(attn, piece[None], (at["c"], 0, place))
-        attn = lax.dynamic_update_slice(attn, shifted(piece, c=1)[None], (1 - at["c"], 0, place))
-    own = two_level(up, down)
-    mlp = jnp.zeros((2, width, up.shape[1]), BF16)
-    for distance, piece in ring_gather("x", own).items():
-        place = (at["x"] + distance) % 4 * (4 * rows)
-        mlp = lax.dynamic_update_slice(mlp, piece[None], (at["c"], place, 0))
-        mlp = lax.dynamic_update_slice(mlp, shifted(piece, c=1)[None], (1 - at["c"], place, 0))
-    return attn, mlp
 
 
 def contract_rows(a, b):
@@ -446,10 +663,13 @@
     total_rows = micro_count * row_count
     at = places()
     bias = score_bias(segments)
-    weights = [
-        gather_layer(at, qkv_weight[l], out_weight[l], up_weight[l], down_weight[l], vectors[l])
-        for l in range(layers)
-    ]
+    weights = gather_layers(
+        [
+            shard_rows(qkv_weight[l], out_weight[l], up_weight[l], down_weight[l], vectors[l], at["z"])
+            for l in range(layers)
+        ],
+        3,
+    )
     wide = lambda row: jnp.pad(row, (0, PADDED - width))
     residual = tokens.reshape(total_rows, width).astype(F32)
     memory = []

time: 918 us -> 777 us (0.85)
  Pallas kernels: 116 us -> 270 us
  local copies, waits for them, and re-layouts: 214 us -> 74.5 us
  waiting for transfers between devices: 210 us -> 124 us
  starting transfers between devices: 126 us -> 93.2 us
  other arithmetic: 51.9 us -> 35.1 us
  matrix products: 163 us -> 147 us
    pallas_call x0 -> x1, Pallas kernels: none -> 161 us  [gather_layers(): pl.pallas_call(functools.partial(gather_kernel, layers=layers), out_shape...]
    ppermute x118 -> x70, waiting for transfers between devices: 210 us -> 124 us  [shifted(): return lax.ppermute(value, ('dp', 'ctx', 'tensor'), pairs)]
    dynamic_update_slice x34 -> x0, local copies, waits for them, and re-layouts: 53.1 us -> none  [the longest x8 16.6 us: gather_layer(): lax.dynamic_update_slice(mlp, shifted(piece, c=1)[None], (1 - at['c'], pl...]
    broadcast_in_dim x16 -> x0, local copies, waits for them, and re-layouts: 52.8 us -> none  [the longest x8 26.4 us: gather_layer(): attn = lax.dynamic_update_slice(attn, piece[None], (at['c'], 0, place))]
    ppermute x118 -> x70, starting transfers between devices: 126 us -> 93.2 us  [shifted(): return lax.ppermute(value, ('dp', 'ctx', 'tensor'), pairs)]
    another operation x14 -> x8, local copies, waits for them, and re-layouts: 20.6 us -> 0.26 us
    select_n x10 -> x0, other arithmetic: 10 us -> none  [the longest x6 8.26 us: pair_up(): jnp.where(first, jnp.concatenate([mine, other], 0), jnp.concatenate([othe...]
    dot_general x14, matrix products: 68.7 us -> 58.9 us  [dot(): return jnp.dot(a, b, preferred_element_type=F32)]
  transfers between devices with their start and end apart: 118 -> 70, of which waited for: 41 -> 27; matrix products, arithmetic and copies ran while one was open for 44% -> 26% of each run, Pallas kernels for 13% -> 11%
where the time goes in v2:
time: 777 us; the launch traced here: 766 us
  Pallas kernels  270 us (35%)
  matrix products  147 us (19%)
  waiting for transfers between devices  124 us (16%)
  starting transfers between devices  93.2 us (12%)
  local copies, waits for them, and re-layouts  74.5 us (10%)
  other arithmetic  35.1 us (5%)
  blocking collectives  18.4 us (2%)
    pallas_call x1, Pallas kernels, gather_layers(): pl.pallas_call(functools.partial(gather_kernel, layers=layers), out_shape...  161 us
    ppermute x70, waiting for transfers between devices, shifted(): return lax.ppermute(value, ('dp', 'ctx', 'tensor'), pairs)  124 us
    ppermute x70, starting transfers between devices, shifted(): return lax.ppermute(value, ('dp', 'ctx', 'tensor'), pairs)  93.2 us
    pallas_call x2, Pallas kernels, attend_back(): pl.pallas_call(attend_back_kernel, out_shape=(shape((128, PADDED), BF16),...  59.1 us
    dot_general x14, matrix products, dot(): return jnp.dot(a, b, preferred_element_type=F32)  58.9 us
    pallas_call x2, Pallas kernels, attend(): pl.pallas_call(attend_kernel, out_shape=(shape((128, PADDED), BF16), shap...  49.6 us
    dot_general x14, matrix products, contract_cols(): lax.dot_general(a, b, (((1,), (1,)), ((), ())), preferred_element_type=F32)  47 us
    dot_general x8, matrix products, contract_rows(): lax.dot_general(a, b, (((0,), (0,)), ((), ())), preferred_element_type=F32)  41.3 us
  transfers between devices with their start and end apart: 70, of which 27 were waited for; matrix products, arithmetic and copies ran while one was open for 26% of the time, Pallas kernels for 11%

profile of v2, /device:TPU:0, one launch (start us, length us, event | category | flops | bytes accessed | tf_op | source)
XLA Modules:
  0.0 765.8 jit_solution(16595035355554779033)
XLA Ops:
  0.6 3.0 fusion.271
  11.6 161.1 %shard_map.135 = (bf16[2,1088,2304]{2,1,0:T(8,128)(2,1)}, bf16[2,1088,2304]{2,1,0:T(8,128)(2,1)}, bf16[2,1088,2176]{2,1,0:T(8,128)(2,1)S(1)}, bf16[2,1088,2176]{2,1,0:T(8,128)(2,1)S(1)}) custom-call(bf16[2,80,512]{2,1,0:T(8,128)(2,1)S(1)} %constant_dynamic-slice_fusion.34.refs_0_, bf16[2,80,512]{2,1,0:T(8,128)(2,1)S(1)} %constant_dynamic-slice_fusion.33.refs_1_, ...), custom_call_target="tpu_custom_call" | custom-call | tf_op jit(solution)/shard_map/pallas_call | solution.py:321
  172.7 3.6 copy-done.16
  176.4 3.6 copy-done.17
  184.0 3.4 fusion.10
  189.9 18.4 %all-gather = bf16[8,64,2]{1,2,0:T(2,128)(2,1)S(1)} all-gather(bf16[1,64,2]{1,2,0:T(2,128)(2,1)S(1)} %convert_bitcast_fusion.2), channel_id=1, replica_groups=mesh['dp'=16,'ctx'=4,'tensor'=2] {'ctx','tensor'}, dimensions={0}, use_global_device_ids=true | all-gather | bytes 2304 | tf_op jit(solution)/shard_map/all_gather | solution.py:637
  208.7 24.8 %shard_map.136 = (bf16[128,1152]{1,0:T(8,128)(2,1)S(1)}, bf16[512,384]{1,0:T(8,128)(2,1)S(1)}, bf16[512,384]{1,0:T(8,128)(2,1)S(1)}, bf16[512,384]{1,0:T(8,128)(...) custom-call(bf16[128,1152]{1,0:T(8,128)(2,1)S(1)} %fusion.217.q, bf16[128,1152]{1,0:T(8,128)(2,1)S(1)} %slice.841.k, ...), custom_call_target="tpu_custom_call" | custom-call | tf_op jit(solution)/shard_map/pallas_call | solution.py:540
  233.5 2.9 fusion.278
  240.4 6.5 multiply_convert_fusion.3
  246.9 6.3 multiply_convert_fusion.2
  262.9 4.3 fusion.270
  267.7 3.5 fusion.6
  274.1 24.9 %shard_map.137 = (bf16[128,1152]{1,0:T(8,128)(2,1)S(1)}, bf16[512,384]{1,0:T(8,128)(2,1)S(1)}, bf16[512,384]{1,0:T(8,128)(2,1)S(1)}, bf16[512,384]{1,0:T(8,128)(...) custom-call(bf16[128,1152]{1,0:T(8,128)(2,1)S(1)} %fusion.216.q, bf16[128,1152]{1,0:T(8,128)(2,1)S(1)} %slice.840.k, ...), custom_call_target="tpu_custom_call" | custom-call | tf_op jit(solution)/shard_map/pallas_call | solution.py:540
  304.0 3.7 multiply_convert_fusion.1
  307.7 4.4 add_convert_fusion.17
  313.2 3.8 multiply_convert_fusion
  322.4 5.8 add_convert_fusion.16
  329.0 4.5 fusion.100
  338.7 5.7 convolution_convert_fusion
  344.9 4.4 multiply_reduce_fusion
  349.3 3.6 fusion.269
  354.5 3.2 fusion.109
  363.5 30.3 %shard_map.138 = (bf16[128,1152]{1,0:T(8,128)(2,1)S(1)}, bf16[128,1152]{1,0:T(8,128)(2,1)S(1)}, bf16[128,1152]{1,0:T(8,128)(2,1)S(1)}) custom-call(bf16[128,1152]{1,0:T(8,128)(2,1)S(1)} %pad.63.do, bf16[512,384]{1,0:T(8,128)(2,1)S(1)} %get-tuple-element.35.q_all, bf16[512,384]{1,0:T(8,128)(2,1)S(1)} %copy-done.7, bf16[512,384]{1,0:T(8,128)(2,1)S(1)} %copy-done.9, ...), custom_call_target="tpu_custom_call" | custom-call | tf_op jit(solution)/shard_map/pallas_call | solution.py:617
  394.7 4.3 fusion.4
  400.2 2.9 multiply_reduce_fusion.1
  406.4 5.3 add_convert_fusion.15
  413.5 5.3 fusion.1
  418.8 5.6 add_convert_fusion.14
  431.9 5.7 convolution_convert_fusion.1
  438.9 4.8 multiply_reduce_fusion.2
  452.3 28.8 %shard_map.139 = (bf16[128,1152]{1,0:T(8,128)(2,1)S(1)}, bf16[128,1152]{1,0:T(8,128)(2,1)S(1)}, bf16[128,1152]{1,0:T(8,128)(2,1)S(1)}) custom-call(bf16[128,1152]{1,0:T(8,128)(2,1)S(1)} %pad.64.do, bf16[512,384]{1,0:T(8,128)(2,1)S(1)} %copy-done.1, bf16[512,384]{1,0:T(8,128)(2,1)S(1)} %copy-done.3, bf16[512,384]{1,0:T(8,128)(2,1)S(1)} %copy-done.5, ...), custom_call_target="tpu_custom_call" | custom-call | tf_op jit(solution)/shard_map/pallas_call | solution.py:617
  481.1 4.3 fusion.8
  491.4 5.2 fusion
  498.3 4.2 fusion.3
  506.1 4.2 fusion.2
  510.6 3.2 collective-permute-start.43
  513.8 5.4 add_convert_fusion
  520.4 3.0 collective-permute-start.27
  525.1 5.6 add_convert_fusion.1
  535.0 3.2 collective-permute-done.25
  541.2 17.0 %collective-permute-done.57 = bf16[272,2176]{1,0:T(8,128)(2,1)S(1)} collective-permute-done((bf16[272,2176]{1,0:T(8,128)(2,1)S(1)}, bf16[272,2176]{1,0:T(8,128)(2,1)S(1)}, u32[]{:S(2)}, u32[]{:S(2)}) %collective-permute-start.57) | collective-permute-done | bytes 1183776 | tf_op jit(solution)/shard_map/ppermute | solution.py:41
  564.5 31.3 %collective-permute-done.60 = bf16[136,640]{1,0:T(8,128)(2,1)S(1)} collective-permute-done((bf16[136,640]{1,0:T(8,128)(2,1)S(1)}, bf16[136,640]{1,0:T(8,128)(2,1)S(1)}, u32[]{:S(2)}, u32[]{:S(2)}) %collective-permute-start.60) | collective-permute-done | bytes 174112 | tf_op jit(solution)/shard_map/ppermute | solution.py:41
  596.1 3.3 collective-permute-start.63
  599.6 5.1 collective-permute-done.61
  607.0 3.2 collective-permute-start.64
  614.0 3.6 collective-permute-start.47
  617.7 22.8 %collective-permute-done.45 = bf16[136,640]{1,0:T(8,128)(2,1)S(1)} collective-permute-done((bf16[136,640]{1,0:T(8,128)(2,1)S(1)}, bf16[136,640]{1,0:T(8,128)(2,1)S(1)}, u32[]{:S(2)}, u32[]{:S(2)}) %collective-permute-start.45) | collective-permute-done | bytes 174112 | tf_op jit(solution)/shard_map/ppermute | solution.py:41
  644.0 3.2 collective-permute-start.48
  649.2 3.3 collective-permute-start.68
  658.5 3.1 collective-permute-done.29
  662.5 3.2 collective-permute-start.49
  666.3 4.7 collective-permute-done.49
  681.2 3.2 collective-permute-start.33
  684.4 5.3 collective-permute-done.12
  693.8 3.3 collective-permute-start.53
  704.7 3.1 collective-permute-start.16
  708.7 3.3 collective-permute-start.36
  721.3 3.2 collective-permute-start.38
  728.1 3.7 collective-permute-start.17
  732.1 3.3 collective-permute-done.17
  737.0 4.0 collective-permute-done.18
  741.1 3.2 collective-permute-start.20
  748.0 3.3 collective-permute-start.22
  762.4 2.9 copy.209
  (581 shorter events, 179.9 us)
Async XLA Ops:
  236.8 10.0 %collective-permute-start = (bf16[128,1088]{1,0:T(8,128)(2,1)S(1)}, bf16[128,1088]{1,0:T(8,128)(2,1)S(1)}, u32[]{:S(2)}, u32[]{:S(2)}) collective-permute-start(bf16[128,1088]{1,0:T(8,128)(2,1)S(1)} %add_convert_fusion.25), channel_id=1, source_target_pairs={{0,1},{1,0},{2,3},{3,2},{4,5},{5,4},{6,7},{7,6},{8,9},{9,8},{10,11... | collective-permute-start | bytes 835592 | tf_op jit(solution)/shard_map/ppermute | solution.py:41
  238.8 83.6 %collective-permute-start.4 = (bf16[128,1088]{1,0:T(8,128)(2,1)}, bf16[128,1088]{1,0:T(8,128)(2,1)}, u32[]{:S(2)}, u32[]{:S(2)}) collective-permute-start(bf16[128,1088]{1,0:T(8,128)(2,1)} %get-tuple-element.213), channel_id=1, source_target_pairs={{0,1},{1,0},{2,3},{3,2},{4,5},{5,4},{6,7},{7,6},{8,9},{9,8},{10,11... | collective-permute-start | bytes 835592 | tf_op jit(solution)/shard_map/ppermute | solution.py:41
  255.5 7.4 collective-permute-start.1
  302.2 11.0 %collective-permute-start.2 = (bf16[128,1088]{1,0:T(8,128)(2,1)S(1)}, bf16[128,1088]{1,0:T(8,128)(2,1)S(1)}, u32[]{:S(2)}, u32[]{:S(2)}) collective-permute-start(bf16[128,1088]{1,0:T(8,128)(2,1)S(1)} %add_convert_fusion.23), channel_id=1, source_target_pairs={{0,1},{1,0},{2,3},{3,2},{4,5},{5,4},{6,7},{7,6},{8,9},{9,8},{10,11... | collective-permute-start | bytes 835592 | tf_op jit(solution)/shard_map/ppermute | solution.py:41
  321.7 27.5 %collective-permute-start.3 = (bf16[128,1088]{1,0:T(8,128)(2,1)}, bf16[128,1088]{1,0:T(8,128)(2,1)}, u32[]{:S(2)}, u32[]{:S(2)}) collective-permute-start(bf16[128,1088]{1,0:T(8,128)(2,1)} %copy.181), channel_id=1, source_target_pairs={{0,1},{1,0},{2,3},{3,2},{4,5},{5,4},{6,7},{7,6},{8,9},{9,8},{10,11... | collective-permute-start | bytes 835592 | tf_op jit(solution)/shard_map/ppermute | solution.py:41
  335.3 9.6 %collective-permute-start.5 = (bf16[128,1088]{1,0:T(8,128)(2,1)}, bf16[128,1088]{1,0:T(8,128)(2,1)}, u32[]{:S(2)}, u32[]{:S(2)}) collective-permute-start(bf16[128,1088]{1,0:T(8,128)(2,1)} %copy.183), channel_id=1, source_target_pairs={{0,1},{1,0},{2,3},{3,2},{4,5},{5,4},{6,7},{7,6},{8,9},{9,8},{10,11... | collective-permute-start | bytes 835592 | tf_op jit(solution)/shard_map/ppermute | solution.py:41
  344.4 153.8 %collective-permute-start.55 = (bf16[1088,2176]{1,0:T(8,128)(2,1)}, bf16[1088,2176]{1,0:T(8,128)(2,1)}, u32[]{:S(2)}, u32[]{:S(2)}) collective-permute-start(bf16[1088,2176]{1,0:T(8,128)(2,1)} %convolution_convert_fusion), channel_id=1, source_target_pairs={{0,8},{1,9},{2,10},{3,11},{4,12},{5,13},{6,14},{7,15},{8,0},{9,1},... | collective-permute-start | bytes 14204936 | tf_op jit(solution)/shard_map/ppermute | solution.py:41
  405.0 13.8 %collective-permute-start.6 = (bf16[128,1088]{1,0:T(8,128)(2,1)}, bf16[128,1088]{1,0:T(8,128)(2,1)}, u32[]{:S(2)}, u32[]{:S(2)}) collective-permute-start(bf16[128,1088]{1,0:T(8,128)(2,1)} %get-tuple-element.115), channel_id=1, source_target_pairs={{0,1},{1,0},{2,3},{3,2},{4,5},{5,4},{6,7},{7,6},{8,9},{9,8},{10,11... | collective-permute-start | bytes 835592 | tf_op jit(solution)/shard_map/ppermute | solution.py:41
  418.8 91.8 %collective-permute-start.24 = (bf16[1088,2304]{1,0:T(8,128)(2,1)}, bf16[1088,2304]{1,0:T(8,128)(2,1)}, u32[]{:S(2)}, u32[]{:S(2)}) collective-permute-start(bf16[1088,2304]{1,0:T(8,128)(2,1)} %fusion.1), channel_id=1, source_target_pairs={{0,8},{1,9},{2,10},{3,11},{4,12},{5,13},{6,14},{7,15},{8,0},{9,1},... | collective-permute-start | bytes 15040520 | tf_op jit(solution)/shard_map/ppermute | solution.py:41
  429.2 9.7 %collective-permute-start.7 = (bf16[128,1088]{1,0:T(8,128)(2,1)}, bf16[128,1088]{1,0:T(8,128)(2,1)}, u32[]{:S(2)}, u32[]{:S(2)}) collective-permute-start(bf16[128,1088]{1,0:T(8,128)(2,1)} %copy.188), channel_id=1, source_target_pairs={{0,1},{1,0},{2,3},{3,2},{4,5},{5,4},{6,7},{7,6},{8,9},{9,8},{10,11... | collective-permute-start | bytes 835592 | tf_op jit(solution)/shard_map/ppermute | solution.py:41
  437.6 68.4 %collective-permute-start.40 = (bf16[1088,2176]{1,0:T(8,128)(2,1)}, bf16[1088,2176]{1,0:T(8,128)(2,1)}, u32[]{:S(2)}, u32[]{:S(2)}) collective-permute-start(bf16[1088,2176]{1,0:T(8,128)(2,1)} %convolution_convert_fusion.1), channel_id=1, source_target_pairs={{0,8},{1,9},{2,10},{3,11},{4,12},{5,13},{6,14},{7,15},{8,0},{9,1},... | collective-permute-start | bytes 14204936 | tf_op jit(solution)/shard_map/ppermute | solution.py:41
  496.6 27.4 %collective-permute-start.8 = (bf16[1088,2304]{1,0:T(8,128)(2,1)}, bf16[1088,2304]{1,0:T(8,128)(2,1)}, u32[]{:S(2)}, u32[]{:S(2)}) collective-permute-start(bf16[1088,2304]{1,0:T(8,128)(2,1)} %fusion), channel_id=1, source_target_pairs={{0,8},{1,9},{2,10},{3,11},{4,12},{5,13},{6,14},{7,15},{8,0},{9,1},... | collective-permute-start | bytes 15040520 | tf_op jit(solution)/shard_map/ppermute | solution.py:41
  502.7 17.4 %collective-permute-start.56 = (bf16[136,2176]{1,0:T(8,128)(2,1)S(1)}, bf16[136,2176]{1,0:T(8,128)(2,1)S(1)}, u32[]{:S(2)}, u32[]{:S(2)}) collective-permute-start(bf16[136,2176]{1,0:T(8,128)(2,1)S(1)} %get-tuple-element.152), channel_id=1, source_target_pairs={{0,32},{1,33},{2,34},{3,35},{4,36},{5,37},{6,38},{7,39},{8,40},{9,... | collective-permute-start | bytes 1775624 | tf_op jit(solution)/shard_map/ppermute | solution.py:41
  503.9 16.4 %collective-permute-start.58 = (bf16[136,2176]{1,0:T(8,128)(2,1)S(1)}, bf16[136,2176]{1,0:T(8,128)(2,1)S(1)}, u32[]{:S(2)}, u32[]{:S(2)}) collective-permute-start(bf16[136,2176]{1,0:T(8,128)(2,1)S(1)} %get-tuple-element.154), channel_id=1, source_target_pairs={{0,96},{1,97},{2,98},{3,99},{4,100},{5,101},{6,102},{7,103},{8,104... | collective-permute-start | bytes 1775624 | tf_op jit(solution)/shard_map/ppermute | solution.py:41
  510.5 22.4 %collective-permute-start.41 = (bf16[136,2176]{1,0:T(8,128)(2,1)S(1)}, bf16[136,2176]{1,0:T(8,128)(2,1)S(1)}, u32[]{:S(2)}, u32[]{:S(2)}) collective-permute-start(bf16[136,2176]{1,0:T(8,128)(2,1)S(1)} %get-tuple-element.146), channel_id=1, source_target_pairs={{0,32},{1,33},{2,34},{3,35},{4,36},{5,37},{6,38},{7,39},{8,40},{9,... | collective-permute-start | bytes 1775624 | tf_op jit(solution)/shard_map/ppermute | solution.py:41
  510.6 22.6 %collective-permute-start.43 = (bf16[136,2176]{1,0:T(8,128)(2,1)S(1)}, bf16[136,2176]{1,0:T(8,128)(2,1)S(1)}, u32[]{:S(2)}, u32[]{:S(2)}) collective-permute-start(bf16[136,2176]{1,0:T(8,128)(2,1)S(1)} %get-tuple-element.148), channel_id=1, source_target_pairs={{0,96},{1,97},{2,98},{3,99},{4,100},{5,101},{6,102},{7,103},{8,104... | collective-permute-start | bytes 1775624 | tf_op jit(solution)/shard_map/ppermute | solution.py:41
  520.2 18.0 %collective-permute-start.25 = (bf16[544,640]{1,0:T(8,128)(2,1)S(1)}, bf16[544,640]{1,0:T(8,128)(2,1)S(1)}, u32[]{:S(2)}, u32[]{:S(2)}) collective-permute-start(bf16[544,640]{1,0:T(8,128)(2,1)S(1)} %get-tuple-element.140), channel_id=1, source_target_pairs={{0,2},{1,3},{2,4},{3,5},{4,6},{5,7},{6,0},{7,1},{8,10},{9,11},{10,... | collective-permute-start | bytes 2088968 | tf_op jit(solution)/shard_map/ppermute | solution.py:41
  520.4 19.1 %collective-permute-start.27 = (bf16[544,640]{1,0:T(8,128)(2,1)S(1)}, bf16[544,640]{1,0:T(8,128)(2,1)}, u32[]{:S(2)}, u32[]{:S(2)}) collective-permute-start(bf16[544,640]{1,0:T(8,128)(2,1)S(1)} %get-tuple-element.142), channel_id=1, source_target_pairs={{0,6},{1,7},{2,0},{3,1},{4,2},{5,3},{6,4},{7,5},{8,14},{9,15},{10,... | collective-permute-start | bytes 2088968 | tf_op jit(solution)/shard_map/ppermute | solution.py:41
  524.0 34.3 %collective-permute-start.57 = (bf16[272,2176]{1,0:T(8,128)(2,1)S(1)}, bf16[272,2176]{1,0:T(8,128)(2,1)S(1)}, u32[]{:S(2)}, u32[]{:S(2)}) collective-permute-start(bf16[272,2176]{1,0:T(8,128)(2,1)S(1)} %pad_maximum_fusion.6), channel_id=1, source_target_pairs={{0,32},{1,33},{2,34},{3,35},{4,36},{5,37},{6,38},{7,39},{8,40},{9,... | collective-permute-start | bytes 3551240 | tf_op jit(solution)/shard_map/ppermute | solution.py:41
  532.9 27.2 %collective-permute-start.59 = (bf16[272,2176]{1,0:T(8,128)(2,1)S(1)}, bf16[272,2176]{1,0:T(8,128)(2,1)S(1)}, u32[]{:S(2)}, u32[]{:S(2)}) collective-permute-start(bf16[272,2176]{1,0:T(8,128)(2,1)S(1)} %pad_maximum_fusion.7), channel_id=1, source_target_pairs={{0,96},{1,97},{2,98},{3,99},{4,100},{5,101},{6,102},{7,103},{8,104... | collective-permute-start | bytes 3551240 | tf_op jit(solution)/shard_map/ppermute | solution.py:41
  533.2 27.6 %collective-permute-start.11 = (bf16[544,640]{1,0:T(8,128)(2,1)S(1)}, bf16[544,640]{1,0:T(8,128)(2,1)S(1)}, u32[]{:S(2)}, u32[]{:S(2)}) collective-permute-start(bf16[544,640]{1,0:T(8,128)(2,1)S(1)} %get-tuple-element.136), channel_id=1, source_target_pairs={{0,6},{1,7},{2,0},{3,1},{4,2},{5,3},{6,4},{7,5},{8,14},{9,15},{10,... | collective-permute-start | bytes 2088968 | tf_op jit(solution)/shard_map/ppermute | solution.py:41
  538.2 24.4 %collective-permute-start.9 = (bf16[544,640]{1,0:T(8,128)(2,1)S(1)}, bf16[544,640]{1,0:T(8,128)(2,1)S(1)}, u32[]{:S(2)}, u32[]{:S(2)}) collective-permute-start(bf16[544,640]{1,0:T(8,128)(2,1)S(1)} %get-tuple-element.134), channel_id=1, source_target_pairs={{0,2},{1,3},{2,4},{3,5},{4,6},{5,7},{6,0},{7,1},{8,10},{9,11},{10,... | collective-permute-start | bytes 2088968 | tf_op jit(solution)/shard_map/ppermute | solution.py:41
  539.5 67.5 %collective-permute-start.42 = (bf16[272,2176]{1,0:T(8,128)(2,1)S(1)}, bf16[272,2176]{1,0:T(8,128)(2,1)S(1)}, u32[]{:S(2)}, u32[]{:S(2)}) collective-permute-start(bf16[272,2176]{1,0:T(8,128)(2,1)S(1)} %pad_maximum_fusion.4), channel_id=1, source_target_pairs={{0,32},{1,33},{2,34},{3,35},{4,36},{5,37},{6,38},{7,39},{8,40},{9,... | collective-permute-start | bytes 3551240 | tf_op jit(solution)/shard_map/ppermute | solution.py:41
  558.2 51.9 %collective-permute-start.44 = (bf16[272,2176]{1,0:T(8,128)(2,1)S(1)}, bf16[272,2176]{1,0:T(8,128)(2,1)S(1)}, u32[]{:S(2)}, u32[]{:S(2)}) collective-permute-start(bf16[272,2176]{1,0:T(8,128)(2,1)S(1)} %pad_maximum_fusion.5), channel_id=1, source_target_pairs={{0,96},{1,97},{2,98},{3,99},{4,100},{5,101},{6,102},{7,103},{8,104... | collective-permute-start | bytes 3551240 | tf_op jit(solution)/shard_map/ppermute | solution.py:41
  560.1 83.8 %collective-permute-start.26 = (bf16[1088,640]{1,0:T(8,128)(2,1)S(1)}, bf16[1088,640]{1,0:T(8,128)(2,1)S(1)}, u32[]{:S(2)}, u32[]{:S(2)}) collective-permute-start(bf16[1088,640]{1,0:T(8,128)(2,1)S(1)} %pad_maximum_fusion.2), channel_id=1, source_target_pairs={{0,2},{1,3},{2,4},{3,5},{4,6},{5,7},{6,0},{7,1},{8,10},{9,11},{10,... | collective-permute-start | bytes 4177928 | tf_op jit(solution)/shard_map/ppermute | solution.py:41
  560.8 35.0 %collective-permute-start.60 = (bf16[136,640]{1,0:T(8,128)(2,1)S(1)}, bf16[136,640]{1,0:T(8,128)(2,1)S(1)}, u32[]{:S(2)}, u32[]{:S(2)}) collective-permute-start(bf16[136,640]{1,0:T(8,128)(2,1)S(1)} %get-tuple-element.180), channel_id=1, source_target_pairs={{0,2},{1,3},{2,4},{3,5},{4,6},{5,7},{6,0},{7,1},{8,10},{9,11},{10,... | collective-permute-start | bytes 522248 | tf_op jit(solution)/shard_map/ppermute | solution.py:41
  562.5 33.3 %collective-permute-start.62 = (bf16[136,640]{1,0:T(8,128)(2,1)S(1)}, bf16[136,640]{1,0:T(8,128)(2,1)S(1)}, u32[]{:S(2)}, u32[]{:S(2)}) collective-permute-start(bf16[136,640]{1,0:T(8,128)(2,1)S(1)} %get-tuple-element.182), channel_id=1, source_target_pairs={{0,6},{1,7},{2,0},{3,1},{4,2},{5,3},{6,4},{7,5},{8,14},{9,15},{10,... | collective-permute-start | bytes 522248 | tf_op jit(solution)/shard_map/ppermute | solution.py:41
  596.0 8.8 %collective-permute-start.61 = (bf16[272,640]{1,0:T(8,128)(2,1)S(1)}, bf16[272,640]{1,0:T(8,128)(2,1)S(1)}, u32[]{:S(2)}, u32[]{:S(2)}) collective-permute-start(bf16[272,640]{1,0:T(8,128)(2,1)S(1)} %pad_maximum_fusion.44), channel_id=1, source_target_pairs={{0,2},{1,3},{2,4},{3,5},{4,6},{5,7},{6,0},{7,1},{8,10},{9,11},{10,... | collective-permute-start | bytes 1044488 | tf_op jit(solution)/shard_map/ppermute | solution.py:41
  596.1 10.6 %collective-permute-start.63 = (bf16[272,640]{1,0:T(8,128)(2,1)S(1)}, bf16[272,640]{1,0:T(8,128)(2,1)S(1)}, u32[]{:S(2)}, u32[]{:S(2)}) collective-permute-start(bf16[272,640]{1,0:T(8,128)(2,1)S(1)} %pad_maximum_fusion.45), channel_id=1, source_target_pairs={{0,6},{1,7},{2,0},{3,1},{4,2},{5,3},{6,4},{7,5},{8,14},{9,15},{10,... | collective-permute-start | bytes 1044488 | tf_op jit(solution)/shard_map/ppermute | solution.py:41
  604.7 39.3 %collective-permute-start.28 = (bf16[1088,640]{1,0:T(8,128)(2,1)S(1)}, bf16[1088,640]{1,0:T(8,128)(2,1)S(1)}, u32[]{:S(2)}, u32[]{:S(2)}) collective-permute-start(bf16[1088,640]{1,0:T(8,128)(2,1)S(1)} %pad_maximum_fusion.3), channel_id=1, source_target_pairs={{0,6},{1,7},{2,0},{3,1},{4,2},{5,3},{6,4},{7,5},{8,14},{9,15},{10,... | collective-permute-start | bytes 4177928 | tf_op jit(solution)/shard_map/ppermute | solution.py:41
  606.7 77.6 %collective-permute-start.10 = (bf16[1088,640]{1,0:T(8,128)(2,1)S(1)}, bf16[1088,640]{1,0:T(8,128)(2,1)S(1)}, u32[]{:S(2)}, u32[]{:S(2)}) collective-permute-start(bf16[1088,640]{1,0:T(8,128)(2,1)S(1)} %pad_maximum_fusion), channel_id=1, source_target_pairs={{0,2},{1,3},{2,4},{3,5},{4,6},{5,7},{6,0},{7,1},{8,10},{9,11},{10,... | collective-permute-start | bytes 4177928 | tf_op jit(solution)/shard_map/ppermute | solution.py:41
  607.0 7.0 collective-permute-start.64
  610.7 29.8 %collective-permute-start.45 = (bf16[136,640]{1,0:T(8,128)(2,1)S(1)}, bf16[136,640]{1,0:T(8,128)(2,1)S(1)}, u32[]{:S(2)}, u32[]{:S(2)}) collective-permute-start(bf16[136,640]{1,0:T(8,128)(2,1)S(1)} %get-tuple-element.174), channel_id=1, source_target_pairs={{0,2},{1,3},{2,4},{3,5},{4,6},{5,7},{6,0},{7,1},{8,10},{9,11},{10,... | collective-permute-start | bytes 522248 | tf_op jit(solution)/shard_map/ppermute | solution.py:41
  614.0 27.1 %collective-permute-start.47 = (bf16[136,640]{1,0:T(8,128)(2,1)S(1)}, bf16[136,640]{1,0:T(8,128)(2,1)S(1)}, u32[]{:S(2)}, u32[]{:S(2)}) collective-permute-start(bf16[136,640]{1,0:T(8,128)(2,1)S(1)} %get-tuple-element.176), channel_id=1, source_target_pairs={{0,6},{1,7},{2,0},{3,1},{4,2},{5,3},{6,4},{7,5},{8,14},{9,15},{10,... | collective-permute-start | bytes 522248 | tf_op jit(solution)/shard_map/ppermute | solution.py:41
  640.5 8.6 %collective-permute-start.65 = (bf16[136,640]{1,0:T(8,128)(2,1)S(1)}, bf16[136,640]{1,0:T(8,128)(2,1)S(1)}, u32[]{:S(2)}, u32[]{:S(2)}) collective-permute-start(bf16[136,640]{1,0:T(8,128)(2,1)S(1)} %get-tuple-element.111), channel_id=1, source_target_pairs={{0,2},{1,3},{2,4},{3,5},{4,6},{5,7},{6,0},{7,1},{8,10},{9,11},{10,... | collective-permute-start | bytes 522248 | tf_op jit(solution)/shard_map/ppermute | solution.py:41
  641.0 8.1 %collective-permute-start.66 = (bf16[136,640]{1,0:T(8,128)(2,1)S(1)}, bf16[136,640]{1,0:T(8,128)(2,1)S(1)}, u32[]{:S(2)}, u32[]{:S(2)}) collective-permute-start(bf16[136,640]{1,0:T(8,128)(2,1)S(1)} %get-tuple-element.111), channel_id=1, source_target_pairs={{0,6},{1,7},{2,0},{3,1},{4,2},{5,3},{6,4},{7,5},{8,14},{9,15},{10,... | collective-permute-start | bytes 522248 | tf_op jit(solution)/shard_map/ppermute | solution.py:41
  643.9 18.4 %collective-permute-start.46 = (bf16[272,640]{1,0:T(8,128)(2,1)S(1)}, bf16[272,640]{1,0:T(8,128)(2,1)S(1)}, u32[]{:S(2)}, u32[]{:S(2)}) collective-permute-start(bf16[272,640]{1,0:T(8,128)(2,1)S(1)} %pad_maximum_fusion.42), channel_id=1, source_target_pairs={{0,2},{1,3},{2,4},{3,5},{4,6},{5,7},{6,0},{7,1},{8,10},{9,11},{10,... | collective-permute-start | bytes 1044488 | tf_op jit(solution)/shard_map/ppermute | solution.py:41
  644.0 18.3 %collective-permute-start.48 = (bf16[272,640]{1,0:T(8,128)(2,1)S(1)}, bf16[272,640]{1,0:T(8,128)(2,1)S(1)}, u32[]{:S(2)}, u32[]{:S(2)}) collective-permute-start(bf16[272,640]{1,0:T(8,128)(2,1)S(1)} %pad_maximum_fusion.43), channel_id=1, source_target_pairs={{0,6},{1,7},{2,0},{3,1},{4,2},{5,3},{6,4},{7,5},{8,14},{9,15},{10,... | collective-permute-start | bytes 1044488 | tf_op jit(solution)/shard_map/ppermute | solution.py:41
  649.1 5.8 collective-permute-start.67
  649.2 7.4 collective-permute-start.68
  654.9 6.6 collective-permute-start.29
  661.6 28.1 %collective-permute-start.12 = (bf16[1088,640]{1,0:T(8,128)(2,1)S(1)}, bf16[1088,640]{1,0:T(8,128)(2,1)S(1)}, u32[]{:S(2)}, u32[]{:S(2)}) collective-permute-start(bf16[1088,640]{1,0:T(8,128)(2,1)S(1)} %pad_maximum_fusion.1), channel_id=1, source_target_pairs={{0,6},{1,7},{2,0},{3,1},{4,2},{5,3},{6,4},{7,5},{8,14},{9,15},{10,... | collective-permute-start | bytes 4177928 | tf_op jit(solution)/shard_map/ppermute | solution.py:41
  662.2 11.6 %collective-permute-start.69 = (bf16[68,2176]{1,0:T(8,128)(2,1)S(1)}, bf16[68,2176]{1,0:T(8,128)(2,1)S(1)}, u32[]{:S(2)}, u32[]{:S(2)}) collective-permute-start(bf16[68,2176]{1,0:T(8,128)(2,1)S(1)} %constant_dynamic-slice_fusion.9), channel_id=1, source_target_pairs={{0,8},{1,9},{2,10},{3,11},{4,12},{5,13},{6,14},{7,15},{8,0},{9,1},... | collective-permute-start | bytes 887816 | tf_op jit(solution)/shard_map/ppermute | solution.py:41
  662.5 8.4 %collective-permute-start.49 = (bf16[136,640]{1,0:T(8,128)(2,1)S(1)}, bf16[136,640]{1,0:T(8,128)(2,1)S(1)}, u32[]{:S(2)}, u32[]{:S(2)}) collective-permute-start(bf16[136,640]{1,0:T(8,128)(2,1)S(1)} %constant_dynamic-slice_fusion.16), channel_id=1, source_target_pairs={{0,16},{1,17},{2,18},{3,19},{4,20},{5,21},{6,22},{7,23},{8,24},{9,... | collective-permute-start | bytes 522248 | tf_op jit(solution)/shard_map/ppermute | solution.py:41
  665.8 11.6 %collective-permute-start.30 = (bf16[272,640]{1,0:T(8,128)(2,1)S(1)}, bf16[272,640]{1,0:T(8,128)(2,1)S(1)}, u32[]{:S(2)}, u32[]{:S(2)}) collective-permute-start(bf16[272,640]{1,0:T(8,128)(2,1)S(1)} %pad_maximum_fusion.40), channel_id=1, source_target_pairs={{0,32},{1,33},{2,34},{3,35},{4,36},{5,37},{6,38},{7,39},{8,40},{9,... | collective-permute-start | bytes 1044488 | tf_op jit(solution)/shard_map/ppermute | solution.py:41
  671.0 10.1 %collective-permute-start.32 = (bf16[272,640]{1,0:T(8,128)(2,1)S(1)}, bf16[272,640]{1,0:T(8,128)(2,1)S(1)}, u32[]{:S(2)}, u32[]{:S(2)}) collective-permute-start(bf16[272,640]{1,0:T(8,128)(2,1)S(1)} %pad_maximum_fusion.41), channel_id=1, source_target_pairs={{0,96},{1,97},{2,98},{3,99},{4,100},{5,101},{6,102},{7,103},{8,104... | collective-permute-start | bytes 1044488 | tf_op jit(solution)/shard_map/ppermute | solution.py:41
  673.8 19.8 %collective-permute-start.50 = (bf16[136,640]{1,0:T(8,128)(2,1)S(1)}, bf16[136,640]{1,0:T(8,128)(2,1)S(1)}, u32[]{:S(2)}, u32[]{:S(2)}) collective-permute-start(bf16[136,640]{1,0:T(8,128)(2,1)S(1)} %get-tuple-element.109), channel_id=1, source_target_pairs={{0,2},{1,3},{2,4},{3,5},{4,6},{5,7},{6,0},{7,1},{8,10},{9,11},{10,... | collective-permute-start | bytes 522248 | tf_op jit(solution)/shard_map/ppermute | solution.py:41
  677.4 16.4 %collective-permute-start.51 = (bf16[136,640]{1,0:T(8,128)(2,1)S(1)}, bf16[136,640]{1,0:T(8,128)(2,1)S(1)}, u32[]{:S(2)}, u32[]{:S(2)}) collective-permute-start(bf16[136,640]{1,0:T(8,128)(2,1)S(1)} %get-tuple-element.109), channel_id=1, source_target_pairs={{0,6},{1,7},{2,0},{3,1},{4,2},{5,3},{6,4},{7,5},{8,14},{9,15},{10,... | collective-permute-start | bytes 522248 | tf_op jit(solution)/shard_map/ppermute | solution.py:41
  681.2 19.2 %collective-permute-start.33 = (bf16[136,640]{1,0:T(8,128)(2,1)S(1)}, bf16[136,640]{1,0:T(8,128)(2,1)S(1)}, u32[]{:S(2)}, u32[]{:S(2)}) collective-permute-start(bf16[136,640]{1,0:T(8,128)(2,1)S(1)} %constant_dynamic-slice_fusion.21), channel_id=1, source_target_pairs={{0,17},{1,16},{2,19},{3,18},{4,21},{5,20},{6,23},{7,22},{8,25},{9,... | collective-permute-start | bytes 522248 | tf_op jit(solution)/shard_map/ppermute | solution.py:41
  690.4 12.6 %collective-permute-start.13 = (bf16[136,640]{1,0:T(8,128)(2,1)S(1)}, bf16[136,640]{1,0:T(8,128)(2,1)S(1)}, u32[]{:S(2)}, u32[]{:S(2)}) collective-permute-start(bf16[136,640]{1,0:T(8,128)(2,1)S(1)} %get-tuple-element.162), channel_id=1, source_target_pairs={{0,32},{1,33},{2,34},{3,35},{4,36},{5,37},{6,38},{7,39},{8,40},{9,... | collective-permute-start | bytes 522248 | tf_op jit(solution)/shard_map/ppermute | solution.py:41
  692.8 10.1 %collective-permute-start.15 = (bf16[136,640]{1,0:T(8,128)(2,1)S(1)}, bf16[136,640]{1,0:T(8,128)(2,1)S(1)}, u32[]{:S(2)}, u32[]{:S(2)}) collective-permute-start(bf16[136,640]{1,0:T(8,128)(2,1)S(1)} %get-tuple-element.164), channel_id=1, source_target_pairs={{0,96},{1,97},{2,98},{3,99},{4,100},{5,101},{6,102},{7,103},{8,104... | collective-permute-start | bytes 522248 | tf_op jit(solution)/shard_map/ppermute | solution.py:41
  693.7 5.8 collective-permute-start.52
  700.4 12.9 %collective-permute-start.54 = (bf16[68,2176]{1,0:T(8,128)(2,1)}, bf16[68,2176]{1,0:T(8,128)(2,1)}, u32[]{:S(2)}, u32[]{:S(2)}) collective-permute-start(bf16[68,2176]{1,0:T(8,128)(2,1)} %constant_dynamic-slice_fusion.15), channel_id=1, source_target_pairs={{0,8},{1,9},{2,10},{3,11},{4,12},{5,13},{6,14},{7,15},{8,0},{9,1},... | collective-permute-start | bytes 887816 | tf_op jit(solution)/shard_map/ppermute | solution.py:41
  700.4 7.6 collective-permute-start.34
  703.8 23.0 %collective-permute-start.14 = (bf16[272,640]{1,0:T(8,128)(2,1)}, bf16[272,640]{1,0:T(8,128)(2,1)}, u32[]{:S(2)}, u32[]{:S(2)}) collective-permute-start(bf16[272,640]{1,0:T(8,128)(2,1)} %pad_maximum_fusion.38), channel_id=1, source_target_pairs={{0,32},{1,33},{2,34},{3,35},{4,36},{5,37},{6,38},{7,39},{8,40},{9,... | collective-permute-start | bytes 1044488 | tf_op jit(solution)/shard_map/ppermute | solution.py:41
  704.7 22.1 %collective-permute-start.16 = (bf16[272,640]{1,0:T(8,128)(2,1)}, bf16[272,640]{1,0:T(8,128)(2,1)}, u32[]{:S(2)}, u32[]{:S(2)}) collective-permute-start(bf16[272,640]{1,0:T(8,128)(2,1)} %pad_maximum_fusion.39), channel_id=1, source_target_pairs={{0,96},{1,97},{2,98},{3,99},{4,100},{5,101},{6,102},{7,103},{8,104... | collective-permute-start | bytes 1044488 | tf_op jit(solution)/shard_map/ppermute | solution.py:41
  708.7 10.1 %collective-permute-start.35 = (bf16[136,640]{1,0:T(8,128)(2,1)}, bf16[136,640]{1,0:T(8,128)(2,1)}, u32[]{:S(2)}, u32[]{:S(2)}) collective-permute-start(bf16[136,640]{1,0:T(8,128)(2,1)} %add_convert_fusion.33), channel_id=1, source_target_pairs={{0,2},{1,3},{2,4},{3,5},{4,6},{5,7},{6,0},{7,1},{8,10},{9,11},{10,... | collective-permute-start | bytes 522248 | tf_op jit(solution)/shard_map/ppermute | solution.py:41
  708.7 11.1 %collective-permute-start.36 = (bf16[136,640]{1,0:T(8,128)(2,1)}, bf16[136,640]{1,0:T(8,128)(2,1)}, u32[]{:S(2)}, u32[]{:S(2)}) collective-permute-start(bf16[136,640]{1,0:T(8,128)(2,1)} %add_convert_fusion.33), channel_id=1, source_target_pairs={{0,6},{1,7},{2,0},{3,1},{4,2},{5,3},{6,4},{7,5},{8,14},{9,15},{10,... | collective-permute-start | bytes 522248 | tf_op jit(solution)/shard_map/ppermute | solution.py:41
  719.7 12.1 %collective-permute-start.37 = (bf16[68,640]{1,0:T(8,128)(2,1)S(1)}, bf16[68,640]{1,0:T(8,128)(2,1)S(1)}, u32[]{:S(2)}, u32[]{:S(2)}) collective-permute-start(bf16[68,640]{1,0:T(8,128)(2,1)S(1)} %slice.639), channel_id=1, source_target_pairs={{0,2},{1,3},{2,4},{3,5},{4,6},{5,7},{6,0},{7,1},{8,10},{9,11},{10,... | collective-permute-start | bytes 261128 | tf_op jit(solution)/shard_map/ppermute | solution.py:41
  721.3 10.5 %collective-permute-start.38 = (bf16[68,640]{1,0:T(8,128)(2,1)}, bf16[68,640]{1,0:T(8,128)(2,1)S(1)}, u32[]{:S(2)}, u32[]{:S(2)}) collective-permute-start(bf16[68,640]{1,0:T(8,128)(2,1)} %slice.640), channel_id=1, source_target_pairs={{0,6},{1,7},{2,0},{3,1},{4,2},{5,3},{6,4},{7,5},{8,14},{9,15},{10,... | collective-permute-start | bytes 261128 | tf_op jit(solution)/shard_map/ppermute | solution.py:41
  728.1 7.3 collective-permute-start.17
  737.0 7.7 collective-permute-start.39
  741.0 6.9 collective-permute-start.19
  741.1 6.9 collective-permute-start.20
  (110 other events, 557.8 us)

commit v3 on v2

v3 whole, which is shorter than its diff:
```python
import functools

import jax
import jax.numpy as jnp
from jax import lax
from jax.experimental import pallas as pl
from jax.experimental.pallas import tpu as pltpu
from jax.sharding import PartitionSpec as P

EPSILON = 1e-05
MASKED = -1e30
MESH = pl.DeviceIdType.MESH
F32 = jnp.float32
BF16 = jnp.bfloat16
GROUP = 8
SLOTS = 5
HEAD = 64
WINDOW = 384
STRIDE = 256
PADDED = 1152
CHUNK = 128


def places():
    dp = lax.axis_index("dp")
    return {
        "x": dp // 4,
        "y": (dp // 2) % 2,
        "c": dp % 2,
        "z": lax.axis_index("ctx"),
        "t": lax.axis_index("tensor"),
    }


def shifted(value, x=0, y=0, c=0, z=0, t=0):
    pairs = []
    for i in range(128):
        ix, iy, ic, iz, it = i // 32, (i // 16) % 2, (i // 8) % 2, (i // 2) % 4, i % 2
        ix, iy, ic, iz, it = (ix + x) % 4, (iy + y) % 2, (ic + c) % 2, (iz + z) % 4, (it + t) % 2
        pairs.append((i, (((ix * 2 + iy) * 2 + ic) * 4 + iz) * 2 + it))
    return lax.ppermute(value, ("dp", "ctx", "tensor"), pairs)


ROWS = 68
TALL = 80
BLOCK = 272
NEAR = 144
Q_COLS = 512
T_START = 2048
T_COLS = 256
M_COLS = 2176


def peer_at(x=0, y=0, c=0, z=0, t=0):
    at = places()
    dp = (lax.rem(at["x"] + x + 4, 4) * 2 + lax.rem(at["y"] + y, 2)) * 2 + lax.rem(at["c"] + c, 2)
    return (dp, lax.rem(at["z"] + z + 4, 4), lax.rem(at["t"] + t, 2))


class Copies:
    def __init__(self, send_sem, recv_sem):
        self.send_sem, self.recv_sem = send_sem, recv_sem
        self.count = 0
        self.open = []

    def to(self, peer, src, dst):
        n = self.count
        self.count += 1
        copy = pltpu.make_async_remote_copy(
            src_ref=src,
            dst_ref=dst,
            send_sem=self.send_sem.at[n],
            recv_sem=self.recv_sem.at[n],
            device_id=peer,
            device_id_type=MESH,
        )
        copy.start()
        self.open.append(copy.wait_send)
        return copy.wait_recv

    def here(self, src, dst):
        n = self.count
        self.count += 1
        copy = pltpu.make_async_copy(src, dst, self.send_sem.at[n])
        copy.start()
        return copy.wait

    def close(self):
        for wait in self.open:
            wait()
        self.open = []


def rows_at(block, count=BLOCK, skip=0):
    return pl.ds(pl.multiple_of(block * BLOCK + skip, 16), count)


class RingX:
    def __init__(self, copies, own, buf, lanes, share):
        self.copies, self.own, self.buf, self.lanes, self.share = copies, own, buf, lanes, share
        at = places()
        self.c, self.x = at["c"], at["x"]
        self.last = []

    def view(self, distance, count=BLOCK, skip=0):
        block = lax.rem(self.x + distance + 4, 4)
        return self.buf.at[self.c, rows_at(block, count, skip), self.lanes]

    def sibling(self, src, dst):
        if self.share:
            self.last.append(self.copies.to(peer_at(c=1), src, dst))

    def start(self):
        self.from_below = self.copies.to(peer_at(x=1), self.own, self.view(0))
        self.from_above = self.copies.to(peer_at(x=-1), self.own, self.view(0))
        self.last.append(self.copies.here(self.own, self.view(0)))
        self.sibling(self.own, self.view(0))

    def forward(self):
        self.from_below()
        part = self.view(-1, NEAR)
        far_a = self.copies.to(peer_at(x=1), part, part)
        self.from_above()
        part = self.view(1, BLOCK - NEAR, NEAR)
        far_b = self.copies.to(peer_at(x=-1), part, part)
        self.far = (far_a, far_b)
        self.sibling(self.view(-1), self.view(-1))
        self.sibling(self.view(1), self.view(1))

    def finish(self):
        for wait in self.far:
            wait()
        self.sibling(self.view(2), self.view(2))

    def close(self):
        for wait in self.last:
            wait()


class RingZ:
    def __init__(self, copies, buf):
        self.copies, self.buf = copies, buf
        at = places()
        self.c, self.z = at["c"], at["z"]
        self.last = []

    def view(self, distance, rows=slice(None)):
        block = lax.rem(self.z + distance + 4, 4)
        return self.buf.at[self.c, rows, pl.ds(pl.multiple_of(block * Q_COLS, 128), Q_COLS)]

    def sibling(self, src):
        self.last.append(self.copies.to(peer_at(c=1), src, src))

    def start(self):
        own = self.view(0)
        self.from_below = self.copies.to(peer_at(z=1), own, own)
        self.from_above = self.copies.to(peer_at(z=-1), own, own)
        self.sibling(own)

    def forward(self):
        self.from_below()
        part = self.view(-1, pl.ds(0, 544))
        far_a = self.copies.to(peer_at(z=1), part, part)
        self.from_above()
        part = self.view(1, pl.ds(544, 544))
        far_b = self.copies.to(peer_at(z=-1), part, part)
        self.far = (far_a, far_b)
        self.sibling(self.view(-1))
        self.sibling(self.view(1))

    def finish(self):
        for wait in self.far:
            wait()
        self.sibling(self.view(2))

    def close(self):
        for wait in self.last:
            wait()


def exchange_shards(copies, mine, landed):
    c = places()["c"]
    waits = [
        copies.to(peer_at(c=1), mine.at[1 - c], landed.at[1]),
        copies.to(peer_at(y=1), mine.at[c], landed.at[2]),
        copies.to(peer_at(y=1, c=1), mine.at[1 - c], landed.at[3]),
    ]
    waits.append(copies.here(mine.at[c], landed.at[0]))
    return waits


def assemble(landed, own):
    at = places()
    width = own.shape[1]
    for start in range(0, width, 256):
        lanes = slice(start, min(start + 256, width))
        parts = []
        for j in range(4):
            slot = lax.rem(j // 2 + at["y"], 2) * 2 + lax.rem(j % 2 + at["c"], 2)
            parts.append(landed[slot, :, lanes].astype(F32)[:ROWS])
        own[:, lanes] = jnp.concatenate(parts, 0).astype(BF16)


def gather_kernel(
    q0, mt0, q1, mt1, docs, attn, mlp, vec_tail, q_next, mt_next, docs_all,
    q_land, mt_land, q_own, mt_own, q_own1, mt_own1, send_sem, recv_sem,
):
    me = group_place()
    greet([dict(c=1), dict(y=1), dict(y=1, c=1), dict(x=1), dict(x=-1)], me)
    copies = Copies(send_sem, recv_sem)
    quarter = pl.ds(pl.multiple_of(places()["z"] * Q_COLS, 128), Q_COLS)
    arrive_q = exchange_shards(copies, q0, q_land.at[0])
    arrive_mt = exchange_shards(copies, mt0, mt_land.at[0])
    later = [copies.here(docs, docs_all.at[me])]
    for n in range(1, GROUP):
        later.append(copies.to(member(lax.rem(me + n, GROUP)), docs, docs_all.at[me]))
    arrive_q1 = exchange_shards(copies, q1, q_land.at[1])
    arrive_mt1 = exchange_shards(copies, mt1, mt_land.at[1])
    q = RingX(copies, q_own, attn, quarter, False)
    m = RingX(copies, mt_own.at[:, pl.ds(0, M_COLS)], mlp, slice(None), True)
    t = RingX(copies, mt_own.at[:, pl.ds(M_COLS, T_COLS)], attn, pl.ds(T_START, T_COLS), True)
    along_z = RingZ(copies, attn)

    def landed(waits, land, own):
        for wait in waits:
            wait()
        assemble(land, own)

    landed(arrive_q, q_land.at[0], q_own)
    q.start()
    q.forward()
    landed(arrive_mt, mt_land.at[0], mt_own)
    t.start()
    m.start()
    q.finish()
    q.close()
    along_z.start()
    t.forward()
    landed(arrive_q1, q_land.at[1], q_own1)
    later.append(copies.here(q_own1, q_next))
    m.forward()
    along_z.forward()
    landed(arrive_mt1, mt_land.at[1], mt_own1)
    later.append(copies.here(mt_own1, mt_next))
    t.finish()
    m.finish()
    along_z.finish()
    for ring in (t, m, along_z):
        ring.close()
    later.append(copies.here(attn.at[0, :, pl.ds(PADDED - 128, 128)], vec_tail))
    for wait in later:
        wait()
    copies.close()


def shard_rows(qkv, out, up, down, vec, z):
    width = out.shape[1]
    role0 = jnp.concatenate([padded(qkv[:, :width], vec.T), padded(qkv[:, width : 2 * width])], 1)
    role1 = jnp.concatenate([padded(qkv[:, 2 * width :]), padded(out)], 1)
    attn = jnp.pad(jnp.stack([role0, role1]), ((0, 0), (0, TALL - ROWS), (0, 0)))
    mlp = jnp.pad(jnp.stack([up, down]), ((0, 0), (0, TALL - ROWS), (0, 0)))
    quarter = lax.dynamic_slice_in_dim(attn, z * Q_COLS, Q_COLS, 2)
    return quarter, jnp.concatenate([mlp, attn[:, :, T_START:]], 2)


def gather_first(shards, docs, collective):
    hbm = pl.BlockSpec(memory_space=pl.ANY)
    shape = jax.ShapeDtypeStruct
    (q0, mt0), (q1, mt1) = shards
    low = lambda *dims: pltpu.VMEM(dims, BF16)
    return pl.pallas_call(
        gather_kernel,
        out_shape=[
            shape((2, 4 * BLOCK, 2 * PADDED), BF16),
            shape((2, 4 * BLOCK, M_COLS), BF16),
            shape((4 * BLOCK, 128), BF16),
            shape((BLOCK, Q_COLS), BF16),
            shape((BLOCK, M_COLS + T_COLS), BF16),
            shape((GROUP, *docs.shape), docs.dtype),
        ],
        in_specs=[hbm] * 5,
        out_specs=[hbm] * 6,
        scratch_shapes=[
            low(2, 4, TALL, Q_COLS),
            low(2, 4, TALL, M_COLS + T_COLS),
            low(BLOCK, Q_COLS),
            low(BLOCK, M_COLS + T_COLS),
            low(BLOCK, Q_COLS),
            low(BLOCK, M_COLS + T_COLS),
            pltpu.SemaphoreType.DMA((64,)),
            pltpu.SemaphoreType.DMA((64,)),
        ],
        compiler_params=pltpu.CompilerParams(
            collective_id=collective, has_side_effects=True, vmem_limit_bytes=32 * 2**20
        ),
    )(q0, mt0, q1, mt1, docs)


def padded(matrix, extra=None):
    rows, width = matrix.shape
    parts = [matrix]
    if extra is not None:
        parts.append(extra)
        width += extra.shape[1]
    parts.append(jnp.zeros((rows, PADDED - width), matrix.dtype))
    return jnp.concatenate(parts, 1)


PIECE = 640
HALF = 136
HALF_TALL = 144


def attn_start(z):
    return z * 13 // 3 * 128


def mlp_start(z):
    return z * 512


def contract_rows(a, b):
    return lax.dot_general(a, b, (((0,), (0,)), ((), ())), preferred_element_type=F32)


def contract_cols(a, b):
    return lax.dot_general(a, b, (((1,), (1,)), ((), ())), preferred_element_type=F32)


def block_diagonal(a, b):
    zero = jnp.zeros_like(a)
    return jnp.concatenate(
        [jnp.concatenate([a, zero], 1), jnp.concatenate([zero, b], 1)], 0
    )


def chip_sums(at, operands):
    a, dq, dk, dv, o, dz, m, du, dy, g, vec = operands
    c0 = at["c"] == 0
    width = a.shape[1]
    pick = lambda p, q: jnp.where(c0, p, q)
    vec_cols = jnp.pad(vec.T, ((0, 0), (width, 2 * PADDED - width - vec.shape[0])))
    give = contract_rows(
        jnp.concatenate([a, pick(o, a)], 0), block_diagonal(pick(dv, dq), pick(dz, dk))
    ) + pick(0.0, 1.0) * vec_cols
    got = shifted(give.astype(BF16), c=1)
    keep = contract_rows(
        jnp.concatenate([a, pick(a, o)], 0), block_diagonal(pick(dq, dv), pick(dk, dz))
    ) + pick(1.0, 0.0) * vec_cols
    attn = (keep + got.astype(F32)).astype(BF16)
    give = contract_rows(pick(dy, m), pick(g, du)).astype(BF16)
    got = shifted(give, c=1)
    mlp = (contract_rows(pick(m, dy), pick(du, g)) + got.astype(F32)).astype(BF16)
    return attn, mlp


def in_chunks(count, step, do):
    def one(i, carry):
        do(pl.ds(pl.multiple_of(i * step, 16), step))
        return carry

    lax.fori_loop(0, count // step, one, 0)


class RingSum:
    def __init__(self, copies, axis, view, rows, near, via, step, stage=None):
        self.copies, self.axis, self.view, self.rows = copies, axis, view, rows
        self.near, self.via, self.step, self.stage = near, via, step, stage
        cut = via.shape[1]
        self.first, self.last = pl.ds(0, cut), pl.ds(cut, rows - cut)
        self.counts = (cut, rows - cut)
        self.up, self.down = peer_at(**{axis: 1}), peer_at(**{axis: -1})

    def start(self):
        first, last = self.first, self.last
        far, up, down = self.view(2), self.view(1), self.view(-1)
        rest = pl.ds(0, self.counts[1])
        self.via_up = self.copies.to(self.up, far.at[first], self.via.at[0])
        self.via_down = self.copies.to(self.down, far.at[last], self.via.at[1, rest])
        self.near_a = self.copies.to(self.up, up.at[last], self.near.at[0, last])
        self.near_b = self.copies.to(self.down, down.at[first], self.near.at[1, first])
        self.parts = (up.at[first], down.at[last])
        self.staged = []
        if self.stage is not None:
            staged = (self.stage.at[0], self.stage.at[1, rest])
            for src, dst in zip(self.parts, staged):
                self.staged.append(self.copies.here(src, dst))
            self.parts = staged

    def forward(self):
        for wait in self.staged:
            wait()
        arrived = (self.via_up, self.via_down)
        ends = ((self.up, 0, self.first), (self.down, 1, self.last))
        self.nears = [self.near_a, self.near_b]
        for n, (peer, side, rows) in enumerate(ends):
            arrived[n]()
            part = self.parts[n]

            def add(r):
                self.via[n, r, :] = (part[r, :].astype(F32) + self.via[n, r, :].astype(F32)).astype(BF16)

            in_chunks(self.counts[n], self.step, add)
            src = self.via.at[n, pl.ds(0, self.counts[n])]
            self.nears.append(self.copies.to(peer, src, self.near.at[side, rows]))

    def land(self):
        for wait in self.nears:
            wait()


def add_near(own, near, rows, step, write):
    def add(r):
        write(r, own[r, :].astype(F32) + near[0, r, :].astype(F32) + near[1, r, :].astype(F32))

    in_chunks(rows, step, add)


def turn(value, distance):
    return lax.rem(value + distance + 4, 4)


def columns_of(array, start_of, z):
    return array.at[:, pl.ds(pl.multiple_of(start_of(z), 128), PIECE)]


def attn_ring(copies, array, near, via, stage):
    view = lambda d: columns_of(array, attn_start, turn(places()["z"], d))
    return RingSum(copies, "z", view, 4 * BLOCK, near, via, 32, stage)


def mlp_ring(copies, array, near, via, stage):
    view = lambda d: array.at[rows_at(turn(places()["x"], d))]
    return RingSum(copies, "x", view, BLOCK, near, via, 16, stage)


def reduce_kernel(
    attn0, mlp0, attn1, mlp1, attn_near1, mlp_near1, out,
    attn_near, attn_via, attn_stage, mlp_near, mlp_via, mlp_stage, attn_own, mlp_own,
    attn_part, mlp_part, near2, via2, halves, got, owned, owned_got, send_sem, recv_sem,
):
    barrier = pltpu.get_barrier_semaphore()
    peers = [dict(c=1), dict(x=1), dict(x=-1), dict(y=1, t=1), dict(y=1), dict(t=1)]
    peers += [dict(z=1), dict(z=2), dict(z=3)]
    for peer in peers:
        pl.semaphore_signal(barrier, inc=1, device_id=peer_at(**peer), device_id_type=MESH)
    pl.semaphore_wait(barrier, len(peers))
    copies = Copies(send_sem, recv_sem)
    at = places()
    ring_a = attn_ring(copies, attn0, attn_near, attn_via, attn_stage)
    ring_m = mlp_ring(copies, mlp0, mlp_near, mlp_via, mlp_stage)
    ring_a.start()
    ring_m.start()
    loads = {}
    for l, (attn, mlp) in ((1, (attn1, mlp1)), (0, (attn0, mlp0))):
        loads[l] = (
            copies.here(columns_of(attn, attn_start, at["z"]), attn_own.at[l]),
            copies.here(mlp.at[rows_at(at["x"])], mlp_own.at[l]),
        )

    def second(l, near_a, near_m):
        def write_attn(r, value):
            attn_part[l, r, :] = value.astype(BF16)

        def write_mlp(r, value):
            mlp_part[l, r, :] = value.astype(BF16)

        for wait in loads[l]:
            wait()
        add_near(mlp_own.at[l], near_m, BLOCK, 16, write_mlp)
        m2 = RingSum(
            copies, "z", lambda d: columns_of(mlp_part.at[l], mlp_start, turn(at["z"], d)),
            BLOCK, near2.at[l, 1], via2.at[l, 1], 16,
        )
        m2.start()
        add_near(attn_own.at[l], near_a, 4 * BLOCK, 32, write_attn)
        a2 = RingSum(
            copies, "x", lambda d: attn_part.at[l, rows_at(turn(at["x"], d))],
            BLOCK, near2.at[l, 0], via2.at[l, 0], 16,
        )
        a2.start()
        return a2, m2

    def third(l, rings):
        waits = []
        for n, ring in enumerate(rings):
            ring.land()
            own = ring.view(0)
            total = (
                own[...].astype(F32) + ring.near[0].astype(F32) + ring.near[1].astype(F32)
            )
            halves[l, n, 0, :HALF] = total[:HALF].astype(BF16)
            halves[l, n, 1, :HALF] = total[HALF:].astype(BF16)
            halves[l, n, 0, HALF:] = jnp.zeros((HALF_TALL - HALF, PIECE), BF16)
            halves[l, n, 1, HALF:] = jnp.zeros((HALF_TALL - HALF, PIECE), BF16)
            peer = peer_at(y=1, t=1) if n == 0 else peer_at(y=1)
            waits.append(copies.to(peer, halves.at[l, n, 1 - at["y"]], got.at[l, n]))
        return waits

    def fourth(l, waits):
        waits[0]()
        mine = halves[l, 0, at["y"]].astype(F32) + got[l, 0].astype(F32)
        halves[l, 0, at["y"]] = mine.astype(BF16)
        return copies.to(peer_at(t=1), halves.at[l, 0, at["y"]], got.at[l, 2])

    def fifth(l, waits, wait):
        waits[1]()
        wait()
        ends = []
        for n, landed in ((0, 2), (1, 1)):
            total = halves[l, n, at["y"]].astype(F32) + got[l, landed].astype(F32)
            for core in range(2):
                owned[l, n, core, :ROWS] = total[core * ROWS : core * ROWS + ROWS].astype(BF16)
                owned[l, n, core, ROWS:] = jnp.zeros((TALL - ROWS, PIECE), BF16)
            ends.append(copies.to(peer_at(c=1), owned.at[l, n, 1 - at["c"]], owned_got.at[l, n]))
        return ends

    def sixth(l, ends):
        for wait in ends:
            wait()
        rest = []
        for n in range(2):
            for role, src in ((at["c"], owned.at[l, n, at["c"]]), (1 - at["c"], owned_got.at[l, n])):
                dst = out.at[l, at["z"], n, role]
                rest.append(copies.here(src, dst))
                for d in (1, 2, 3):
                    rest.append(copies.to(peer_at(z=d), src, dst))
        return rest

    rings, waits, rest = {}, {}, []
    rings[1] = second(1, attn_near1, mlp_near1)
    ring_m.forward()
    ring_a.forward()
    for ring in reversed(rings[1]):
        ring.forward()
    waits[1] = third(1, rings[1])
    turned = fourth(1, waits[1])
    rest += sixth(1, fifth(1, waits[1], turned))
    ring_m.land()
    ring_a.land()
    rings[0] = second(0, attn_near, mlp_near)
    for ring in reversed(rings[0]):
        ring.forward()
    waits[0] = third(0, rings[0])
    turned = fourth(0, waits[0])
    rest += sixth(0, fifth(0, waits[0], turned))
    for wait in rest:
        wait()
    copies.close()


def reduce_layers(sums, near, collective):
    hbm = pl.BlockSpec(memory_space=pl.ANY)
    vmem = pl.BlockSpec(memory_space=pltpu.VMEM)
    low = lambda *dims: pltpu.VMEM(dims, BF16)
    return pl.pallas_call(
        reduce_kernel,
        out_shape=jax.ShapeDtypeStruct((2, 4, 2, 2, TALL, PIECE), BF16),
        in_specs=[hbm] * 4 + [vmem] * 2,
        out_specs=hbm,
        scratch_shapes=[
            low(2, 4 * BLOCK, PIECE),
            low(2, 2 * BLOCK, PIECE),
            low(2, 2 * BLOCK, PIECE),
            low(2, BLOCK, M_COLS),
            low(2, NEAR, M_COLS),
            low(2, NEAR, M_COLS),
            low(2, 4 * BLOCK, PIECE),
            low(2, BLOCK, M_COLS),
            low(2, 4 * BLOCK, PIECE),
            low(2, BLOCK, M_COLS),
            low(2, 2, 2, BLOCK, PIECE),
            low(2, 2, 2, NEAR, PIECE),
            low(2, 2, 2, HALF_TALL, PIECE),
            low(2, 3, HALF_TALL, PIECE),
            low(2, 2, 2, TALL, PIECE),
            low(2, 2, TALL, PIECE),
            pltpu.SemaphoreType.DMA((96,)),
            pltpu.SemaphoreType.DMA((96,)),
        ],
        compiler_params=pltpu.CompilerParams(
            collective_id=collective, has_side_effects=True, vmem_limit_bytes=56 * 2**20
        ),
    )(*sums[0], *sums[1], *near)


def owned_gradients(parts, width):
    parts = parts[:, :, :, :ROWS]

    def joined(n, role, widths):
        return jnp.concatenate([parts[z, n, role, :, :w] for z, w in enumerate(widths)], 1)

    attn = [joined(0, role, (512, 512, 640, 640)) for role in range(2)]
    up, down = (joined(1, role, (512, 512, 512, 640)) for role in range(2))
    qk, vo = attn
    in_back = jnp.concatenate([qk[:, :width], qk[:, PADDED : PADDED + width], vo[:, :width]], 1)
    vec_back = qk[:, width : width + 12].T
    results = (in_back, vo[:, PADDED : PADDED + width], up, down, vec_back)
    return tuple(value.astype(F32) for value in results)


def group_place():
    return lax.axis_index("ctx") * 2 + lax.axis_index("tensor")


def member(index):
    return (lax.axis_index("dp"), index // 2, lax.rem(index, 2))


def meet(me):
    barrier = pltpu.get_barrier_semaphore()
    for k in range(1, GROUP):
        pl.semaphore_signal(
            barrier, inc=1, device_id=member(lax.rem(me + k, GROUP)), device_id_type=MESH
        )
    pl.semaphore_wait(barrier, GROUP - 1)


def to_heads(me, sources, landed, local_sem, send_sem, recv_sem):
    copies = []
    for k in range(1, GROUP):
        peer = lax.rem(me + k, GROUP)
        rows = pl.ds(pl.multiple_of(peer // 4 * 64, 64), 64)
        lanes = pl.ds(pl.multiple_of(lax.rem(peer, 4) * STRIDE, 128), WINDOW)
        for n, (src, dst) in enumerate(zip(sources, landed)):
            copy = pltpu.make_async_remote_copy(
                src_ref=src.at[rows, lanes],
                dst_ref=dst.at[pl.ds(pl.multiple_of(me * 64, 64), 64)],
                send_sem=send_sem.at[n, k],
                recv_sem=recv_sem.at[n, k],
                device_id=member(peer),
                device_id_type=MESH,
            )
            copy.start()
            copies.append(copy)
    rows = pl.ds(pl.multiple_of(me // 4 * 64, 64), 64)
    lanes = pl.ds(pl.multiple_of(lax.rem(me, 4) * STRIDE, 128), WINDOW)
    for n, (src, dst) in enumerate(zip(sources, landed)):
        copy = pltpu.make_async_copy(
            src.at[rows, lanes], dst.at[pl.ds(pl.multiple_of(me * 64, 64), 64)], local_sem.at[n]
        )
        copy.start()
        copies.append(copy)
    return copies


def to_rows(me, sources, landed, local_sem, send_sem, recv_sem):
    copies = []
    for k in range(1, GROUP):
        peer = lax.rem(me + k, GROUP)
        for n, (src, dst) in enumerate(zip(sources, landed)):
            copy = pltpu.make_async_remote_copy(
                src_ref=src.at[pl.ds(pl.multiple_of(peer * 64, 64), 64)],
                dst_ref=dst.at[me],
                send_sem=send_sem.at[n, k],
                recv_sem=recv_sem.at[n, k],
                device_id=member(peer),
                device_id_type=MESH,
            )
            copy.start()
            copies.append(copy)
    for n, (src, dst) in enumerate(zip(sources, landed)):
        copy = pltpu.make_async_copy(
            src.at[pl.ds(pl.multiple_of(me * 64, 64), 64)], dst.at[me], local_sem.at[n]
        )
        copy.start()
        copies.append(copy)
    return copies


def side_by_side(landed, out):
    for micro in range(2):
        rows = slice(micro * 64, micro * 64 + 64)
        for group in range(4):
            width = WINDOW if group == 3 else STRIDE
            out[rows, group * STRIDE : group * STRIDE + width] = landed[micro * 4 + group, :, :width]


def matmul(a, b, dims):
    return lax.dot_general(a, b, ((dims[:1], dims[1:]), ((), ())), preferred_element_type=F32)


def score_bias(docs):
    docs = lax.dynamic_index_in_dim(docs, lax.axis_index("ctx") // 2, 1, keepdims=False)
    docs = docs[:, :64].reshape(-1)
    place = jnp.arange(docs.shape[0], dtype=jnp.int32)
    allowed = (docs[:, None] == docs[None, :]) & (place[None, :] <= place[:, None])
    return jnp.where(allowed, 0.0, MASKED).astype(F32)


def tiles_of(width, step):
    return [(start, min(start + step, width)) for start in range(0, width, step)]


def normalise(inputs):
    centred = inputs - jnp.mean(inputs, 1, keepdims=True)
    spread = jnp.mean(centred * centred, 1, keepdims=True)
    scale = lax.rsqrt(spread + EPSILON)
    return centred * scale, scale


def gelu_and_slope(u):
    share = 0.5 * (1.0 + lax.erf(u * 0.7071067811865476))
    return u * share, share + u * jnp.exp(-0.5 * u * u) * 0.3989422804014327


def greet(peers, me):
    barrier = pltpu.get_barrier_semaphore()
    members = [member(lax.rem(me + k, GROUP)) for k in range(1, GROUP)]
    for peer in members + [peer_at(**peer) for peer in peers]:
        pl.semaphore_signal(barrier, inc=1, device_id=peer, device_id_type=MESH)
    pl.semaphore_wait(barrier, len(members) + len(peers))


def forward_kernel(*refs, carry):
    resid, vec, bias_up, mask, attn_in, mlp_in = refs[:6]
    refs = refs[6:]
    if carry:
        q_own, mt_own = refs[:2]
        refs = refs[2:]
    (
        resid_out, normed, q_all, k_all, v_all, o_all, log_total, o_out, midway, m_out, g_out, d_out,
    ) = refs[:12]
    refs = refs[12:]
    if carry:
        next_attn, next_mlp, next_tail = refs[:3]
        refs = refs[3:]
    (
        attn, mlp, q, k, v, o_low, o_landed, part, part_got, load_sem, local_sem, send_sem, recv_sem,
    ) = refs[:13]
    me = group_place()
    greet([dict(c=1), dict(x=1), dict(x=-1)] if carry else [], me)
    loads = []
    for n, (src, dst) in enumerate(
        [(attn_in.at[0], attn.at[0]), (attn_in.at[1], attn.at[1]), (mlp_in.at[0], mlp.at[0]), (mlp_in.at[1], mlp.at[1])]
    ):
        copy = pltpu.make_async_copy(src, dst, load_sem.at[n])
        copy.start()
        loads.append(copy.wait)
    if carry:
        copies = Copies(*refs[13:15])
        quarter = pl.ds(pl.multiple_of(places()["z"] * Q_COLS, 128), Q_COLS)
        ring_q = RingX(copies, q_own, next_attn, quarter, False)
        ring_m = RingX(copies, mt_own.at[:, pl.ds(0, M_COLS)], next_mlp, slice(None), True)
        ring_t = RingX(copies, mt_own.at[:, pl.ds(M_COLS, T_COLS)], next_attn, pl.ds(T_START, T_COLS), True)
        ring_z = RingZ(copies, next_attn)
        ring_q.start()
    row = lambda n: vec[n : n + 1, :]
    width = resid.shape[1]
    x, _ = normalise(resid[...])
    a = (x * row(0)[:, :width] + row(1)[:, :width]).astype(BF16)
    normed[...] = a
    loads[0]()
    for start, stop in tiles_of(PADDED, 384):
        lanes = slice(start, stop)
        q[:, lanes] = (matmul(a, attn[0, :, lanes], (1, 0)) + vec[2:3, lanes]).astype(BF16)
        k[:, lanes] = matmul(a, attn[0, :, PADDED + start : PADDED + stop], (1, 0)).astype(BF16)
    loads[1]()
    for start, stop in tiles_of(PADDED, 384):
        lanes = slice(start, stop)
        v[:, lanes] = (matmul(a, attn[1, :, lanes], (1, 0)) + vec[3:4, lanes]).astype(BF16)
    exchanged = to_heads(me, (q, k, v), (q_all, k_all, v_all), local_sem, send_sem, recv_sem)
    o_low[...] = jnp.zeros_like(o_low)
    o_all[...] = jnp.zeros_like(o_all)
    log_total[...] = jnp.zeros_like(log_total)
    if carry:
        ring_q.forward()
        ring_t.start()
        ring_m.start()
    for copy in exchanged:
        copy.wait()
    if carry:
        ring_q.finish()
        ring_q.close()
        ring_z.start()
    for head in range(SLOTS):
        lanes = slice(head * HEAD, head * HEAD + HEAD)
        keys, values = k_all[:, lanes], v_all[:, lanes]
        for start in range(0, 512, CHUNK):
            rows, reach = slice(start, start + CHUNK), start + CHUNK
            queries = q_all[rows, lanes] * 0.125
            scores = matmul(queries, keys[:reach], (1, 1)) + mask[rows, :reach]
            top = jnp.max(scores, 1, keepdims=True)
            weights = jnp.exp(scores - top)
            total = jnp.sum(weights, 1, keepdims=True)
            result = matmul(weights.astype(BF16), values[:reach], (1, 0)) / total
            o_all[rows, lanes] = result
            o_low[rows, lanes] = result.astype(BF16)
            log_total[rows, head : head + 1] = top + jnp.log(total)
    exchanged = to_rows(
        me, (o_low,), (o_landed,), local_sem.at[3:4], send_sem.at[3:4], recv_sem.at[3:4]
    )
    if carry:
        ring_t.forward()
        ring_m.forward()
    for copy in exchanged:
        copy.wait()
    if carry:
        ring_z.forward()
    side_by_side(o_landed, o_out)
    o = o_out[:, :width]
    for start, stop in tiles_of(width, 384):
        lanes = slice(start, stop)
        midway[:, lanes] = (
            resid[:, lanes]
            + matmul(o, attn[1, :, PADDED + start : PADDED + stop], (1, 0))
            + vec[4:5, lanes]
        )
    x, _ = normalise(midway[...])
    m_out[0] = (x * row(5)[:, :width] + row(6)[:, :width]).astype(BF16)

    def to_pair(src, dst, n):
        copy = pltpu.make_async_remote_copy(
            src_ref=src,
            dst_ref=dst,
            send_sem=send_sem.at[4, n],
            recv_sem=recv_sem.at[4, n],
            device_id=peer_at(t=1),
            device_id_type=MESH,
        )
        copy.start()
        return copy

    rows_sent = to_pair(m_out.at[0], m_out.at[1], 0)
    loads[2]()

    def up(side):
        for start, stop in tiles_of(M_COLS, 256):
            lanes = slice(start, stop)
            u = matmul(m_out[side], mlp[0, :, lanes], (1, 0)) + bias_up[0:1, lanes]
            g, d = gelu_and_slope(u)
            g_out[side, :, lanes] = g.astype(BF16)
            d_out[side, :, lanes] = d.astype(BF16)

    up(0)
    rows_sent.wait()
    up(1)
    loads[3]()
    for start, stop in tiles_of(width, 256):
        part[:, start:stop] = matmul(g_out[1], mlp[1, start:stop, :], (1, 1)).astype(BF16)
    part_sent = to_pair(part, part_got, 1)
    for start, stop in tiles_of(width, 256):
        resid_out[:, start:stop] = matmul(g_out[0], mlp[1, start:stop, :], (1, 1))
    part_sent.wait()
    resid_out[...] += midway[...] + part_got[...].astype(F32) + row(7)[:, :width]
    if carry:
        ring_t.finish()
        ring_z.finish()
        ring_m.finish()
        for ring in (ring_t, ring_z, ring_m):
            ring.close()
        copies.here(next_attn.at[0, :, pl.ds(PADDED - 128, 128)], next_tail)()
        copies.close()


def forward_layer(resid, vec, bias_up, mask, weights, pieces, collective):
    shape = jax.ShapeDtypeStruct
    vmem = pl.BlockSpec(memory_space=pltpu.VMEM)
    hbm = pl.BlockSpec(memory_space=pl.ANY)
    rows, width = resid.shape
    carry = pieces is not None
    low = lambda *dims: pltpu.VMEM(dims, BF16)
    out_shape = [
        shape((rows, width), F32),
        shape((rows, width), BF16),
        shape((512, WINDOW), BF16),
        shape((512, WINDOW), BF16),
        shape((512, WINDOW), BF16),
        shape((512, WINDOW), F32),
        shape((512, 128), F32),
        shape((rows, PADDED), BF16),
        shape((rows, width), F32),
        shape((2, rows, width), BF16),
        shape((2, rows, M_COLS), BF16),
        shape((2, rows, M_COLS), BF16),
    ]
    scratch = [
        low(2, 4 * BLOCK, 2 * PADDED),
        low(2, 4 * BLOCK, M_COLS),
        low(rows, PADDED),
        low(rows, PADDED),
        low(rows, PADDED),
        low(512, WINDOW),
        low(GROUP, 64, WINDOW),
        low(rows, width),
        low(rows, width),
        pltpu.SemaphoreType.DMA((4,)),
        pltpu.SemaphoreType.DMA((4,)),
        pltpu.SemaphoreType.DMA((5, GROUP)),
        pltpu.SemaphoreType.DMA((5, GROUP)),
    ]
    if carry:
        out_shape += [shape(w.shape, w.dtype) for w in weights]
        out_shape += [shape((4 * BLOCK, 128), BF16)]
        scratch += [pltpu.SemaphoreType.DMA((40,))] * 2
    results = pl.pallas_call(
        functools.partial(forward_kernel, carry=carry),
        out_shape=out_shape,
        in_specs=[vmem] * 4 + [hbm] * (4 if carry else 2),
        out_specs=[vmem] * 12 + [hbm] * (3 if carry else 0),
        scratch_shapes=scratch,
        compiler_params=pltpu.CompilerParams(
            collective_id=collective, has_side_effects=True, vmem_limit_bytes=56 * 2**20
        ),
    )(resid, vec, bias_up, mask, *weights, *(pieces or ()))
    return results[:12], tuple(results[12:])


def norm_back(inputs, gain, back):
    x, scale = normalise(inputs)
    e = back * gain
    grad = scale * (
        e - jnp.mean(e, 1, keepdims=True) - x * jnp.mean(e * x, 1, keepdims=True)
    )
    return grad, jnp.sum(back * x, 0, keepdims=True), jnp.sum(back, 0, keepdims=True)


def backward_kernel(*refs, carry):
    (
        grad, vec, mask, layer_in, midway, d_in, q_all, k_all, v_all, o_all, log_total, attn_in, mlp_in,
    ) = refs[:13]
    refs = refs[13:]
    if carry:
        attn_sum, mlp_sum = refs[:2]
        refs = refs[2:]
    grad_out, dy, du, dz, dq, dk, dv, small, bias_back = refs[:9]
    refs = refs[9:]
    if carry:
        attn_near, mlp_near = refs[:2]
        refs = refs[2:]
    (
        attn, mlp, part, part_got, through, do, do_all, dq_low, dk_low, dv_low, dq_landed, dk_landed, dv_landed,
        dk_sum, dv_sum, load_sem, local_sem, send_sem, recv_sem,
    ) = refs[:19]
    me = group_place()
    greet([dict(x=1), dict(x=-1)] if carry else [], me)
    width = grad.shape[1]
    dy[0] = grad[...].astype(BF16)

    def to_pair(src, dst, n):
        copy = pltpu.make_async_remote_copy(
            src_ref=src,
            dst_ref=dst,
            send_sem=send_sem.at[4, n],
            recv_sem=recv_sem.at[4, n],
            device_id=peer_at(t=1),
            device_id_type=MESH,
        )
        copy.start()
        return copy

    rows_sent = to_pair(dy.at[0], dy.at[1], 0)
    loads = []
    for n, (src, dst) in enumerate(
        [(mlp_in.at[1], mlp.at[1]), (mlp_in.at[0], mlp.at[0]), (attn_in.at[1], attn.at[1]), (attn_in.at[0], attn.at[0])]
    ):
        copy = pltpu.make_async_copy(src, dst, load_sem.at[n])
        copy.start()
        loads.append(copy.wait)
    if carry:
        attn_via, attn_stage, mlp_via, mlp_stage = refs[19:23]
        copies = Copies(*refs[23:25])
        ring_a = attn_ring(copies, attn_sum, attn_near, attn_via, attn_stage)
        ring_m = mlp_ring(copies, mlp_sum, mlp_near, mlp_via, mlp_stage)
        ring_a.start()
        ring_m.start()
    loads[0]()

    def hidden_back(side):
        for start, stop in tiles_of(M_COLS, 256):
            lanes = slice(start, stop)
            back = matmul(dy[side], mlp[1, :, lanes], (1, 0)) * d_in[side, :, lanes].astype(F32)
            du[side, :, lanes] = back.astype(BF16)

    hidden_back(0)
    rows_sent.wait()
    hidden_back(1)
    loads[1]()
    for start, stop in tiles_of(width, 256):
        part[:, start:stop] = matmul(du[1], mlp[0, start:stop, :], (1, 1)).astype(BF16)
    part_sent = to_pair(part, part_got, 1)
    for start, stop in tiles_of(width, 256):
        through[:, start:stop] = matmul(du[0], mlp[0, start:stop, :], (1, 1))
    part_sent.wait()
    dm = through[...] + part_got[...].astype(F32)
    step, gain, shift = norm_back(midway[...], vec[5:6, :width], dm)
    small[5:6, :] = gain
    small[6:7, :] = shift
    through[...] = grad[...] + step
    dz[...] = jnp.zeros_like(dz)
    dz[:, :width] = through[...].astype(BF16)
    do[...] = jnp.zeros_like(do)
    loads[2]()
    for start, stop in tiles_of(width, 256):
        do[:, start:stop] = matmul(dz[...], attn[1, start:stop, PADDED:], (1, 1)).astype(BF16)
    exchanged = to_heads(
        me, (do,), (do_all,), local_sem.at[3:4], send_sem.at[3:4], recv_sem.at[3:4]
    )
    dq_low[...] = jnp.zeros_like(dq_low)
    dk_low[...] = jnp.zeros_like(dk_low)
    dv_low[...] = jnp.zeros_like(dv_low)
    low_sum = lambda value: jnp.sum(value.astype(F32), 0, keepdims=True)
    small[4:5, :] = low_sum(dz[:, :width])
    small[7:8, :] = low_sum(dy[0])
    bias_back[...] = jnp.broadcast_to(low_sum(du[0]) + low_sum(du[1]), bias_back.shape)
    if carry:
        ring_a.forward()
    for copy in exchanged:
        copy.wait()
    for head in range(SLOTS):
        lanes = slice(head * HEAD, head * HEAD + HEAD)
        keys, values = k_all[:, lanes], v_all[:, lanes]
        dk_sum[...] = jnp.zeros_like(dk_sum)
        dv_sum[...] = jnp.zeros_like(dv_sum)
        for start in range(0, 512, CHUNK):
            rows, reach = slice(start, start + CHUNK), start + CHUNK
            queries = q_all[rows, lanes] * 0.125
            grads = do_all[rows, lanes]
            scores = matmul(queries, keys[:reach], (1, 1)) + mask[rows, :reach]
            probs = jnp.exp(scores - log_total[rows, head : head + 1])
            probs_back = matmul(grads, values[:reach], (1, 1))
            delta = jnp.sum(grads.astype(F32) * o_all[rows, lanes], 1, keepdims=True)
            scores_back = (probs * (probs_back - delta)).astype(BF16)
            dq_low[rows, lanes] = (matmul(scores_back, keys[:reach], (1, 0)) * 0.125).astype(BF16)
            dk_sum[:reach] += matmul(scores_back, queries, (0, 0))
            dv_sum[:reach] += matmul(probs.astype(BF16), grads, (0, 0))
        dk_low[:, lanes] = dk_sum[...].astype(BF16)
        dv_low[:, lanes] = dv_sum[...].astype(BF16)
        if carry and head == 2:
            ring_m.forward()
    exchanged = to_rows(
        me,
        (dq_low, dk_low, dv_low),
        (dq_landed, dk_landed, dv_landed),
        local_sem,
        send_sem,
        recv_sem,
    )
    loads[3]()
    for copy in exchanged:
        copy.wait()
    side_by_side(dq_landed, dq)
    side_by_side(dk_landed, dk)
    side_by_side(dv_landed, dv)
    small[2:3, :] = low_sum(dq[:, :width])
    small[3:4, :] = low_sum(dv[:, :width])
    for start, stop in tiles_of(width, 256):
        back = matmul(dq[...], attn[0, start:stop, :PADDED], (1, 1))
        back += matmul(dk[...], attn[0, start:stop, PADDED:], (1, 1))
        grad_out[:, start:stop] = back + matmul(dv[...], attn[1, start:stop, :PADDED], (1, 1))
    step, gain, shift = norm_back(layer_in[...], vec[0:1, :width], grad_out[...])
    small[0:1, :] = gain
    small[1:2, :] = shift
    grad_out[...] = through[...] + step
    if carry:
        ring_a.land()
        ring_m.land()
        copies.close()


def backward_layer(grad, vec, mask, kept, weights, sums, collective):
    shape = jax.ShapeDtypeStruct
    vmem = pl.BlockSpec(memory_space=pltpu.VMEM)
    hbm = pl.BlockSpec(memory_space=pl.ANY)
    rows, width = grad.shape
    carry = sums is not None
    low = lambda *dims: pltpu.VMEM(dims, BF16)
    out_shape = [
        shape((rows, width), F32),
        shape((2, rows, width), BF16),
        shape((2, rows, M_COLS), BF16),
        *[shape((rows, PADDED), BF16)] * 4,
        shape((8, width), F32),
        shape((8, M_COLS), F32),
    ]
    scratch = [
        low(2, 4 * BLOCK, 2 * PADDED),
        low(2, 4 * BLOCK, M_COLS),
        low(rows, width),
        low(rows, width),
        pltpu.VMEM((rows, width), F32),
        low(rows, PADDED),
        *[low(512, WINDOW)] * 4,
        *[low(GROUP, 64, WINDOW)] * 3,
        *[pltpu.VMEM((512, HEAD), F32)] * 2,
        pltpu.SemaphoreType.DMA((4,)),
        pltpu.SemaphoreType.DMA((4,)),
        pltpu.SemaphoreType.DMA((5, GROUP)),
        pltpu.SemaphoreType.DMA((5, GROUP)),
    ]
    if carry:
        out_shape += [shape((2, 4 * BLOCK, PIECE), BF16), shape((2, BLOCK, M_COLS), BF16)]
        scratch += [low(2, 2 * BLOCK, PIECE)] * 2 + [low(2, NEAR, M_COLS)] * 2
        scratch += [pltpu.SemaphoreType.DMA((16,))] * 2
    results = pl.pallas_call(
        functools.partial(backward_kernel, carry=carry),
        out_shape=out_shape,
        in_specs=[vmem] * 11 + [hbm] * (4 if carry else 2),
        out_specs=[vmem] * 9 + [hbm] * (2 if carry else 0),
        scratch_shapes=scratch,
        compiler_params=pltpu.CompilerParams(
            collective_id=collective, has_side_effects=True, vmem_limit_bytes=58 * 2**20
        ),
    )(grad, vec, mask, *kept, *weights, *(sums or ()))
    return results[:9], tuple(results[9:])


def body(tokens, qkv_weight, out_weight, up_weight, down_weight, vectors, segments, cotangent):
    micro_count, row_count, width = tokens.shape
    layers = qkv_weight.shape[0]
    hidden_half = up_weight.shape[2]
    total_rows = micro_count * row_count
    at = places()
    docs = jnp.pad(segments, ((0, 8 - micro_count), (0, 128 - row_count)))
    *first, tail, q_next, mt_next, docs = gather_first(
        [
            shard_rows(qkv_weight[l], out_weight[l], up_weight[l], down_weight[l], vectors[l], at["z"])
            for l in range(layers)
        ],
        docs,
        3,
    )
    bias = score_bias(docs)
    weights = [tuple(first)]
    residual = tokens.reshape(total_rows, width).astype(F32)
    memory = []
    for l in range(layers):
        vec = tail[:, width - PADDED + 128 :][:, :12].T.astype(F32)
        bias_up = lax.dynamic_slice_in_dim(vec[8:].reshape(-1), at["t"] * hidden_half, hidden_half)
        vec = jnp.pad(vec, ((0, 4), (0, PADDED - width)))
        kept, following = forward_layer(
            residual,
            vec,
            jnp.broadcast_to(bias_up, (8, hidden_half)),
            bias,
            weights[l],
            (q_next, mt_next) if l == 0 else None,
            5 + l,
        )
        if l == 0:
            *following, tail = following
            weights.append(tuple(following))
        memory.append((vec, residual, *kept[1:]))
        residual = kept[0]
    result = residual
    gradient = cotangent.reshape(total_rows, width)
    sums = [None] * layers
    near = None
    for l in reversed(range(layers)):
        vec, layer_in, normed, *saved, o, midway, m, g, d = memory[l]
        kept, passed = backward_layer(
            gradient,
            vec,
            bias,
            (layer_in, midway, d, *saved),
            weights[l],
            sums[1] if l == 0 else None,
            7 + l,
        )
        near = passed or near
        gradient, dy, du, dz, dq, dk, dv, small, bias_back = kept
        bias_back = lax.dynamic_update_slice_in_dim(
            jnp.zeros((2 * hidden_half,), F32), bias_back[0], at["t"] * hidden_half, 0
        )
        vec_back = jnp.concatenate([small, bias_back.reshape(-1, width)], 0)
        sums[l] = chip_sums(
            at,
            (
                normed, dq, dk, dv, o[:, :width], dz, m.reshape(-1, width),
                du.reshape(-1, hidden_half), dy.reshape(-1, width), g.reshape(-1, hidden_half), vec_back,
            ),
        )
    parts = reduce_layers(sums, near, 4)
    totals = [owned_gradients(parts[l], width) for l in range(layers)]
    stacked = [jnp.stack([totals[l][n] for l in range(layers)]) for n in range(5)]
    shape = (micro_count, row_count, width)
    return (result.reshape(shape), gradient.reshape(shape), *stacked)


def solution(mesh):
    return jax.shard_map(
        body,
        mesh=mesh,
        in_specs=(
            P(None, ("dp", "ctx", "tensor"), None),
            P(None, "dp", None),
            P(None, "dp", None),
            P(None, "dp", "tensor"),
            P(None, "dp", "tensor"),
            P(None, None, "dp"),
            P(None, ("dp", "ctx", "tensor")),
            P(None, ("dp", "ctx", "tensor"), None),
        ),
        out_specs=(
            P(None, ("dp", "ctx", "tensor"), None),
            P(None, ("dp", "ctx", "tensor"), None),
            P(None, "dp", None),
            P(None, "dp", None),
            P(None, "dp", "tensor"),
            P(None, "dp", "tensor"),
            P(None, None, "dp"),
        ),
        check_vma=False,
    )
```

time: 777 us -> 599 us (0.77)
  Pallas kernels: 270 us -> 500 us
  waiting for transfers between devices: 124 us -> 1.79 us
  matrix products: 147 us -> 43.7 us
  starting transfers between devices: 93.2 us -> 1.18 us
  local copies, waits for them, and re-layouts: 74.5 us -> 33.8 us
  other arithmetic: 35.1 us -> 10.4 us
  blocking collectives: 18.4 us -> 0 us
    pallas_call x5 -> x6, Pallas kernels: 270 us -> 500 us  [the longest x2 150 us: forward_layer(): pl.pallas_call(functools.partial(forward_kernel, carry=carry), out_shape=...]
    ppermute x70 -> x4, waiting for transfers between devices: 124 us -> 1.79 us  [shifted(): return lax.ppermute(value, ('dp', 'ctx', 'tensor'), pairs)]
    dot_general x28 -> x0, matrix products: 106 us -> none  [the longest x14 58.9 us: dot(): return jnp.dot(a, b, preferred_element_type=F32)]
    ppermute x70 -> x4, starting transfers between devices: 93.2 us -> 1.18 us  [shifted(): return lax.ppermute(value, ('dp', 'ctx', 'tensor'), pairs)]
    all_gather x1 -> x0, blocking collectives: 18.4 us -> none  [score_bias(): lax.all_gather(segments.astype(BF16), ('ctx', 'tensor'), axis=1, tiled=True)]
    unnamed x216 -> x88, local copies, waits for them, and re-layouts: 31.7 us -> 16.1 us
    convert_element_type x8 -> x0, local copies, waits for them, and re-layouts: 9.75 us -> none  [the longest x2 3.68 us: body(): got = shifted(contract_cols(du_peer, mlp_w[0]).astype(BF16), t=1)]
    reduce_sum x18 -> x0, other arithmetic: 9.55 us -> none  [the longest x8 3.89 us: body(): down_rows = lambda v: jnp.sum(v.astype(F32), 0)[:width]]
  transfers between devices with their start and end apart: 70 -> 4, of which waited for: 27 -> 2; matrix products, arithmetic and copies ran while one was open for 26% -> 5% of each run, Pallas kernels for 11% -> 0%
where the time goes in v3:
time: 599 us; the launch traced here: 593 us
  Pallas kernels  500 us (83%)
  matrix products  43.7 us (7%)
  local copies, waits for them, and re-layouts  33.8 us (6%)
  other arithmetic  10.4 us (2%)
    pallas_call x2, Pallas kernels, forward_layer(): pl.pallas_call(functools.partial(forward_kernel, carry=carry), out_shape=...  150 us
    pallas_call x1, Pallas kernels, reduce_layers(): pl.pallas_call(reduce_kernel, out_shape=jax.ShapeDtypeStruct((2, 4, 2, 2,...  141 us
    pallas_call x2, Pallas kernels, backward_layer(): pl.pallas_call(functools.partial(backward_kernel, carry=carry), out_shape...  127 us
    pallas_call x1, Pallas kernels, gather_first(): pl.pallas_call(gather_kernel, out_shape=[shape((2, 4 * BLOCK, 2 * PADDED)...  81.7 us
    dot_general x8, matrix products, contract_rows(): lax.dot_general(a, b, (((0,), (0,)), ((), ())), preferred_element_type=F32)  43.7 us
    unnamed x88, local copies, waits for them, and re-layouts  16.1 us
  transfers between devices with their start and end apart: 4, of which 2 were waited for; matrix products, arithmetic and copies ran while one was open for 5% of the time, Pallas kernels for 0%

profile of v3, /device:TPU:0, one launch (start us, length us, event | category | flops | bytes accessed | tf_op | source)
XLA Modules:
  0.0 592.8 jit_solution(11817329772676810448)
XLA Ops:
  0.6 3.0 fusion.98
  3.7 0.2 copy_bitcast_fusion
  4.0 0.4 copy-done.36
  4.5 0.2 copy-done.15
  4.7 0.4 fusion.103
  6.0 0.4 copy-done.13
  6.5 0.5 copy-done.11
  6.9 0.8 fusion.100
  7.8 0.2 copy-done.12
  8.0 0.8 fusion.99
  9.0 0.5 copy-done.37
  9.6 0.2 slice-done
  9.9 0.8 slice-done.1
  10.7 81.7 %shard_map.135 = (bf16[2,1088,2304]{2,1,0:T(8,128)(2,1)}, bf16[2,1088,2176]{2,1,0:T(8,128)(2,1)S(1)}, bf16[1088,128]{1,0:T(8,128)(2,1)S(1)}, bf16[272,512]{1,0:T...) custom-call(bf16[2,80,512]{2,1,0:T(8,128)(2,1)S(1)} %constant_dynamic-slice_fusion.2.q0, ...), custom_call_target="tpu_custom_call" | custom-call | tf_op jit(solution)/shard_map/pallas_call | solution.py:271
  92.4 3.5 copy-done
  96.0 1.1 copy-done.1
  97.0 0.7 copy-done.2
  97.8 1.2 fusion.57.refs_3_.refs_2_
  99.0 0.2 copy.73
  99.3 0.6 pad.45.refs_1_
  100.0 0.9 bitcast_convert_fusion.refs_0_.refs_3_
  100.9 0.6 broadcast_in_dim.16.refs_2_
  101.5 91.5 %shard_map.136 = (f32[128,1088]{1,0:T(8,128)}, bf16[128,1088]{1,0:T(8,128)(2,1)}, bf16[512,384]{1,0:T(8,128)(2,1)}, bf16[512,384]{1,0:T(8,128)(2,1)}, bf16[512,3...) custom-call(f32[128,1088]{1,0:T(8,128)} %bitcast_convert_fusion.refs, ...), custom_call_target="tpu_custom_call" | custom-call | tf_op jit(solution)/shard_map/pallas_call | solution.py:896
  193.0 1.2 copy.74
  194.4 0.6 pad.46.refs_1_
  195.0 0.6 broadcast_in_dim.19.refs_2_
  195.6 58.4 %shard_map.137 = (f32[128,1088]{1,0:T(8,128)}, bf16[128,1088]{1,0:T(8,128)(2,1)}, bf16[512,384]{1,0:T(8,128)(2,1)}, bf16[512,384]{1,0:T(8,128)(2,1)}, bf16[512,3...) custom-call(f32[128,1088]{1,0:T(8,128)} %get-tuple-element.66.refs_0, ...), custom_call_target="tpu_custom_call" | custom-call | tf_op jit(solution)/shard_map/pallas_call | solution.py:896
  254.1 51.1 %shard_map.138 = (f32[128,1088]{1,0:T(8,128)}, bf16[2,128,1088]{2,1,0:T(8,128)(2,1)}, bf16[2,128,2176]{2,1,0:T(8,128)(2,1)}, bf16[128,1152]{1,0:T(8,128)(2,1)}, ...) custom-call(f32[128,1088]{1,0:T(8,128)} %bitcast.144, ...), custom_call_target="tpu_custom_call" | custom-call | tf_op jit(solution)/shard_map/pallas_call | solution.py:1095
  305.3 4.9 fusion
  310.2 0.9 slice_reduce_fusion.1
  311.1 0.3 dynamic_update_slice.6
  311.5 0.2 copy.75
  311.8 1.0 broadcast_select_fusion.11
  312.8 1.9 broadcast_select_fusion.7
  314.7 0.9 broadcast_select_fusion.6
  315.6 5.0 fusion.2
  320.6 0.7 collective-permute-start
  321.2 1.9 broadcast_select_fusion.9
  323.2 6.3 %add_convert_fusion.3.refs_14_.mlp1 = bf16[1088,2176]{1,0:T(8,128)(2,1)} fusion(bf16[1088,2176]{1,0:T(8,128)(2,1)} %collective-permute-done.1, bf16[2,128,2176]{2,1,0:T(8,128)(2,1)S(1)} %copy-done.9, bf16[2,128,2176]{2,1,0:T(8,128)(2,1)S(1)} %copy-done.8, pred[]{:T(512)S(6)} %eq.25, bf16[2,128,1088]{2,1,0:T(8,128)(2,1)S(1)} %copy-done.4, ...), kind=kOutput, calls=%fused_computation.19 | convolution fusion | flops 1220091904 | bytes 12812289 | tf_op jit(solution)/shard_map/dot_general | solution.py:323
  329.6 7.2 %add_convert_fusion.1.refs_13_.attn1 = bf16[1088,2304]{1,0:T(8,128)(2,1)} fusion(bf16[1088,2304]{1,0:T(8,128)(2,1)} %collective-permute-done, f32[1088,12]{1,0:T(8,128)S(1)} %bitcast.148, f32[]{:T(128)S(6)} %select_n.153, bf16[128,1152]{1,0:T(8,128)(2,1)S(1)} %copy-done.33, bf16[128,1152]{1,0:T(8,128)(2,1)S(1)} %copy-done.32, ...), kind=kOutput, calls=%fused_computation.17 | convolution fusion | flops 1301823488 | bytes 11226116 | tf_op jit(solution)/shard_map/dot_general | solution.py:323
  336.8 76.1 %shard_map.139 = (f32[128,1088]{1,0:T(8,128)}, bf16[2,128,1088]{2,1,0:T(8,128)(2,1)}, bf16[2,128,2176]{2,1,0:T(8,128)(2,1)}, bf16[128,1152]{1,0:T(8,128)(2,1)}, ...) custom-call(f32[128,1088]{1,0:T(8,128)} %get-tuple-element.78.refs_0, ...), custom_call_target="tpu_custom_call" | custom-call | tf_op jit(solution)/shard_map/pallas_call | solution.py:1095
  412.9 4.9 fusion.1
  417.8 1.0 slice_reduce_fusion
  418.8 0.3 dynamic_update_slice.7
  419.2 0.2 copy.78
  419.5 1.1 broadcast_select_fusion.3
  420.7 3.7 fusion.3
  424.4 0.5 collective-permute-start.2
  425.0 1.1 collective-permute-done.3
  426.1 6.2 %add_convert_fusion.2.mlp0 = bf16[1088,2176]{1,0:T(8,128)(2,1)} fusion(bf16[1088,2176]{1,0:T(8,128)(2,1)} %collective-permute-done.3, bf16[2,128,2176]{2,1,0:T(8,128)(2,1)S(1)} %copy-done.10, bf16[2,128,2176]{2,1,0:T(8,128)(2,1)S(1)} %copy-done.7, pred[]{:T(512)S(6)} %eq.25, bf16[2,128,1088]{2,1,0:T(8,128)(2,1)S(1)} %copy-done.3, ...), kind=kOutput, calls=%fused_computation.18 | convolution fusion | flops 1220091904 | bytes 12812289 | tf_op jit(solution)/shard_map/dot_general | solution.py:323
  432.3 0.6 collective-permute-done.2
  432.9 5.6 add_convert_fusion.attn0
  438.5 141.2 %shard_map.140 = bf16[2,4,2,2,80,640]{5,4,3,2,1,0:T(8,128)(2,1)} custom-call(bf16[1088,2304]{1,0:T(8,128)(2,1)} %add_convert_fusion.attn0, bf16[1088,2176]{1,0:T(8,128)(2,1)} %add_convert_fusion.2.mlp0, bf16[1088,2304]{1,0:T(8,128)(2,1)} %add_convert_fusion.1.refs_13_.attn1, bf16[1088,2176]{1,0:T(8,128)(2,1)} %add_convert_fusion.3.refs_14_.mlp1, ...), custom_call_target="tpu_custom_call" | custom-call | tf_op jit(solution)/shard_map/pallas_call | solution.py:556
  579.8 2.2 slice_bitcast_fusion.1
  582.7 1.6 copy.86
  584.4 1.6 copy.85
  586.2 1.1 copy.84
  587.4 0.2 concatenate.234
  587.6 0.2 concatenate.241
  587.8 0.1 maximum_convert_fusion
  587.9 2.2 copy.83
  590.1 0.6 maximum_convert_fusion.4
  590.7 0.8 copy.113
  591.5 0.8 copy.114
  (130 shorter events, 3.4 us)
Async XLA Ops:
  3.7 0.7 copy-start.36
  3.7 1.0 copy-start.15
  5.5 0.9 copy-start.13
  5.9 1.1 copy-start.11
  6.4 1.4 copy-start.14
  6.9 1.1 copy-start.12
  8.8 0.7 copy-start.37
  8.9 0.9 slice-start
  9.8 0.9 slice-start.1
  92.4 3.5 copy-start
  96.0 1.1 copy-start.1
  97.0 0.7 copy-start.2
  97.7 2.2 copy-start.20
  254.1 51.1 %copy-start.4 = (bf16[2,128,1088]{2,1,0:T(8,128)(2,1)S(1)}, bf16[2,128,1088]{2,1,0:T(8,128)(2,1)}, u32[]{:S(2)}) copy-start(bf16[2,128,1088]{2,1,0:T(8,128)(2,1)} %get-tuple-element.94) | copy-start | bytes 1671172
  254.1 51.1 %copy-start.8 = (bf16[2,128,2176]{2,1,0:T(8,128)(2,1)S(1)}, bf16[2,128,2176]{2,1,0:T(8,128)(2,1)}, u32[]{:S(2)}) copy-start(bf16[2,128,2176]{2,1,0:T(8,128)(2,1)} %get-tuple-element.97) | copy-start | bytes 3342340
  305.2 6.3 %copy-start.35 = (f32[8,1088]{1,0:T(8,128)S(1)}, f32[8,1088]{1,0:T(8,128)}, u32[]{:S(2)}) copy-start(f32[8,1088]{1,0:T(8,128)} %get-tuple-element.92) | copy-start | bytes 104452
  305.3 6.5 %copy-start.23 = (bf16[128,1088]{1,0:T(8,128)(2,1)S(1)}, bf16[128,1088]{1,0:T(8,128)(2,1)}, u32[]{:S(2)}) copy-start(bf16[128,1088]{1,0:T(8,128)(2,1)} %get-tuple-element.86) | copy-start | bytes 835588
  305.3 6.5 %copy-start.28 = (bf16[128,1152]{1,0:T(8,128)(2,1)S(1)}, bf16[128,1152]{1,0:T(8,128)(2,1)}, u32[]{:S(2)}) copy-start(bf16[128,1152]{1,0:T(8,128)(2,1)} %get-tuple-element.87) | copy-start | bytes 884740
  310.1 13.0 %collective-permute-start.1 = (bf16[1088,2176]{1,0:T(8,128)(2,1)}, bf16[1088,2176]{1,0:T(8,128)(2,1)}, u32[]{:S(2)}, u32[]{:S(2)}) collective-permute-start(bf16[1088,2176]{1,0:T(8,128)(2,1)} %fusion), channel_id=1, source_target_pairs={{0,8},{1,9},{2,10},{3,11},{4,12},{5,13},{6,14},{7,15},{8,0},{9,1},... | collective-permute-start | bytes 14204936 | tf_op jit(solution)/shard_map/ppermute | solution.py:41
  311.5 3.2 copy-start.29
  311.5 3.2 copy-start.30
  311.8 3.8 copy-start.18
  315.6 7.6 %copy-start.9 = (bf16[2,128,2176]{2,1,0:T(8,128)(2,1)S(1)}, bf16[2,128,2176]{2,1,0:T(8,128)(2,1)}, u32[]{:S(2)}) copy-start(bf16[2,128,2176]{2,1,0:T(8,128)(2,1)} %get-tuple-element.96) | copy-start | bytes 3342340
  320.6 2.6 copy-start.5
  320.6 9.0 %collective-permute-start = (bf16[1088,2304]{1,0:T(8,128)(2,1)}, bf16[1088,2304]{1,0:T(8,128)(2,1)}, u32[]{:S(2)}, u32[]{:S(2)}) collective-permute-start(bf16[1088,2304]{1,0:T(8,128)(2,1)} %fusion.2), channel_id=1, source_target_pairs={{0,8},{1,9},{2,10},{3,11},{4,12},{5,13},{6,14},{7,15},{8,0},{9,1},... | collective-permute-start | bytes 15040520 | tf_op jit(solution)/shard_map/ppermute | solution.py:41
  323.2 6.4 %copy-start.19 = (f32[12,1088]{0,1:T(8,128)S(1)}, f32[12,1088]{0,1:T(8,128)}, u32[]{:S(2)}) copy-start(f32[12,1088]{0,1:T(8,128)} %copy-done.18) | copy-start | bytes 156676
  323.2 6.4 %copy-start.24 = (bf16[128,1088]{1,0:T(8,128)(2,1)S(1)}, bf16[128,1088]{1,0:T(8,128)(2,1)}, u32[]{:S(2)}) copy-start(bf16[128,1088]{1,0:T(8,128)(2,1)} %get-tuple-element.86) | copy-start | bytes 835588
  323.2 6.4 %copy-start.31 = (bf16[128,1088]{1,0:T(8,128)(2,1)S(1)}, bf16[128,1088]{1,0:T(8,128)(2,1)}, u32[]{:S(2)}) copy-start(bf16[128,1088]{1,0:T(8,128)(2,1)} %get-tuple-element.180) | copy-start | bytes 835588
  323.2 6.4 %copy-start.32 = (bf16[128,1152]{1,0:T(8,128)(2,1)S(1)}, bf16[128,1152]{1,0:T(8,128)(2,1)}, u32[]{:S(2)}) copy-start(bf16[128,1152]{1,0:T(8,128)(2,1)} %get-tuple-element.182) | copy-start | bytes 884740
  323.2 6.4 %copy-start.33 = (bf16[128,1152]{1,0:T(8,128)(2,1)S(1)}, bf16[128,1152]{1,0:T(8,128)(2,1)}, u32[]{:S(2)}) copy-start(bf16[128,1152]{1,0:T(8,128)(2,1)} %get-tuple-element.184) | copy-start | bytes 884740
  336.8 76.1 %copy-start.3 = (bf16[2,128,1088]{2,1,0:T(8,128)(2,1)S(1)}, bf16[2,128,1088]{2,1,0:T(8,128)(2,1)}, u32[]{:S(2)}) copy-start(bf16[2,128,1088]{2,1,0:T(8,128)(2,1)} %get-tuple-element.107) | copy-start | bytes 1671172
  336.8 76.1 %copy-start.7 = (bf16[2,128,2176]{2,1,0:T(8,128)(2,1)S(1)}, bf16[2,128,2176]{2,1,0:T(8,128)(2,1)}, u32[]{:S(2)}) copy-start(bf16[2,128,2176]{2,1,0:T(8,128)(2,1)} %get-tuple-element.110) | copy-start | bytes 3342340
  412.9 6.3 %copy-start.34 = (f32[8,1088]{1,0:T(8,128)S(1)}, f32[8,1088]{1,0:T(8,128)}, u32[]{:S(2)}) copy-start(f32[8,1088]{1,0:T(8,128)} %get-tuple-element.105) | copy-start | bytes 104452
  417.8 2.8 copy-start.26
  417.8 2.8 copy-start.27
  417.8 8.3 %collective-permute-start.3 = (bf16[1088,2176]{1,0:T(8,128)(2,1)}, bf16[1088,2176]{1,0:T(8,128)(2,1)}, u32[]{:S(2)}, u32[]{:S(2)}) collective-permute-start(bf16[1088,2176]{1,0:T(8,128)(2,1)} %fusion.1), channel_id=1, source_target_pairs={{0,8},{1,9},{2,10},{3,11},{4,12},{5,13},{6,14},{7,15},{8,0},{9,1},... | collective-permute-start | bytes 14204936 | tf_op jit(solution)/shard_map/ppermute | solution.py:41
  419.2 1.5 copy-start.21
  419.2 1.5 copy-start.25
  420.7 5.3 copy-start.6
  420.7 5.3 copy-start.10
  424.4 8.5 %collective-permute-start.2 = (bf16[1088,2304]{1,0:T(8,128)(2,1)S(1)}, bf16[1088,2304]{1,0:T(8,128)(2,1)S(1)}, u32[]{:S(2)}, u32[]{:S(2)}) collective-permute-start(bf16[1088,2304]{1,0:T(8,128)(2,1)S(1)} %fusion.3), channel_id=1, source_target_pairs={{0,8},{1,9},{2,10},{3,11},{4,12},{5,13},{6,14},{7,15},{8,0},{9,1},... | collective-permute-start | bytes 15040520 | tf_op jit(solution)/shard_map/ppermute | solution.py:41
  425.0 8.0 %copy-start.22 = (bf16[128,1088]{1,0:T(8,128)(2,1)S(1)}, bf16[128,1088]{1,0:T(8,128)(2,1)}, u32[]{:S(2)}) copy-start(bf16[128,1088]{1,0:T(8,128)(2,1)} %get-tuple-element.174) | copy-start | bytes 835588
  587.9 2.8 copy-start.16
  590.1 1.4 copy-start.17

commit v4 on v3

--- a/solution.py
+++ b/solution.py
@@ -66,6 +66,7 @@
     def to(self, peer, src, dst):
         n = self.count
         self.count += 1
+        assert n < self.send_sem.shape[0]
         copy = pltpu.make_async_remote_copy(
             src_ref=src,
             dst_ref=dst,
@@ -81,6 +82,7 @@
     def here(self, src, dst):
         n = self.count
         self.count += 1
+        assert n < self.send_sem.shape[0]
         copy = pltpu.make_async_copy(src, dst, self.send_sem.at[n])
         copy.start()
         return copy.wait
@@ -178,27 +180,31 @@
             wait()
 
 
-def exchange_shards(copies, mine, landed):
+def exchange_shards(copies, mine, landed, lanes=slice(None)):
     c = places()["c"]
+    part = lambda ref, n: ref.at[n, :, lanes]
     waits = [
-        copies.to(peer_at(c=1), mine.at[1 - c], landed.at[1]),
-        copies.to(peer_at(y=1), mine.at[c], landed.at[2]),
-        copies.to(peer_at(y=1, c=1), mine.at[1 - c], landed.at[3]),
+        copies.to(peer_at(c=1), part(mine, 1 - c), part(landed, 1)),
+        copies.to(peer_at(y=1), part(mine, c), part(landed, 2)),
+        copies.to(peer_at(y=1, c=1), part(mine, 1 - c), part(landed, 3)),
     ]
-    waits.append(copies.here(mine.at[c], landed.at[0]))
+    waits.append(copies.here(part(mine, c), part(landed, 0)))
     return waits
 
 
-def assemble(landed, own):
+def assemble(landed, own, begin=0, end=None):
     at = places()
-    width = own.shape[1]
-    for start in range(0, width, 256):
-        lanes = slice(start, min(start + 256, width))
+    end = end or own.shape[1]
+    for start in range(begin, end, 256):
+        lanes = slice(start, min(start + 256, end))
         parts = []
         for j in range(4):
             slot = lax.rem(j // 2 + at["y"], 2) * 2 + lax.rem(j % 2 + at["c"], 2)
             parts.append(landed[slot, :, lanes].astype(F32)[:ROWS])
         own[:, lanes] = jnp.concatenate(parts, 0).astype(BF16)
+
+
+M_CUT = 1152
 
 
 def gather_kernel(
@@ -210,42 +216,49 @@
     copies = Copies(send_sem, recv_sem)
     quarter = pl.ds(pl.multiple_of(places()["z"] * Q_COLS, 128), Q_COLS)
     arrive_q = exchange_shards(copies, q0, q_land.at[0])
-    arrive_mt = exchange_shards(copies, mt0, mt_land.at[0])
+    arrive_m = exchange_shards(copies, mt0, mt_land.at[0], pl.ds(0, M_CUT))
+    arrive_mt = exchange_shards(copies, mt0, mt_land.at[0], pl.ds(M_CUT, M_COLS + T_COLS - M_CUT))
     later = [copies.here(docs, docs_all.at[me])]
     for n in range(1, GROUP):
         later.append(copies.to(member(lax.rem(me + n, GROUP)), docs, docs_all.at[me]))
     arrive_q1 = exchange_shards(copies, q1, q_land.at[1])
     arrive_mt1 = exchange_shards(copies, mt1, mt_land.at[1])
     q = RingX(copies, q_own, attn, quarter, False)
-    m = RingX(copies, mt_own.at[:, pl.ds(0, M_COLS)], mlp, slice(None), True)
+    m_lanes = (pl.ds(0, M_CUT), pl.ds(M_CUT, M_COLS - M_CUT))
+    m = RingX(copies, mt_own.at[:, m_lanes[0]], mlp, m_lanes[0], True)
+    m2 = RingX(copies, mt_own.at[:, m_lanes[1]], mlp, m_lanes[1], True)
     t = RingX(copies, mt_own.at[:, pl.ds(M_COLS, T_COLS)], attn, pl.ds(T_START, T_COLS), True)
     along_z = RingZ(copies, attn)
 
-    def landed(waits, land, own):
+    def landed(waits, land, own, begin=0, end=None):
         for wait in waits:
             wait()
-        assemble(land, own)
+        assemble(land, own, begin, end)
 
     landed(arrive_q, q_land.at[0], q_own)
     q.start()
+    landed(arrive_m, mt_land.at[0], mt_own, 0, M_CUT)
     q.forward()
-    landed(arrive_mt, mt_land.at[0], mt_own)
-    t.start()
     m.start()
+    landed(arrive_mt, mt_land.at[0], mt_own, M_CUT)
     q.finish()
     q.close()
     along_z.start()
-    t.forward()
+    t.start()
+    m2.start()
+    m.forward()
     landed(arrive_q1, q_land.at[1], q_own1)
     later.append(copies.here(q_own1, q_next))
-    m.forward()
-    along_z.forward()
     landed(arrive_mt1, mt_land.at[1], mt_own1)
     later.append(copies.here(mt_own1, mt_next))
-    t.finish()
+    along_z.forward()
+    t.forward()
+    m2.forward()
     m.finish()
     along_z.finish()
-    for ring in (t, m, along_z):
+    t.finish()
+    m2.finish()
+    for ring in (t, m, m2, along_z):
         ring.close()
     later.append(copies.here(attn.at[0, :, pl.ds(PADDED - 128, 128)], vec_tail))
     for wait in later:
@@ -253,9 +266,9 @@
     copies.close()
 
 
-def shard_rows(qkv, out, up, down, vec, z):
+def shard_rows(qkv, out, up, down, extra, z):
     width = out.shape[1]
-    role0 = jnp.concatenate([padded(qkv[:, :width], vec.T), padded(qkv[:, width : 2 * width])], 1)
+    role0 = jnp.concatenate([padded(qkv[:, :width], extra), padded(qkv[:, width : 2 * width])], 1)
     role1 = jnp.concatenate([padded(qkv[:, 2 * width :]), padded(out)], 1)
     attn = jnp.pad(jnp.stack([role0, role1]), ((0, 0), (0, TALL - ROWS), (0, 0)))
     mlp = jnp.pad(jnp.stack([up, down]), ((0, 0), (0, TALL - ROWS), (0, 0)))
@@ -287,8 +300,8 @@
             low(BLOCK, M_COLS + T_COLS),
             low(BLOCK, Q_COLS),
             low(BLOCK, M_COLS + T_COLS),
-            pltpu.SemaphoreType.DMA((64,)),
-            pltpu.SemaphoreType.DMA((64,)),
+            pltpu.SemaphoreType.DMA((80,)),
+            pltpu.SemaphoreType.DMA((80,)),
         ],
         compiler_params=pltpu.CompilerParams(
             collective_id=collective, has_side_effects=True, vmem_limit_bytes=32 * 2**20
@@ -334,8 +347,8 @@
     )
 
 
-def chip_sums(at, operands):
-    a, dq, dk, dv, o, dz, m, du, dy, g, vec = operands
+def attn_sums(at, operands):
+    a, dq, dk, dv, o, dz, vec = operands
     c0 = at["c"] == 0
     width = a.shape[1]
     pick = lambda p, q: jnp.where(c0, p, q)
@@ -347,11 +360,7 @@
     keep = contract_rows(
         jnp.concatenate([a, pick(a, o)], 0), block_diagonal(pick(dq, dv), pick(dk, dz))
     ) + pick(1.0, 0.0) * vec_cols
-    attn = (keep + got.astype(F32)).astype(BF16)
-    give = contract_rows(pick(dy, m), pick(g, du)).astype(BF16)
-    got = shifted(give, c=1)
-    mlp = (contract_rows(pick(m, dy), pick(du, g)) + got.astype(F32)).astype(BF16)
-    return attn, mlp
+    return (keep + got.astype(F32)).astype(BF16)
 
 
 def in_chunks(count, step, do):
@@ -372,14 +381,15 @@
         self.up, self.down = peer_at(**{axis: 1}), peer_at(**{axis: -1})
 
     def start(self):
-        first, last = self.first, self.last
-        far, up, down = self.view(2), self.view(1), self.view(-1)
+        self.start_far()
+        self.start_near()
+
+    def start_far(self):
+        far = self.view(2)
         rest = pl.ds(0, self.counts[1])
-        self.via_up = self.copies.to(self.up, far.at[first], self.via.at[0])
-        self.via_down = self.copies.to(self.down, far.at[last], self.via.at[1, rest])
-        self.near_a = self.copies.to(self.up, up.at[last], self.near.at[0, last])
-        self.near_b = self.copies.to(self.down, down.at[first], self.near.at[1, first])
-        self.parts = (up.at[first], down.at[last])
+        self.via_up = self.copies.to(self.up, far.at[self.first], self.via.at[0])
+        self.via_down = self.copies.to(self.down, far.at[self.last], self.via.at[1, rest])
+        self.parts = (self.view(1).at[self.first], self.view(-1).at[self.last])
         self.staged = []
         if self.stage is not None:
             staged = (self.stage.at[0], self.stage.at[1, rest])
@@ -387,12 +397,24 @@
                 self.staged.append(self.copies.here(src, dst))
             self.parts = staged
 
+    def start_near(self, steps=(0, 1)):
+        if 0 in steps:
+            self.nears = []
+        cut, rest = self.counts
+        for n in steps:
+            for peer, view, side, begin, count in (
+                (self.up, self.view(1), 0, cut, rest),
+                (self.down, self.view(-1), 1, 0, cut),
+            ):
+                half = count // 32 * 16
+                rows = pl.ds(begin, half) if n == 0 else pl.ds(begin + half, count - half)
+                self.nears.append(self.copies.to(peer, view.at[rows], self.near.at[side, rows]))
+
     def forward(self):
         for wait in self.staged:
             wait()
         arrived = (self.via_up, self.via_down)
         ends = ((self.up, 0, self.first), (self.down, 1, self.last))
-        self.nears = [self.near_a, self.near_b]
         for n, (peer, side, rows) in enumerate(ends):
             arrived[n]()
             part = self.parts[n]
@@ -449,8 +471,8 @@
     at = places()
     ring_a = attn_ring(copies, attn0, attn_near, attn_via, attn_stage)
     ring_m = mlp_ring(copies, mlp0, mlp_near, mlp_via, mlp_stage)
-    ring_a.start()
     ring_m.start()
+    ring_a.start_far()
     loads = {}
     for l, (attn, mlp) in ((1, (attn1, mlp1)), (0, (attn0, mlp0))):
         loads[l] = (
@@ -527,23 +549,27 @@
                     rest.append(copies.to(peer_at(z=d), src, dst))
         return rest
 
-    rings, waits, rest = {}, {}, []
+    rings, waits, turned, ends, rest = {}, {}, {}, {}, []
+    order = (1, 0)
     rings[1] = second(1, attn_near1, mlp_near1)
+    ring_a.start_near()
     ring_m.forward()
     ring_a.forward()
     for ring in reversed(rings[1]):
         ring.forward()
-    waits[1] = third(1, rings[1])
-    turned = fourth(1, waits[1])
-    rest += sixth(1, fifth(1, waits[1], turned))
     ring_m.land()
     ring_a.land()
     rings[0] = second(0, attn_near, mlp_near)
+    waits[1] = third(1, rings[1])
+    turned[1] = fourth(1, waits[1])
     for ring in reversed(rings[0]):
         ring.forward()
+    ends[1] = fifth(1, waits[1], turned[1])
     waits[0] = third(0, rings[0])
-    turned = fourth(0, waits[0])
-    rest += sixth(0, fifth(0, waits[0], turned))
+    turned[0] = fourth(0, waits[0])
+    rest += sixth(1, ends[1])
+    ends[0] = fifth(0, waits[0], turned[0])
+    rest += sixth(0, ends[0])
     for wait in rest:
         wait()
     copies.close()
@@ -575,8 +601,8 @@
             low(2, 3, HALF_TALL, PIECE),
             low(2, 2, 2, TALL, PIECE),
             low(2, 2, TALL, PIECE),
-            pltpu.SemaphoreType.DMA((96,)),
-            pltpu.SemaphoreType.DMA((96,)),
+            pltpu.SemaphoreType.DMA((128,)),
+            pltpu.SemaphoreType.DMA((128,)),
         ],
         compiler_params=pltpu.CompilerParams(
             collective_id=collective, has_side_effects=True, vmem_limit_bytes=56 * 2**20
@@ -723,8 +749,8 @@
     ) = refs[:12]
     refs = refs[12:]
     if carry:
-        next_attn, next_mlp, next_tail = refs[:3]
-        refs = refs[3:]
+        next_attn, next_mlp = refs[:2]
+        refs = refs[2:]
     (
         attn, mlp, q, k, v, o_low, o_landed, part, part_got, load_sem, local_sem, send_sem, recv_sem,
     ) = refs[:13]
@@ -756,6 +782,10 @@
         q[:, lanes] = (matmul(a, attn[0, :, lanes], (1, 0)) + vec[2:3, lanes]).astype(BF16)
         k[:, lanes] = matmul(a, attn[0, :, PADDED + start : PADDED + stop], (1, 0)).astype(BF16)
     loads[1]()
+    if carry:
+        ring_q.forward()
+        ring_t.start()
+        ring_m.start()
     for start, stop in tiles_of(PADDED, 384):
         lanes = slice(start, stop)
         v[:, lanes] = (matmul(a, attn[1, :, lanes], (1, 0)) + vec[3:4, lanes]).astype(BF16)
@@ -764,15 +794,11 @@
     o_all[...] = jnp.zeros_like(o_all)
     log_total[...] = jnp.zeros_like(log_total)
     if carry:
-        ring_q.forward()
-        ring_t.start()
-        ring_m.start()
-    for copy in exchanged:
-        copy.wait()
-    if carry:
         ring_q.finish()
         ring_q.close()
         ring_z.start()
+    for copy in exchanged:
+        copy.wait()
     for head in range(SLOTS):
         lanes = slice(head * HEAD, head * HEAD + HEAD)
         keys, values = k_all[:, lanes], v_all[:, lanes]
@@ -787,16 +813,16 @@
             o_all[rows, lanes] = result
             o_low[rows, lanes] = result.astype(BF16)
             log_total[rows, head : head + 1] = top + jnp.log(total)
+        if carry and head == 3:
+            ring_t.forward()
+            ring_m.forward()
     exchanged = to_rows(
         me, (o_low,), (o_landed,), local_sem.at[3:4], send_sem.at[3:4], recv_sem.at[3:4]
     )
     if carry:
-        ring_t.forward()
-        ring_m.forward()
+        ring_z.forward()
     for copy in exchanged:
         copy.wait()
-    if carry:
-        ring_z.forward()
     side_by_side(o_landed, o_out)
     o = o_out[:, :width]
     for start, stop in tiles_of(width, 384):
@@ -849,7 +875,6 @@
         ring_m.finish()
         for ring in (ring_t, ring_z, ring_m):
             ring.close()
-        copies.here(next_attn.at[0, :, pl.ds(PADDED - 128, 128)], next_tail)()
         copies.close()
 
 
@@ -891,13 +916,12 @@
     ]
     if carry:
         out_shape += [shape(w.shape, w.dtype) for w in weights]
-        out_shape += [shape((4 * BLOCK, 128), BF16)]
         scratch += [pltpu.SemaphoreType.DMA((40,))] * 2
     results = pl.pallas_call(
         functools.partial(forward_kernel, carry=carry),
         out_shape=out_shape,
         in_specs=[vmem] * 4 + [hbm] * (4 if carry else 2),
-        out_specs=[vmem] * 12 + [hbm] * (3 if carry else 0),
+        out_specs=[vmem] * 12 + [hbm] * (2 if carry else 0),
         scratch_shapes=scratch,
         compiler_params=pltpu.CompilerParams(
             collective_id=collective, has_side_effects=True, vmem_limit_bytes=56 * 2**20
@@ -917,37 +941,48 @@
 
 def backward_kernel(*refs, carry):
     (
-        grad, vec, mask, layer_in, midway, d_in, q_all, k_all, v_all, o_all, log_total, attn_in, mlp_in,
-    ) = refs[:13]
-    refs = refs[13:]
+        grad, vec, mask, layer_in, midway, d_in, m_in, g_in, q_all, k_all, v_all, o_all, log_total,
+        attn_in, mlp_in,
+    ) = refs[:15]
+    refs = refs[15:]
     if carry:
         attn_sum, mlp_sum = refs[:2]
         refs = refs[2:]
-    grad_out, dy, du, dz, dq, dk, dv, small, bias_back = refs[:9]
-    refs = refs[9:]
+    grad_out, dz, dq, dk, dv, small, bias_back, mlp_total = refs[:8]
+    refs = refs[8:]
     if carry:
         attn_near, mlp_near = refs[:2]
         refs = refs[2:]
     (
         attn, mlp, part, part_got, through, do, do_all, dq_low, dk_low, dv_low, dq_landed, dk_landed, dv_landed,
-        dk_sum, dv_sum, load_sem, local_sem, send_sem, recv_sem,
-    ) = refs[:19]
+        dk_sum, dv_sum, load_sem, local_sem, send_sem, recv_sem, dy, du, mlp_got, turned,
+    ) = refs[:23]
     me = group_place()
-    greet([dict(x=1), dict(x=-1)] if carry else [], me)
+    greet([dict(c=1)] + ([dict(x=1), dict(x=-1)] if carry else []), me)
     width = grad.shape[1]
     dy[0] = grad[...].astype(BF16)
 
-    def to_pair(src, dst, n):
+    def to_pair(src, dst, n, peer=peer_at(t=1)):
         copy = pltpu.make_async_remote_copy(
             src_ref=src,
             dst_ref=dst,
             send_sem=send_sem.at[4, n],
             recv_sem=recv_sem.at[4, n],
-            device_id=peer_at(t=1),
+            device_id=peer,
             device_id_type=MESH,
         )
         copy.start()
         return copy
+
+    def mlp_products(up, write):
+        for side in range(2):
+            left = jnp.where(up, m_in[side].astype(F32), dy[side].astype(F32))
+            turned[:, side * 128 : side * 128 + 128] = jnp.transpose(left).astype(BF16)
+        for start, stop in tiles_of(M_COLS, 256):
+            lanes = slice(start, stop)
+            right = [jnp.where(up, du[n, :, lanes].astype(F32), g_in[n, :, lanes].astype(F32)) for n in range(2)]
+            right = jnp.concatenate(right, 0).astype(BF16)
+            write(lanes, matmul(turned[...], right, (1, 0)))
 
     rows_sent = to_pair(dy.at[0], dy.at[1], 0)
     loads = []
@@ -958,11 +993,12 @@
         copy.start()
         loads.append(copy.wait)
     if carry:
-        attn_via, attn_stage, mlp_via, mlp_stage = refs[19:23]
-        copies = Copies(*refs[23:25])
+        attn_via, attn_stage, mlp_via, mlp_stage = refs[23:27]
+        copies = Copies(*refs[27:29])
         ring_a = attn_ring(copies, attn_sum, attn_near, attn_via, attn_stage)
         ring_m = mlp_ring(copies, mlp_sum, mlp_near, mlp_via, mlp_stage)
-        ring_a.start()
+        ring_a.start_far()
+        ring_a.start_near((0,))
         ring_m.start()
     loads[0]()
 
@@ -1003,10 +1039,17 @@
     small[4:5, :] = low_sum(dz[:, :width])
     small[7:8, :] = low_sum(dy[0])
     bias_back[...] = jnp.broadcast_to(low_sum(du[0]) + low_sum(du[1]), bias_back.shape)
-    if carry:
-        ring_a.forward()
+
+    def give(lanes, value):
+        mlp[0, :, lanes] = value.astype(BF16)
+
+    mlp_products(places()["c"] == 1, give)
+    mlp_sent = to_pair(mlp.at[0], mlp_got, 2, peer_at(c=1))
     for copy in exchanged:
         copy.wait()
+    if carry:
+        ring_a.start_near((1,))
+        ring_a.forward()
     for head in range(SLOTS):
         lanes = slice(head * HEAD, head * HEAD + HEAD)
         keys, values = k_all[:, lanes], v_all[:, lanes]
@@ -1037,6 +1080,14 @@
         recv_sem,
     )
     loads[3]()
+    mlp_sent.wait()
+
+    def keep(lanes, value):
+        mlp[1, :, lanes] = (value + mlp_got[:, lanes].astype(F32)).astype(BF16)
+
+    mlp_products(places()["c"] == 0, keep)
+    store = pltpu.make_async_copy(mlp.at[1], mlp_total, load_sem.at[0])
+    store.start()
     for copy in exchanged:
         copy.wait()
     side_by_side(dq_landed, dq)
@@ -1052,6 +1103,7 @@
     small[0:1, :] = gain
     small[1:2, :] = shift
     grad_out[...] = through[...] + step
+    store.wait()
     if carry:
         ring_a.land()
         ring_m.land()
@@ -1067,11 +1119,10 @@
     low = lambda *dims: pltpu.VMEM(dims, BF16)
     out_shape = [
         shape((rows, width), F32),
-        shape((2, rows, width), BF16),
-        shape((2, rows, M_COLS), BF16),
         *[shape((rows, PADDED), BF16)] * 4,
         shape((8, width), F32),
         shape((8, M_COLS), F32),
+        shape((4 * BLOCK, M_COLS), BF16),
     ]
     scratch = [
         low(2, 4 * BLOCK, 2 * PADDED),
@@ -1087,22 +1138,26 @@
         pltpu.SemaphoreType.DMA((4,)),
         pltpu.SemaphoreType.DMA((5, GROUP)),
         pltpu.SemaphoreType.DMA((5, GROUP)),
+        low(2, rows, width),
+        low(2, rows, M_COLS),
+        low(4 * BLOCK, M_COLS),
+        low(4 * BLOCK, 256),
     ]
     if carry:
         out_shape += [shape((2, 4 * BLOCK, PIECE), BF16), shape((2, BLOCK, M_COLS), BF16)]
         scratch += [low(2, 2 * BLOCK, PIECE)] * 2 + [low(2, NEAR, M_COLS)] * 2
-        scratch += [pltpu.SemaphoreType.DMA((16,))] * 2
+        scratch += [pltpu.SemaphoreType.DMA((24,))] * 2
     results = pl.pallas_call(
         functools.partial(backward_kernel, carry=carry),
         out_shape=out_shape,
-        in_specs=[vmem] * 11 + [hbm] * (4 if carry else 2),
-        out_specs=[vmem] * 9 + [hbm] * (2 if carry else 0),
+        in_specs=[vmem] * 13 + [hbm] * (4 if carry else 2),
+        out_specs=[vmem] * 7 + [hbm] * (3 if carry else 1),
         scratch_shapes=scratch,
         compiler_params=pltpu.CompilerParams(
             collective_id=collective, has_side_effects=True, vmem_limit_bytes=58 * 2**20
         ),
     )(grad, vec, mask, *kept, *weights, *(sums or ()))
-    return results[:9], tuple(results[9:])
+    return results[:8], tuple(results[8:])
 
 
 def body(tokens, qkv_weight, out_weight, up_weight, down_weight, vectors, segments, cotangent):
@@ -1114,18 +1169,26 @@
     docs = jnp.pad(segments, ((0, 8 - micro_count), (0, 128 - row_count)))
     *first, tail, q_next, mt_next, docs = gather_first(
         [
-            shard_rows(qkv_weight[l], out_weight[l], up_weight[l], down_weight[l], vectors[l], at["z"])
+            shard_rows(
+                qkv_weight[l],
+                out_weight[l],
+                up_weight[l],
+                down_weight[l],
+                vectors.reshape(12 * layers, -1).T if l == 0 else None,
+                at["z"],
+            )
             for l in range(layers)
         ],
         docs,
         3,
     )
     bias = score_bias(docs)
+    all_vectors = tail[:, width - PADDED + 128 :].T.astype(F32)
     weights = [tuple(first)]
     residual = tokens.reshape(total_rows, width).astype(F32)
     memory = []
     for l in range(layers):
-        vec = tail[:, width - PADDED + 128 :][:, :12].T.astype(F32)
+        vec = all_vectors[12 * l : 12 * l + 12]
         bias_up = lax.dynamic_slice_in_dim(vec[8:].reshape(-1), at["t"] * hidden_half, hidden_half)
         vec = jnp.pad(vec, ((0, 4), (0, PADDED - width)))
         kept, following = forward_layer(
@@ -1138,8 +1201,7 @@
             5 + l,
         )
         if l == 0:
-            *following, tail = following
-            weights.append(tuple(following))
+            weights.append(following)
         memory.append((vec, residual, *kept[1:]))
         residual = kept[0]
     result = residual
@@ -1152,24 +1214,18 @@
             gradient,
             vec,
             bias,
-            (layer_in, midway, d, *saved),
+            (layer_in, midway, d, m, g, *saved),
             weights[l],
             sums[1] if l == 0 else None,
             7 + l,
         )
         near = passed or near
-        gradient, dy, du, dz, dq, dk, dv, small, bias_back = kept
+        gradient, dz, dq, dk, dv, small, bias_back, mlp_sum = kept
         bias_back = lax.dynamic_update_slice_in_dim(
             jnp.zeros((2 * hidden_half,), F32), bias_back[0], at["t"] * hidden_half, 0
         )
         vec_back = jnp.concatenate([small, bias_back.reshape(-1, width)], 0)
-        sums[l] = chip_sums(
-            at,
-            (
-                normed, dq, dk, dv, o[:, :width], dz, m.reshape(-1, width),
-                du.reshape(-1, hidden_half), dy.reshape(-1, width), g.reshape(-1, hidden_half), vec_back,
-            ),
-        )
+        sums[l] = (attn_sums(at, (normed, dq, dk, dv, o[:, :width], dz, vec_back)), mlp_sum)
     parts = reduce_layers(sums, near, 4)
     totals = [owned_gradients(parts[l], width) for l in range(layers)]
     stacked = [jnp.stack([totals[l][n] for l in range(layers)]) for n in range(5)]

time: 599 us -> 557 us (0.930)
  Pallas kernels: 500 us -> 469 us
  matrix products: 43.7 us -> 21.6 us
  waiting for transfers between devices: 1.79 us -> 16.9 us
    dot_general x8 -> x4, matrix products: 43.7 us -> 21.6 us  [contract_rows(): lax.dot_general(a, b, (((0,), (0,)), ((), ())), preferred_element_type=F32)]
    pallas_call x1, Pallas kernels: 141 us -> 120 us  [reduce_layers(): pl.pallas_call(reduce_kernel, out_shape=jax.ShapeDtypeStruct((2, 4, 2, 2,...]
    ppermute x4 -> x2, waiting for transfers between devices: 1.79 us -> 16.9 us  [shifted(): return lax.ppermute(value, ('dp', 'ctx', 'tensor'), pairs)]
    pallas_call x1, Pallas kernels: 81.7 us -> 73.9 us  [gather_first(): pl.pallas_call(gather_kernel, out_shape=[shape((2, 4 * BLOCK, 2 * PADDED)...]
    pallas_call x2, Pallas kernels: 150 us -> 142 us  [forward_layer(): pl.pallas_call(functools.partial(forward_kernel, carry=carry), out_shape=...]
    unnamed x88 -> x57, local copies, waits for them, and re-layouts: 16.1 us -> 16.1 us
  transfers between devices with their start and end apart: 4 -> 2, of which waited for: 2 -> 2; matrix products, arithmetic and copies ran while one was open for 5% -> 0% of each run, Pallas kernels for 0% -> 0%
where the time goes in v4:
time: 557 us; the launch traced here: 550 us
  Pallas kernels  469 us (84%)
  local copies, waits for them, and re-layouts  34 us (6%)
  matrix products  21.6 us (4%)
  waiting for transfers between devices  16.9 us (3%)
  other arithmetic  7.58 us (1%)
    pallas_call x2, Pallas kernels, forward_layer(): pl.pallas_call(functools.partial(forward_kernel, carry=carry), out_shape=...  142 us
    pallas_call x2, Pallas kernels, backward_layer(): pl.pallas_call(functools.partial(backward_kernel, carry=carry), out_shape...  133 us
    pallas_call x1, Pallas kernels, reduce_layers(): pl.pallas_call(reduce_kernel, out_shape=jax.ShapeDtypeStruct((2, 4, 2, 2,...  120 us
    pallas_call x1, Pallas kernels, gather_first(): pl.pallas_call(gather_kernel, out_shape=[shape((2, 4 * BLOCK, 2 * PADDED)...  73.9 us
    dot_general x4, matrix products, contract_rows(): lax.dot_general(a, b, (((0,), (0,)), ((), ())), preferred_element_type=F32)  21.6 us
    ppermute x2, waiting for transfers between devices, shifted(): return lax.ppermute(value, ('dp', 'ctx', 'tensor'), pairs)  16.9 us
    unnamed x57, local copies, waits for them, and re-layouts  16.1 us
  transfers between devices with their start and end apart: 2, of which 2 were waited for; matrix products, arithmetic and copies ran while one was open for 0% of the time, Pallas kernels for 0%

profile of v4, /device:TPU:0, one launch (start us, length us, event | category | flops | bytes accessed | tf_op | source)
XLA Modules:
  0.0 550.4 jit_solution(12562198009756316809)
XLA Ops:
  0.6 3.1 fusion.76
  3.7 0.2 copy_bitcast_fusion
  3.9 0.1 fusion.80
  4.0 0.7 copy-done.7
  4.7 0.4 fusion.81
  5.1 0.1 copy.54
  5.5 0.1 concatenate.204
  5.7 0.1 fusion.79
  5.8 0.1 concatenate.208
  6.1 0.4 copy-done.5
  6.5 0.5 copy-done.3
  7.0 0.8 fusion.78
  7.8 0.2 copy-done.4
  8.0 0.8 fusion.77
  9.0 0.5 copy-done.22
  9.6 0.2 slice-done
  9.9 0.8 slice-done.1
  10.8 73.9 %shard_map.135 = (bf16[2,1088,2304]{2,1,0:T(8,128)(2,1)}, bf16[2,1088,2176]{2,1,0:T(8,128)(2,1)S(1)}, bf16[1088,128]{1,0:T(8,128)(2,1)S(1)}, bf16[272,512]{1,0:T...) custom-call(bf16[2,80,512]{2,1,0:T(8,128)(2,1)S(1)} %constant_dynamic-slice_fusion.2.q0, ...), custom_call_target="tpu_custom_call" | custom-call | tf_op jit(solution)/shard_map/pallas_call | solution.py:284
  84.7 3.6 copy-done
  88.3 1.1 copy-done.1
  89.4 0.7 copy-done.2
  90.1 0.2 copy.62
  90.4 0.9 bitcast_convert_fusion.refs_0_.refs_3_
  91.4 1.2 fusion.43.refs_3_.refs_2_
  92.8 0.6 pad.45.refs_1_
  93.5 0.6 pad.46.refs_1_
  94.1 0.6 broadcast_in_dim.20.refs_2_
  94.7 88.0 %shard_map.136 = (f32[128,1088]{1,0:T(8,128)}, bf16[128,1088]{1,0:T(8,128)(2,1)}, bf16[512,384]{1,0:T(8,128)(2,1)}, bf16[512,384]{1,0:T(8,128)(2,1)}, bf16[512,3...) custom-call(f32[128,1088]{1,0:T(8,128)} %bitcast_convert_fusion.refs, ...), custom_call_target="tpu_custom_call" | custom-call | tf_op jit(solution)/shard_map/pallas_call | solution.py:920
  182.7 0.6 broadcast_in_dim.23.refs_2_
  183.4 54.4 %shard_map.137 = (f32[128,1088]{1,0:T(8,128)}, bf16[128,1088]{1,0:T(8,128)(2,1)}, bf16[512,384]{1,0:T(8,128)(2,1)}, bf16[512,384]{1,0:T(8,128)(2,1)}, bf16[512,3...) custom-call(f32[128,1088]{1,0:T(8,128)} %get-tuple-element.63.refs_0, ...), custom_call_target="tpu_custom_call" | custom-call | tf_op jit(solution)/shard_map/pallas_call | solution.py:920
  237.8 54.4 %shard_map.138 = (f32[128,1088]{1,0:T(8,128)}, bf16[128,1152]{1,0:T(8,128)(2,1)}, bf16[128,1152]{1,0:T(8,128)(2,1)}, bf16[128,1152]{1,0:T(8,128)(2,1)}, bf16[128...) custom-call(f32[128,1088]{1,0:T(8,128)} %bitcast.121, ...), custom_call_target="tpu_custom_call" | custom-call | tf_op jit(solution)/shard_map/pallas_call | solution.py:1150
  292.3 1.0 slice_reduce_fusion.1
  293.2 0.3 dynamic_update_slice.6
  293.7 0.8 pad_maximum_fusion.22
  294.5 0.2 copy.63
  294.7 1.1 broadcast_select_fusion.6
  296.0 5.2 fusion
  301.3 8.6 %collective-permute-done = bf16[1088,2304]{1,0:T(8,128)(2,1)} collective-permute-done((bf16[1088,2304]{1,0:T(8,128)(2,1)}, bf16[1088,2304]{1,0:T(8,128)(2,1)}, u32[]{:S(2)}, u32[]{:S(2)}) %collective-permute-start) | collective-permute-done | bytes 5013536 | tf_op jit(solution)/shard_map/ppermute | solution.py:41
  309.9 7.2 %add_convert_fusion.1.refs_15_.attn1 = bf16[1088,2304]{1,0:T(8,128)(2,1)} fusion(bf16[1088,2304]{1,0:T(8,128)(2,1)} %collective-permute-done, f32[1088,12]{1,0:T(8,128)S(1)} %bitcast.125, f32[]{:T(128)S(6)} %select_n.105, bf16[128,1152]{1,0:T(8,128)(2,1)S(1)} %get-tuple-element.178, bf16[128,1152]{1,0:T(8,128)(2,1)S(1)} %get-tuple-element.176, ...), kind=kOutput, calls=%fused_computation.11 | convolution fusion | flops 1301823488 | bytes 11226116 | tf_op jit(solution)/shard_map/dot_general | solution.py:336
  317.0 78.1 %shard_map.139 = (f32[128,1088]{1,0:T(8,128)}, bf16[128,1152]{1,0:T(8,128)(2,1)}, bf16[128,1152]{1,0:T(8,128)(2,1)}, bf16[128,1152]{1,0:T(8,128)(2,1)}, bf16[128...) custom-call(f32[128,1088]{1,0:T(8,128)} %get-tuple-element.76.refs_0, ...), custom_call_target="tpu_custom_call" | custom-call | tf_op jit(solution)/shard_map/pallas_call | solution.py:1150
  395.1 1.0 slice_reduce_fusion
  396.1 0.3 dynamic_update_slice.7
  396.5 0.8 pad_maximum_fusion.23
  397.3 0.2 copy.64
  397.5 1.1 broadcast_select_fusion.2
  398.8 3.7 fusion.1
  402.6 8.3 %collective-permute-done.1 = bf16[1088,2304]{1,0:T(8,128)(2,1)S(1)} collective-permute-done((bf16[1088,2304]{1,0:T(8,128)(2,1)S(1)}, bf16[1088,2304]{1,0:T(8,128)(2,1)S(1)}, u32[]{:S(2)}, u32[]{:S(2)}) %collective-permute-start.1) | collective-permute-done | bytes 5013536 | tf_op jit(solution)/shard_map/ppermute | solution.py:41
  410.9 5.6 %add_convert_fusion.attn0 = bf16[1088,2304]{1,0:T(8,128)(2,1)} fusion(bf16[1088,2304]{1,0:T(8,128)(2,1)S(1)} %collective-permute-done.1, f32[1088,12]{1,0:T(8,128)S(1)} %bitcast.127, f32[]{:T(128)S(6)} %select_n.105, bf16[128,1152]{1,0:T(8,128)(2,1)S(1)} %get-tuple-element.172, bf16[128,1152]{1,0:T(8,128)(2,1)S(1)} %get-tuple-element.170, ...), kind=kOutput, calls=%fused_computation.10 | convolution fusion | flops 1301823488 | bytes 11226116 | tf_op jit(solution)/shard_map/dot_general | solution.py:336
  416.5 119.8 %shard_map.140 = bf16[2,4,2,2,80,640]{5,4,3,2,1,0:T(8,128)(2,1)} custom-call(bf16[1088,2304]{1,0:T(8,128)(2,1)} %add_convert_fusion.attn0, bf16[1088,2176]{1,0:T(8,128)(2,1)} %get-tuple-element.104.mlp0, bf16[1088,2304]{1,0:T(8,128)(2,1)} %add_convert_fusion.1.refs_15_.attn1, bf16[1088,2176]{1,0:T(8,128)(2,1)} %get-tuple-element.94.refs_16_.mlp1, ...), custom_call_target="tpu_custom_call" | custom-call | tf_op jit(solution)/shard_map/pallas_call | solution.py:582
  536.3 2.2 slice_bitcast_fusion.1
  538.8 0.7 slice_bitcast_fusion.34
  539.4 0.7 slice_bitcast_fusion.35
  540.2 0.2 concatenate.241
  540.5 0.2 concatenate.234
  540.7 0.1 maximum_convert_fusion
  540.8 2.2 copy.67
  543.0 1.1 copy.68
  544.2 1.6 copy.69
  546.0 1.6 copy.70
  547.6 0.1 copy.66
  547.7 0.1 copy.65
  547.8 0.6 maximum_convert_fusion.4
  548.5 0.8 copy.91
  549.3 0.8 copy.92
  (90 shorter events, 2.5 us)
Async XLA Ops:
  3.7 1.0 copy-start.7
  3.9 1.2 copy-start.21
  5.6 0.9 copy-start.5
  5.9 1.1 copy-start.3
  6.5 1.3 copy-start.6
  7.0 1.1 copy-start.4
  8.8 0.7 copy-start.22
  8.9 0.9 slice-start
  9.8 0.9 slice-start.1
  10.7 79.6 %copy-start.10 = (bf16[2,64,1088]{2,1,0:T(8,128)(2,1)S(1)}, bf16[2,64,1088]{2,1,0:T(8,128)(2,1)}, u32[]{:S(2)}) copy-start(bf16[2,64,1088]{2,1,0:T(8,128)(2,1)} %param.8) | copy-start | bytes 835588
  84.7 3.6 copy-start
  88.3 1.1 copy-start.1
  89.4 0.7 copy-start.2
  292.2 3.6 copy-start.15
  292.2 3.6 copy-start.16
  294.4 1.5 copy-start.13
  294.4 1.5 copy-start.14
  296.0 5.2 copy-start.11
  296.0 5.2 copy-start.12
  301.2 8.7 %collective-permute-start = (bf16[1088,2304]{1,0:T(8,128)(2,1)}, bf16[1088,2304]{1,0:T(8,128)(2,1)}, u32[]{:S(2)}, u32[]{:S(2)}) collective-permute-start(bf16[1088,2304]{1,0:T(8,128)(2,1)} %fusion), channel_id=1, source_target_pairs={{0,8},{1,9},{2,10},{3,11},{4,12},{5,13},{6,14},{7,15},{8,0},{9,1},... | collective-permute-start | bytes 15040520 | tf_op jit(solution)/shard_map/ppermute | solution.py:41
  395.1 3.6 copy-start.17
  395.1 3.6 copy-start.18
  402.5 8.4 %collective-permute-start.1 = (bf16[1088,2304]{1,0:T(8,128)(2,1)S(1)}, bf16[1088,2304]{1,0:T(8,128)(2,1)S(1)}, u32[]{:S(2)}, u32[]{:S(2)}) collective-permute-start(bf16[1088,2304]{1,0:T(8,128)(2,1)S(1)} %fusion.1), channel_id=1, source_target_pairs={{0,8},{1,9},{2,10},{3,11},{4,12},{5,13},{6,14},{7,15},{8,0},{9,1},... | collective-permute-start | bytes 15040520 | tf_op jit(solution)/shard_map/ppermute | solution.py:41
  546.0 1.7 copy-start.20
  546.0 1.8 copy-start.19
  546.0 2.5 copy-start.8
  546.0 3.3 copy-start.9

commit v5 on v4

--- a/solution.py
+++ b/solution.py
@@ -139,6 +139,9 @@
             wait()
 
 
+UPPER, LOWER = pl.ds(0, 2 * BLOCK), pl.ds(2 * BLOCK, 2 * BLOCK)
+
+
 class RingZ:
     def __init__(self, copies, buf):
         self.copies, self.buf = copies, buf
@@ -154,23 +157,30 @@
         self.last.append(self.copies.to(peer_at(c=1), src, src))
 
     def start(self):
-        own = self.view(0)
-        self.from_below = self.copies.to(peer_at(z=1), own, own)
-        self.from_above = self.copies.to(peer_at(z=-1), own, own)
-        self.sibling(own)
+        self.from_below = self.copies.to(peer_at(z=1), self.view(0, UPPER), self.view(0, UPPER))
+        self.from_above = self.copies.to(peer_at(z=-1), self.view(0, LOWER), self.view(0, LOWER))
+        self.sibling(self.view(0))
+
+    def more(self):
+        self.rest = (
+            self.copies.to(peer_at(z=1), self.view(0, LOWER), self.view(0, LOWER)),
+            self.copies.to(peer_at(z=-1), self.view(0, UPPER), self.view(0, UPPER)),
+        )
 
     def forward(self):
         self.from_below()
-        part = self.view(-1, pl.ds(0, 544))
+        part = self.view(-1, UPPER)
         far_a = self.copies.to(peer_at(z=1), part, part)
         self.from_above()
-        part = self.view(1, pl.ds(544, 544))
+        part = self.view(1, LOWER)
         far_b = self.copies.to(peer_at(z=-1), part, part)
         self.far = (far_a, far_b)
+
+    def finish(self):
+        for wait in self.rest:
+            wait()
         self.sibling(self.view(-1))
         self.sibling(self.view(1))
-
-    def finish(self):
         for wait in self.far:
             wait()
         self.sibling(self.view(2))
@@ -244,6 +254,7 @@
     q.finish()
     q.close()
     along_z.start()
+    along_z.more()
     t.start()
     m2.start()
     m.forward()
@@ -463,7 +474,7 @@
 ):
     barrier = pltpu.get_barrier_semaphore()
     peers = [dict(c=1), dict(x=1), dict(x=-1), dict(y=1, t=1), dict(y=1), dict(t=1)]
-    peers += [dict(z=1), dict(z=2), dict(z=3)]
+    peers += [dict(z=1), dict(z=-1)]
     for peer in peers:
         pl.semaphore_signal(barrier, inc=1, device_id=peer_at(**peer), device_id_type=MESH)
     pl.semaphore_wait(barrier, len(peers))
@@ -540,14 +551,23 @@
     def sixth(l, ends):
         for wait in ends:
             wait()
-        rest = []
+        arrived = []
         for n in range(2):
             for role, src in ((at["c"], owned.at[l, n, at["c"]]), (1 - at["c"], owned_got.at[l, n])):
                 dst = out.at[l, at["z"], n, role]
                 rest.append(copies.here(src, dst))
-                for d in (1, 2, 3):
-                    rest.append(copies.to(peer_at(z=d), src, dst))
-        return rest
+                below = copies.to(peer_at(z=1), src, dst)
+                arrived.append((n, role, below, copies.to(peer_at(z=-1), src, dst)))
+        return arrived
+
+    def seventh(l, arrived):
+        for n, role, below, above in arrived:
+            below()
+            part = out.at[l, turn(at["z"], -1), n, role, pl.ds(0, 48)]
+            rest.append(copies.to(peer_at(z=1), part, part))
+            above()
+            part = out.at[l, turn(at["z"], 1), n, role, pl.ds(48, 32)]
+            rest.append(copies.to(peer_at(z=-1), part, part))
 
     rings, waits, turned, ends, rest = {}, {}, {}, {}, []
     order = (1, 0)
@@ -567,9 +587,11 @@
     ends[1] = fifth(1, waits[1], turned[1])
     waits[0] = third(0, rings[0])
     turned[0] = fourth(0, waits[0])
-    rest += sixth(1, ends[1])
+    late = sixth(1, ends[1])
     ends[0] = fifth(0, waits[0], turned[0])
-    rest += sixth(0, ends[0])
+    last = sixth(0, ends[0])
+    seventh(1, late)
+    seventh(0, last)
     for wait in rest:
         wait()
     copies.close()
@@ -819,10 +841,11 @@
     exchanged = to_rows(
         me, (o_low,), (o_landed,), local_sem.at[3:4], send_sem.at[3:4], recv_sem.at[3:4]
     )
-    if carry:
-        ring_z.forward()
     for copy in exchanged:
         copy.wait()
+    if carry:
+        ring_z.forward()
+        ring_z.more()
     side_by_side(o_landed, o_out)
     o = o_out[:, :width]
     for start, stop in tiles_of(width, 384):

time: 557 us -> 552 us (level)
    pallas_call x1, Pallas kernels: 120 us -> 113 us  [reduce_layers(): pl.pallas_call(reduce_kernel, out_shape=jax.ShapeDtypeStruct((2, 4, 2, 2,...]
where the time goes in v5:
time: 552 us; the launch traced here: 547 us
  Pallas kernels  465 us (84%)
  local copies, waits for them, and re-layouts  34 us (6%)
  matrix products  21.6 us (4%)
  waiting for transfers between devices  16.9 us (3%)
  other arithmetic  7.58 us (1%)
    pallas_call x2, Pallas kernels, forward_layer(): pl.pallas_call(functools.partial(forward_kernel, carry=carry), out_shape=...  145 us
    pallas_call x2, Pallas kernels, backward_layer(): pl.pallas_call(functools.partial(backward_kernel, carry=carry), out_shape...  133 us
    pallas_call x1, Pallas kernels, reduce_layers(): pl.pallas_call(reduce_kernel, out_shape=jax.ShapeDtypeStruct((2, 4, 2, 2,...  113 us
    pallas_call x1, Pallas kernels, gather_first(): pl.pallas_call(gather_kernel, out_shape=[shape((2, 4 * BLOCK, 2 * PADDED)...  73.9 us
    dot_general x4, matrix products, contract_rows(): lax.dot_general(a, b, (((0,), (0,)), ((), ())), preferred_element_type=F32)  21.6 us
    ppermute x2, waiting for transfers between devices, shifted(): return lax.ppermute(value, ('dp', 'ctx', 'tensor'), pairs)  16.9 us
    unnamed x57, local copies, waits for them, and re-layouts  16.1 us
  transfers between devices with their start and end apart: 2, of which 2 were waited for; matrix products, arithmetic and copies ran while one was open for 0% of the time, Pallas kernels for 0%

profile of v5, /device:TPU:0, one launch (start us, length us, event | category | flops | bytes accessed | tf_op | source)
XLA Modules:
  0.0 547.0 jit_solution(6899469359011104014)
XLA Ops:
  0.6 3.1 fusion.76
  3.7 0.2 copy_bitcast_fusion
  3.9 0.1 fusion.80
  4.0 0.7 copy-done.7
  4.7 0.4 fusion.81
  5.1 0.1 copy.54
  5.5 0.1 concatenate.204
  5.7 0.1 fusion.79
  5.9 0.1 concatenate.207
  6.1 0.4 copy-done.5
  6.5 0.5 copy-done.3
  7.0 0.8 fusion.78
  7.8 0.2 copy-done.4
  8.0 0.8 fusion.77
  9.0 0.5 copy-done.22
  9.6 0.2 slice-done
  9.9 0.8 slice-done.1
  10.8 73.9 %shard_map.135 = (bf16[2,1088,2304]{2,1,0:T(8,128)(2,1)}, bf16[2,1088,2176]{2,1,0:T(8,128)(2,1)S(1)}, bf16[1088,128]{1,0:T(8,128)(2,1)S(1)}, bf16[272,512]{1,0:T...) custom-call(bf16[2,80,512]{2,1,0:T(8,128)(2,1)S(1)} %constant_dynamic-slice_fusion.2.q0, ...), custom_call_target="tpu_custom_call" | custom-call | tf_op jit(solution)/shard_map/pallas_call | solution.py:295
  84.7 3.6 copy-done
  88.3 1.1 copy-done.1
  89.4 0.7 copy-done.2
  90.1 0.2 copy.62
  90.4 0.9 bitcast_convert_fusion.refs_0_.refs_3_
  91.4 1.2 fusion.43.refs_3_.refs_2_
  92.8 0.6 pad.45.refs_1_
  93.5 0.6 pad.46.refs_1_
  94.1 0.6 broadcast_in_dim.20.refs_2_
  94.7 88.9 %shard_map.136 = (f32[128,1088]{1,0:T(8,128)}, bf16[128,1088]{1,0:T(8,128)(2,1)}, bf16[512,384]{1,0:T(8,128)(2,1)}, bf16[512,384]{1,0:T(8,128)(2,1)}, bf16[512,3...) custom-call(f32[128,1088]{1,0:T(8,128)} %bitcast_convert_fusion.refs, ...), custom_call_target="tpu_custom_call" | custom-call | tf_op jit(solution)/shard_map/pallas_call | solution.py:943
  183.7 0.6 broadcast_in_dim.23.refs_2_
  184.3 56.0 %shard_map.137 = (f32[128,1088]{1,0:T(8,128)}, bf16[128,1088]{1,0:T(8,128)(2,1)}, bf16[512,384]{1,0:T(8,128)(2,1)}, bf16[512,384]{1,0:T(8,128)(2,1)}, bf16[512,3...) custom-call(f32[128,1088]{1,0:T(8,128)} %get-tuple-element.63.refs_0, ...), custom_call_target="tpu_custom_call" | custom-call | tf_op jit(solution)/shard_map/pallas_call | solution.py:943
  240.3 55.4 %shard_map.138 = (f32[128,1088]{1,0:T(8,128)}, bf16[128,1152]{1,0:T(8,128)(2,1)}, bf16[128,1152]{1,0:T(8,128)(2,1)}, bf16[128,1152]{1,0:T(8,128)(2,1)}, bf16[128...) custom-call(f32[128,1088]{1,0:T(8,128)} %bitcast.121, ...), custom_call_target="tpu_custom_call" | custom-call | tf_op jit(solution)/shard_map/pallas_call | solution.py:1173
  295.7 1.0 slice_reduce_fusion.1
  296.7 0.3 dynamic_update_slice.6
  297.1 0.8 pad_maximum_fusion.22
  297.9 0.2 copy.63
  298.2 1.1 broadcast_select_fusion.6
  299.5 5.2 fusion
  304.7 8.6 %collective-permute-done = bf16[1088,2304]{1,0:T(8,128)(2,1)} collective-permute-done((bf16[1088,2304]{1,0:T(8,128)(2,1)}, bf16[1088,2304]{1,0:T(8,128)(2,1)}, u32[]{:S(2)}, u32[]{:S(2)}) %collective-permute-start) | collective-permute-done | bytes 5013536 | tf_op jit(solution)/shard_map/ppermute | solution.py:41
  313.3 7.2 %add_convert_fusion.1.refs_15_.attn1 = bf16[1088,2304]{1,0:T(8,128)(2,1)} fusion(bf16[1088,2304]{1,0:T(8,128)(2,1)} %collective-permute-done, f32[1088,12]{1,0:T(8,128)S(1)} %bitcast.125, f32[]{:T(128)S(6)} %select_n.105, bf16[128,1152]{1,0:T(8,128)(2,1)S(1)} %get-tuple-element.178, bf16[128,1152]{1,0:T(8,128)(2,1)S(1)} %get-tuple-element.176, ...), kind=kOutput, calls=%fused_computation.11 | convolution fusion | flops 1301823488 | bytes 11226116 | tf_op jit(solution)/shard_map/dot_general | solution.py:347
  320.5 77.9 %shard_map.139 = (f32[128,1088]{1,0:T(8,128)}, bf16[128,1152]{1,0:T(8,128)(2,1)}, bf16[128,1152]{1,0:T(8,128)(2,1)}, bf16[128,1152]{1,0:T(8,128)(2,1)}, bf16[128...) custom-call(f32[128,1088]{1,0:T(8,128)} %get-tuple-element.76.refs_0, ...), custom_call_target="tpu_custom_call" | custom-call | tf_op jit(solution)/shard_map/pallas_call | solution.py:1173
  398.4 1.0 slice_reduce_fusion
  399.4 0.3 dynamic_update_slice.7
  399.8 0.8 pad_maximum_fusion.23
  400.6 0.2 copy.64
  400.8 1.1 broadcast_select_fusion.2
  402.0 3.7 fusion.1
  405.9 8.3 %collective-permute-done.1 = bf16[1088,2304]{1,0:T(8,128)(2,1)S(1)} collective-permute-done((bf16[1088,2304]{1,0:T(8,128)(2,1)S(1)}, bf16[1088,2304]{1,0:T(8,128)(2,1)S(1)}, u32[]{:S(2)}, u32[]{:S(2)}) %collective-permute-start.1) | collective-permute-done | bytes 5013536 | tf_op jit(solution)/shard_map/ppermute | solution.py:41
  414.2 5.6 %add_convert_fusion.attn0 = bf16[1088,2304]{1,0:T(8,128)(2,1)} fusion(bf16[1088,2304]{1,0:T(8,128)(2,1)S(1)} %collective-permute-done.1, f32[1088,12]{1,0:T(8,128)S(1)} %bitcast.127, f32[]{:T(128)S(6)} %select_n.105, bf16[128,1152]{1,0:T(8,128)(2,1)S(1)} %get-tuple-element.172, bf16[128,1152]{1,0:T(8,128)(2,1)S(1)} %get-tuple-element.170, ...), kind=kOutput, calls=%fused_computation.10 | convolution fusion | flops 1301823488 | bytes 11226116 | tf_op jit(solution)/shard_map/dot_general | solution.py:347
  419.8 113.2 %shard_map.140 = bf16[2,4,2,2,80,640]{5,4,3,2,1,0:T(8,128)(2,1)} custom-call(bf16[1088,2304]{1,0:T(8,128)(2,1)} %add_convert_fusion.attn0, bf16[1088,2176]{1,0:T(8,128)(2,1)} %get-tuple-element.104.mlp0, bf16[1088,2304]{1,0:T(8,128)(2,1)} %add_convert_fusion.1.refs_15_.attn1, bf16[1088,2176]{1,0:T(8,128)(2,1)} %get-tuple-element.94.refs_16_.mlp1, ...), custom_call_target="tpu_custom_call" | custom-call | tf_op jit(solution)/shard_map/pallas_call | solution.py:604
  532.9 2.2 slice_bitcast_fusion.1
  535.4 0.7 slice_bitcast_fusion.34
  536.1 0.7 slice_bitcast_fusion.35
  536.8 0.2 concatenate.241
  537.1 0.2 concatenate.234
  537.3 0.1 maximum_convert_fusion
  537.4 2.2 copy.67
  539.6 1.1 copy.68
  540.9 1.6 copy.69
  542.6 1.6 copy.70
  544.3 0.1 copy.66
  544.4 0.1 copy.65
  544.5 0.6 maximum_convert_fusion.4
  545.1 0.8 copy.91
  545.9 0.8 copy.92
  (90 shorter events, 2.5 us)
Async XLA Ops:
  3.7 1.0 copy-start.7
  3.9 1.2 copy-start.21
  5.6 0.9 copy-start.5
  5.9 1.1 copy-start.3
  6.5 1.3 copy-start.6
  7.0 1.1 copy-start.4
  8.8 0.7 copy-start.22
  8.9 0.9 slice-start
  9.8 0.9 slice-start.1
  10.7 79.6 %copy-start.10 = (bf16[2,64,1088]{2,1,0:T(8,128)(2,1)S(1)}, bf16[2,64,1088]{2,1,0:T(8,128)(2,1)}, u32[]{:S(2)}) copy-start(bf16[2,64,1088]{2,1,0:T(8,128)(2,1)} %param.8) | copy-start | bytes 835588
  84.7 3.6 copy-start
  88.3 1.1 copy-start.1
  89.4 0.7 copy-start.2
  295.7 3.6 copy-start.15
  295.7 3.6 copy-start.16
  297.9 1.5 copy-start.13
  297.9 1.5 copy-start.14
  299.5 5.2 copy-start.11
  299.5 5.2 copy-start.12
  304.7 8.7 %collective-permute-start = (bf16[1088,2304]{1,0:T(8,128)(2,1)}, bf16[1088,2304]{1,0:T(8,128)(2,1)}, u32[]{:S(2)}, u32[]{:S(2)}) collective-permute-start(bf16[1088,2304]{1,0:T(8,128)(2,1)} %fusion), channel_id=1, source_target_pairs={{0,8},{1,9},{2,10},{3,11},{4,12},{5,13},{6,14},{7,15},{8,0},{9,1},... | collective-permute-start | bytes 15040520 | tf_op jit(solution)/shard_map/ppermute | solution.py:41
  398.4 3.6 copy-start.17
  398.4 3.6 copy-start.18
  405.8 8.4 %collective-permute-start.1 = (bf16[1088,2304]{1,0:T(8,128)(2,1)S(1)}, bf16[1088,2304]{1,0:T(8,128)(2,1)S(1)}, u32[]{:S(2)}, u32[]{:S(2)}) collective-permute-start(bf16[1088,2304]{1,0:T(8,128)(2,1)S(1)} %fusion.1), channel_id=1, source_target_pairs={{0,8},{1,9},{2,10},{3,11},{4,12},{5,13},{6,14},{7,15},{8,0},{9,1},... | collective-permute-start | bytes 15040520 | tf_op jit(solution)/shard_map/ppermute | solution.py:41
  542.6 1.7 copy-start.20
  542.6 1.8 copy-start.19
  542.6 2.5 copy-start.8
  542.6 3.3 copy-start.9
